TPU v7x, 32 devices: a whole 2x2x4 slice. The times are simulated.
32 devices in a mesh: gx: 4 (over x, core), gy: 2 (over y), gz: 4 (over z).
Axes of the slice: x: 2, y: 2, z: 4, core: 2. Of those that a mesh axis runs over, the one named last changes fastest.
Arguments:
- thermal_anomaly: float32 [64, 16, 512], P('gz', 'gy', 'gx'), may hold values from -6 to 6
- material_label: int32 [64, 16, 512], P('gz', 'gy', 'gx'), may hold values from 0 to 12
- label_thermal_table: float32 [13], replicated, may hold values from 0.25 to 4
- bottom_edge_option: int32 [16, 512], P('gy', 'gx'), may hold values from 0 to 1
Outputs:
- heated: float32 [64, 16, 512], P('gz', 'gy', 'gx')
Inputs may be any that keep to these rules, and one draw needn't show every extreme that they name: material_label picks an entry of label_thermal_table. bottom_edge_option is 1 where the ground under the column is held at zero anomaly and 0 where it is insulated.
All inputs are finite; a program needn't handle non-finite values.
Results may differ from a plain program's by a relative error of at most 0.0006.
Values sent between devices are 32-bit elements; how exact they have to be, the bound alone decides.
No kernel may reach another device: no remote copies, remote signals or barrier semaphores. Data moves between devices by JAX's collectives and lax.ppermute only.
A program may use at most 64 MiB of HBM per device.

v0:
```python
import jax
import jax.numpy as jnp
from jax import lax
from jax.sharding import PartitionSpec as P

THETA_FACTOR = 0.5
FLAT_SCALE = 1000.0
UPWARD_SCALE = 200.0


def with_halo(block, sides, width):
    for axis, dim in sides:
        count = lax.axis_size(axis)
        forward = [(i, i + 1) for i in range(count - 1)]
        backward = [(target, source) for source, target in forward]
        low = lax.ppermute(
            lax.slice_in_dim(block, block.shape[dim] - width, None, axis=dim), axis, forward
        )
        high = lax.ppermute(lax.slice_in_dim(block, 0, width, axis=dim), axis, backward)
        block = jnp.concatenate([low, block, high], axis=dim)
    return block


def shifted(values, offset, along, pad_value):
    length = values.shape[along]
    pad_shape = list(values.shape)
    pad_shape[along] = abs(offset)
    filler = jnp.full(pad_shape, pad_value, values.dtype)
    if offset > 0:
        return jnp.concatenate(
            [filler, lax.slice_in_dim(values, 0, length - offset, axis=along)], along
        )
    return jnp.concatenate([lax.slice_in_dim(values, -offset, length, axis=along), filler], along)


def face_conductance(local_thermal_rate, along, factor):
    before = shifted(local_thermal_rate, 1, along, 0.0)
    return factor * (2.0 * local_thermal_rate * before) / (local_thermal_rate + before)


def face_pairs(conduct_line, along, factor):
    length = conduct_line.shape[along]
    current = lax.slice_in_dim(conduct_line, 1, length, axis=along)
    before = lax.slice_in_dim(conduct_line, 0, length - 1, axis=along)
    return factor * (2.0 * current * before) / (current + before)


def block_flux(values_line, faces_all, along):
    length = values_line.shape[along]
    centre = lax.slice_in_dim(values_line, 1, length - 1, axis=along)
    beyond = lax.slice_in_dim(values_line, 2, length, axis=along)
    before = lax.slice_in_dim(values_line, 0, length - 2, axis=along)
    low_face = lax.slice_in_dim(faces_all, 0, length - 2, axis=along)
    high_face = lax.slice_in_dim(faces_all, 1, length - 1, axis=along)
    return high_face * (beyond - centre) - low_face * (centre - before)


def reduce_bands(low_band, main_band, high_band, sources, along):
    length = main_band.shape[along]
    distance = 1
    while distance < length:
        below_main = shifted(main_band, distance, along, 1.0)
        below_low = shifted(low_band, distance, along, 0.0)
        below_high = shifted(high_band, distance, along, 0.0)
        above_main = shifted(main_band, -distance, along, 1.0)
        above_low = shifted(low_band, -distance, along, 0.0)
        above_high = shifted(high_band, -distance, along, 0.0)
        left_ratio = low_band / below_main
        right_ratio = high_band / above_main
        sources = [
            each_source
            - left_ratio * shifted(each_source, distance, along, 0.0)
            - right_ratio * shifted(each_source, -distance, along, 0.0)
            for each_source in sources
        ]
        main_band = main_band - left_ratio * below_high - right_ratio * above_low
        low_band = -left_ratio * below_low
        high_band = -right_ratio * above_high
        distance = distance * 2
    return [each_source / main_band for each_source in sources]


def reduce_lines(faces, source, along):
    beyond = shifted(faces, -1, along, 0.0)
    main_band = 1.0 + THETA_FACTOR * (faces + beyond)
    low_band = -THETA_FACTOR * faces
    high_band = -THETA_FACTOR * beyond
    return reduce_bands(low_band, main_band, high_band, [source], along)[0]


def vertical_solve(conduct_z, source_z, bottom_edge_option):
    upward_interface_transfer = face_conductance(conduct_z, 0, UPWARD_SCALE)
    row_count = conduct_z.shape[1]
    flag_rows = lax.dynamic_slice_in_dim(
        bottom_edge_option, lax.axis_index("gz") * row_count, row_count, 0
    ).astype(jnp.float32)
    ground_z = UPWARD_SCALE * 2.0 * conduct_z[0] * flag_rows
    upward_interface_transfer = jnp.concatenate([ground_z[None], upward_interface_transfer[1:]], 0)
    return reduce_lines(upward_interface_transfer, source_z, 0)


def local(thermal_anomaly, material_label, label_thermal_table, bottom_edge_option):
    local_thermal_rate = jnp.zeros_like(thermal_anomaly)
    for table_entry in range(label_thermal_table.shape[0]):
        local_thermal_rate = local_thermal_rate + jnp.where(
            material_label == table_entry, label_thermal_table[table_entry], 0.0
        )
    border_padded = with_halo(
        jnp.stack([thermal_anomaly, local_thermal_rate]), (("gx", 3), ("gy", 2), ("gz", 1)), 1
    )
    heat_pad = border_padded[0]
    conduct_pad = border_padded[1]
    faces_x_all = face_pairs(conduct_pad[1:-1, 1:-1, :], 2, FLAT_SCALE)
    faces_y_all = face_pairs(conduct_pad[1:-1, :, 1:-1], 1, FLAT_SCALE)
    faces_z_all = face_pairs(conduct_pad[:, 1:-1, 1:-1], 0, UPWARD_SCALE)
    ground = UPWARD_SCALE * 2.0 * local_thermal_rate[0] * bottom_edge_option.astype(jnp.float32)
    bottom = jnp.where(lax.axis_index("gz") == 0, ground, faces_z_all[0])
    faces_z_all = jnp.concatenate([bottom[None], faces_z_all[1:]], 0)
    solve_first_direction = block_flux(heat_pad[1:-1, 1:-1, :], faces_x_all, 2)
    solve_second_direction = block_flux(heat_pad[1:-1, :, 1:-1], faces_y_all, 1)
    solve_upward_direction = block_flux(heat_pad[:, 1:-1, 1:-1], faces_z_all, 0)
    forward_euler_change = (
        thermal_anomaly
        + (1.0 - THETA_FACTOR) * solve_first_direction
        + solve_second_direction
        + solve_upward_direction
    )
    lines_conduct, lines_source, lines_across_y, lines_across_z = (
        lax.all_to_all(local_thermal_rate, "gx", split_axis=0, concat_axis=2, tiled=True),
        lax.all_to_all(forward_euler_change, "gx", split_axis=0, concat_axis=2, tiled=True),
        lax.all_to_all(solve_second_direction, "gx", split_axis=0, concat_axis=2, tiled=True),
        lax.all_to_all(solve_upward_direction, "gx", split_axis=0, concat_axis=2, tiled=True),
    )
    after_x = reduce_lines(face_conductance(lines_conduct, 2, FLAT_SCALE), lines_source, 2)
    source_y, conduct_y, across_z_y = (
        lax.all_to_all(
            lax.all_to_all(
                after_x - THETA_FACTOR * lines_across_y,
                "gx",
                split_axis=2,
                concat_axis=0,
                tiled=True,
            ),
            "gy",
            split_axis=0,
            concat_axis=1,
            tiled=True,
        ),
        lax.all_to_all(
            lax.all_to_all(lines_conduct, "gx", split_axis=2, concat_axis=0, tiled=True),
            "gy",
            split_axis=0,
            concat_axis=1,
            tiled=True,
        ),
        lax.all_to_all(
            lax.all_to_all(lines_across_z, "gx", split_axis=2, concat_axis=0, tiled=True),
            "gy",
            split_axis=0,
            concat_axis=1,
            tiled=True,
        ),
    )
    after_y = reduce_lines(face_conductance(conduct_y, 1, FLAT_SCALE), source_y, 1)
    source_z, conduct_z = (
        lax.all_to_all(
            lax.all_to_all(
                after_y - THETA_FACTOR * across_z_y, "gy", split_axis=1, concat_axis=0, tiled=True
            ),
            "gz",
            split_axis=1,
            concat_axis=0,
            tiled=True,
        ),
        lax.all_to_all(
            lax.all_to_all(conduct_y, "gy", split_axis=1, concat_axis=0, tiled=True),
            "gz",
            split_axis=1,
            concat_axis=0,
            tiled=True,
        ),
    )
    heated = lax.all_to_all(
        vertical_solve(conduct_z, source_z, bottom_edge_option),
        "gz",
        split_axis=0,
        concat_axis=1,
        tiled=True,
    )
    return heated


def solution(mesh):
    return jax.shard_map(
        local,
        mesh=mesh,
        in_specs=(P("gz", "gy", "gx"), P("gz", "gy", "gx"), P(), P("gy", "gx")),
        out_specs=P("gz", "gy", "gx"),
        check_vma=False,
    )
```

profile of v0, /device:TPU:0, one launch (start us, length us, event | category | flops | bytes accessed | tf_op | source)
XLA Modules:
  0.0 164.7 jit_solution(3888140371672427020)
XLA Ops:
  0.0 1.8 %fusion.91 = (f32[1]{0:T(128)}, f32[1]{0:T(128)}, f32[1]{0:T(128)}, f32[1]{0:T(128)}, f32[1]{0:T(128)}, /*index=5*/f32[1]{0:T(128)}, f32[1]{0:T(128)}, f32[1]{0:...) fusion(f32[13]{0:T(128)} %param.6), kind=kLoop, calls=%fused_computation.235 | loop fusion | bytes 104 | tf_op jit(solution)/shard_map/slice | solution.py:106
  1.8 9.0 %fusion.92 = f32[1,16,8,128]{3,2,1,0:T(8,128)S(1)} fusion(f32[]{:T(128)} %bitcast.13, s32[16,8,128]{2,1,0:T(8,128)} %param.5, f32[]{:T(128)} %bitcast.12, f32[]{:T(128)} %bitcast.11, f32[]{:T(128)} %bitcast.10, f32[]{:T(128)} %bitcast.9, f32[]{:T(128)} %bitcast.8, f32[]{:T(128)} %bitcast.7, f32[]{:T(128)} %bitcast.6, f32[]{:T(128)} %bitcast.5, f32[]{:T(128)} %bitcast.4, ...), kind=kLoop, calls=%fused_computation.236 | loop fusion | flops 622592 | bytes 131124 | tf_op jit(solution)/shard_map/stack | solution.py:109
  10.9 2.4 %collective-permute-start = (f32[2,16,8,1]{3,2,1,0:T(8,128)S(1)}, f32[2,16,8,1]{3,2,1,0:T(8,128)S(1)}, u32[]{:S(2)}, u32[]{:S(2)}) collective-permute-start(f32[2,16,8,1]{3,2,1,0:T(8,128)S(1)} %get-tuple-element.66), channel_id=1, source_target_pairs={{0,8},{8,16},{16,24},{1,9},{9,17},{17,25},{2,10},{10,18},{18,26},{... | collective-permute-start | bytes 3080 | tf_op jit(solution)/shard_map/ppermute | solution.py:16
  14.6 4.0 %collective-permute-done.1 = f32[2,16,8,1]{3,2,1,0:T(8,128)S(1)} collective-permute-done((f32[2,16,8,1]{3,2,1,0:T(8,128)S(1)}, f32[2,16,8,1]{3,2,1,0:T(8,128)S(1)}, u32[]{:S(2)}, u32[]{:S(2)}) %collective-permute-start.1) | collective-permute-done | bytes 1056 | tf_op jit(solution)/shard_map/ppermute | solution.py:19
  18.9 3.4 %collective-permute-start.2 = (f32[2,16,1,130]{3,2,1,0:T(1,128)S(1)}, f32[2,16,1,130]{3,2,1,0:T(1,128)S(1)}, u32[]{:S(2)}, u32[]{:S(2)}) collective-permute-start(f32[2,16,1,130]{3,2,1,0:T(1,128)S(1)} %get-tuple-element.57), channel_id=1, source_target_pairs={{0,4},{1,5},{2,6},{3,7},{8,12},{9,13},{10,14},{11,15},{16,20},{17,... | collective-permute-start | bytes 49928 | tf_op jit(solution)/shard_map/ppermute | solution.py:16
  23.9 4.4 %collective-permute-done.3 = f32[2,16,1,130]{3,2,1,0:T(1,128)S(1)} collective-permute-done((f32[2,16,1,130]{3,2,1,0:T(1,128)S(1)}, f32[2,16,1,130]{3,2,1,0:T(1,128)S(1)}, u32[]{:S(2)}, u32[]{:S(2)}) %collective-permute-start.3) | collective-permute-done | bytes 16672 | tf_op jit(solution)/shard_map/ppermute | solution.py:19
  28.4 3.5 %collective-permute-start.4 = (f32[2,1,10,130]{3,2,1,0:T(8,128)S(1)}, f32[2,1,10,130]{3,2,1,0:T(8,128)S(1)}, u32[]{:S(2)}, u32[]{:S(2)}) collective-permute-start(f32[2,1,10,130]{3,2,1,0:T(8,128)S(1)} %get-tuple-element.55), channel_id=1, source_target_pairs={{0,1},{1,2},{2,3},{4,5},{5,6},{6,7},{8,9},{9,10},{10,11},{12,13},{... | collective-permute-start | bytes 31208 | tf_op jit(solution)/shard_map/ppermute | solution.py:16
  33.2 8.8 %select_add_fusion = f32[16,8,128]{2,1,0:T(8,128)} fusion(s32[16,8,128]{2,1,0:T(8,128)S(1)} %copy-done.1, f32[]{:T(128)} %bitcast.13, f32[]{:T(128)} %bitcast.12, f32[]{:T(128)} %bitcast.11, f32[]{:T(128)} %bitcast.10, f32[]{:T(128)} %bitcast.9, f32[]{:T(128)} %bitcast.8, f32[]{:T(128)} %bitcast.7, f32[]{:T(128)} %bitcast.6, f32[]{:T(128)} %bitcast.5, ...), kind=kLoop, calls=%fused_computation.139 | loop fusion | flops 622592 | bytes 131124 | tf_op jit(solution)/shard_map/add | solution.py:105
  42.0 4.6 %all-to-all-start.1 = ((f32[16,8,128]{2,1,0:T(8,128)}), f32[16,8,128]{2,1,0:T(8,128)S(1)}, u32[]{:S(2)}, u32[]{:S(2)}) async-start(f32[16,8,128]{2,1,0:T(8,128)} %select_add_fusion), calls=%async_computation.1 | async-start | bytes 131072 | tf_op jit(solution)/shard_map/all_to_all | solution.py:129
  50.6 3.3 %all-to-all-start = ((f32[16,8,128]{2,1,0:T(8,128)}), f32[16,8,128]{2,1,0:T(8,128)S(1)}, u32[]{:S(2)}, u32[]{:S(2)}) async-start(f32[16,8,128]{2,1,0:T(8,128)} %get-tuple-element.46), calls=%async_computation | async-start | bytes 131072 | tf_op jit(solution)/shard_map/all_to_all | solution.py:130
  58.0 3.3 %all-to-all-start.2 = ((f32[16,8,128]{2,1,0:T(8,128)}), f32[16,8,128]{2,1,0:T(8,128)S(1)}, u32[]{:S(2)}, u32[]{:S(2)}) async-start(f32[16,8,128]{2,1,0:T(8,128)} %get-tuple-element.47), calls=%async_computation.2 | async-start | bytes 131072 | tf_op jit(solution)/shard_map/all_to_all | solution.py:131
  65.4 3.3 %all-to-all-start.7 = ((f32[16,8,128]{2,1,0:T(8,128)}), f32[16,8,128]{2,1,0:T(8,128)S(1)}, u32[]{:S(2)}, u32[]{:S(2)}) async-start(f32[16,8,128]{2,1,0:T(8,128)} %get-tuple-element.48), calls=%async_computation.7 | async-start | bytes 131072 | tf_op jit(solution)/shard_map/all_to_all | solution.py:132
  68.8 4.0 %all-to-all-done.7 = f32[16,8,128]{2,1,0:T(8,128)S(1)} async-done(((f32[16,8,128]{2,1,0:T(8,128)}), f32[16,8,128]{2,1,0:T(8,128)S(1)}, u32[]{:S(2)}, u32[]{:S(2)}) %all-to-all-start.7) | async-done | bytes 65568 | tf_op jit(solution)/shard_map/all_to_all | solution.py:132
  72.8 3.3 %all-to-all-start.5 = ((f32[4,1,4096]{2,1,0:T(1,128)}), f32[4,1,4096]{2,1,0:T(1,128)S(1)}, u32[]{:S(2)}, u32[]{:S(2)}) async-start(f32[4,1,4096]{2,1,0:T(1,128)} %reshape.12), calls=%async_computation.5 | async-start | bytes 131072 | tf_op jit(solution)/shard_map/all_to_all | solution.py:150
  78.3 1.9 %all-to-all-done.5 = f32[4,1,4096]{2,1,0:T(1,128)S(1)} async-done(((f32[4,1,4096]{2,1,0:T(1,128)}), f32[4,1,4096]{2,1,0:T(1,128)S(1)}, u32[]{:S(2)}, u32[]{:S(2)}) %all-to-all-start.5) | async-done | bytes 65568 | tf_op jit(solution)/shard_map/all_to_all | solution.py:150
  80.2 3.3 %all-to-all-start.3 = ((f32[4,1,4096]{2,1,0:T(1,128)}), f32[4,1,4096]{2,1,0:T(1,128)S(1)}, u32[]{:S(2)}, u32[]{:S(2)}) async-start(f32[4,1,4096]{2,1,0:T(1,128)} %reshape.16), calls=%async_computation.3 | async-start | bytes 131072 | tf_op jit(solution)/shard_map/all_to_all | solution.py:137
  85.7 1.9 %all-to-all-done.3 = f32[4,1,4096]{2,1,0:T(1,128)S(1)} async-done(((f32[4,1,4096]{2,1,0:T(1,128)}), f32[4,1,4096]{2,1,0:T(1,128)S(1)}, u32[]{:S(2)}, u32[]{:S(2)}) %all-to-all-start.3) | async-done | bytes 65568 | tf_op jit(solution)/shard_map/all_to_all | solution.py:137
  87.6 3.3 %all-to-all-start.8 = ((f32[4,1,4096]{2,1,0:T(1,128)}), f32[4,1,4096]{2,1,0:T(1,128)S(1)}, u32[]{:S(2)}, u32[]{:S(2)}) async-start(f32[4,1,4096]{2,1,0:T(1,128)} %reshape.14), calls=%async_computation.8 | async-start | bytes 131072 | tf_op jit(solution)/shard_map/all_to_all | solution.py:157
  95.0 3.5 %all-to-all-start.6 = ((f32[16,8,128]{2,1,0:T(8,128)}), f32[16,8,128]{2,1,0:T(8,128)S(1)}, u32[]{:S(2)}, u32[]{:S(2)}) async-start(f32[16,8,128]{2,1,0:T(8,128)} %bitcast.37), calls=%async_computation.6 | async-start | bytes 131072 | tf_op jit(solution)/shard_map/all_to_all | solution.py:149
  104.4 3.3 %all-to-all-start.4 = ((f32[16,8,128]{2,1,0:T(8,128)}), f32[16,8,128]{2,1,0:T(8,128)S(1)}, u32[]{:S(2)}, u32[]{:S(2)}) async-start(f32[16,8,128]{2,1,0:T(8,128)} %bitcast.31), calls=%async_computation.4 | async-start | bytes 131072 | tf_op jit(solution)/shard_map/all_to_all | solution.py:136
  108.5 3.3 %all-to-all-done.4 = f32[16,8,128]{2,1,0:T(8,128)S(1)} async-done(((f32[16,8,128]{2,1,0:T(8,128)}), f32[16,8,128]{2,1,0:T(8,128)S(1)}, u32[]{:S(2)}, u32[]{:S(2)}) %all-to-all-start.4) | async-done | bytes 65568 | tf_op jit(solution)/shard_map/all_to_all | solution.py:136
  111.8 3.3 %all-to-all-start.9 = ((f32[16,8,128]{2,1,0:T(8,128)}), f32[16,8,128]{2,1,0:T(8,128)S(1)}, u32[]{:S(2)}, u32[]{:S(2)}) async-start(f32[16,8,128]{2,1,0:T(8,128)} %bitcast.47), calls=%async_computation.9 | async-start | bytes 131072 | tf_op jit(solution)/shard_map/all_to_all | solution.py:156
  115.7 3.5 %all-to-all-done.9 = f32[16,8,128]{2,1,0:T(8,128)S(1)} async-done(((f32[16,8,128]{2,1,0:T(8,128)}), f32[16,8,128]{2,1,0:T(8,128)S(1)}, u32[]{:S(2)}, u32[]{:S(2)}) %all-to-all-start.9) | async-done | bytes 65568 | tf_op jit(solution)/shard_map/all_to_all | solution.py:156
  119.2 3.3 %all-to-all-start.12 = ((f32[8,16,128]{2,0,1:T(8,128)}), f32[8,16,128]{2,0,1:T(8,128)S(1)}, u32[]{:S(2)}, u32[]{:S(2)}) async-start(f32[8,16,128]{2,0,1:T(8,128)} %copy.75), calls=%async_computation.12 | async-start | bytes 131072 | tf_op jit(solution)/shard_map/all_to_all | solution.py:176
  123.2 3.4 %all-to-all-done.12 = f32[8,16,128]{2,0,1:T(8,128)S(1)} async-done(((f32[8,16,128]{2,0,1:T(8,128)}), f32[8,16,128]{2,0,1:T(8,128)S(1)}, u32[]{:S(2)}, u32[]{:S(2)}) %all-to-all-start.12) | async-done | bytes 65568 | tf_op jit(solution)/shard_map/all_to_all | solution.py:176
  126.6 3.3 %all-to-all-start.10 = ((f32[8,16,128]{2,0,1:T(8,128)}), f32[8,16,128]{2,0,1:T(8,128)S(1)}, u32[]{:S(2)}, u32[]{:S(2)}) async-start(f32[8,16,128]{2,0,1:T(8,128)} %copy.70), calls=%async_computation.10 | async-start | bytes 131072 | tf_op jit(solution)/shard_map/all_to_all | solution.py:167
  130.6 3.5 %all-to-all-done.10 = f32[8,16,128]{2,0,1:T(8,128)S(1)} async-done(((f32[8,16,128]{2,0,1:T(8,128)}), f32[8,16,128]{2,0,1:T(8,128)S(1)}, u32[]{:S(2)}, u32[]{:S(2)}) %all-to-all-start.10) | async-done | bytes 65568 | tf_op jit(solution)/shard_map/all_to_all | solution.py:167
  134.0 5.9 %all-to-all-start.13 = ((f32[16,8,128]{2,0,1:T(8,128)}), f32[16,8,128]{2,0,1:T(8,128)S(1)}, u32[]{:S(2)}, u32[]{:S(2)}) async-start(f32[16,8,128]{2,0,1:T(8,128)} %copy.78), calls=%async_computation.13 | async-start | bytes 131072 | tf_op jit(solution)/shard_map/all_to_all | solution.py:175
  140.6 5.1 %all-to-all-done.13 = f32[16,8,128]{2,0,1:T(8,128)S(1)} async-done(((f32[16,8,128]{2,0,1:T(8,128)}), f32[16,8,128]{2,0,1:T(8,128)S(1)}, u32[]{:S(2)}, u32[]{:S(2)}) %all-to-all-start.13) | async-done | bytes 65568 | tf_op jit(solution)/shard_map/all_to_all | solution.py:175
  145.7 3.3 %all-to-all-start.11 = ((f32[16,8,128]{2,0,1:T(8,128)}), f32[16,8,128]{2,0,1:T(8,128)S(1)}, u32[]{:S(2)}, u32[]{:S(2)}) async-start(f32[16,8,128]{2,0,1:T(8,128)} %copy.73), calls=%async_computation.11 | async-start | bytes 131072 | tf_op jit(solution)/shard_map/all_to_all | solution.py:166
  149.1 5.7 %all-to-all-done.11 = f32[16,8,128]{2,0,1:T(8,128)S(1)} async-done(((f32[16,8,128]{2,0,1:T(8,128)}), f32[16,8,128]{2,0,1:T(8,128)S(1)}, u32[]{:S(2)}, u32[]{:S(2)}) %all-to-all-start.11) | async-done | bytes 65568 | tf_op jit(solution)/shard_map/all_to_all | solution.py:166
  155.9 8.1 %all_to_all.252 = f32[64,2,128]{2,1,0:T(2,128)S(1)} all-to-all(f32[64,2,128]{2,1,0:T(2,128)S(1)} %copy.81), channel_id=1, replica_groups=mesh['gx'=4,'gy'=2,'gz'=4] {'gz'}, dimensions={0} | all-to-all | bytes 131072 | tf_op jit(solution)/shard_map/all_to_all | solution.py:183
  (182 shorter events, 35.8 us)
Async XLA Ops:
  1.8 9.0 %copy-start = (f32[16,8,128]{2,1,0:T(8,128)S(1)}, f32[16,8,128]{2,1,0:T(8,128)}, u32[]{:S(2)}) copy-start(f32[16,8,128]{2,1,0:T(8,128)} %param.4) | copy-start | bytes 196612
  10.9 3.7 %collective-permute-start = (f32[2,16,8,1]{3,2,1,0:T(8,128)S(1)}, f32[2,16,8,1]{3,2,1,0:T(8,128)S(1)}, u32[]{:S(2)}, u32[]{:S(2)}) collective-permute-start(f32[2,16,8,1]{3,2,1,0:T(8,128)S(1)} %get-tuple-element.66), channel_id=1, source_target_pairs={{0,8},{8,16},{16,24},{1,9},{9,17},{17,25},{2,10},{10,18},{18,26},{... | collective-permute-start | bytes 3080 | tf_op jit(solution)/shard_map/ppermute | solution.py:16
  13.3 5.3 %collective-permute-start.1 = (f32[2,16,8,1]{3,2,1,0:T(8,128)S(1)}, f32[2,16,8,1]{3,2,1,0:T(8,128)S(1)}, u32[]{:S(2)}, u32[]{:S(2)}) collective-permute-start(f32[2,16,8,1]{3,2,1,0:T(8,128)S(1)} %get-tuple-element.67), channel_id=1, source_target_pairs={{8,0},{16,8},{24,16},{9,1},{17,9},{25,17},{10,2},{18,10},{26,18},{... | collective-permute-start | bytes 3080 | tf_op jit(solution)/shard_map/ppermute | solution.py:19
  18.9 5.0 %collective-permute-start.2 = (f32[2,16,1,130]{3,2,1,0:T(1,128)S(1)}, f32[2,16,1,130]{3,2,1,0:T(1,128)S(1)}, u32[]{:S(2)}, u32[]{:S(2)}) collective-permute-start(f32[2,16,1,130]{3,2,1,0:T(1,128)S(1)} %get-tuple-element.57), channel_id=1, source_target_pairs={{0,4},{1,5},{2,6},{3,7},{8,12},{9,13},{10,14},{11,15},{16,20},{17,... | collective-permute-start | bytes 49928 | tf_op jit(solution)/shard_map/ppermute | solution.py:16
  22.4 10.8 %copy-start.1 = (s32[16,8,128]{2,1,0:T(8,128)S(1)}, s32[16,8,128]{2,1,0:T(8,128)}, u32[]{:S(2)}) copy-start(s32[16,8,128]{2,1,0:T(8,128)} %param.5) | copy-start | bytes 196612
  22.4 5.9 %collective-permute-start.3 = (f32[2,16,1,130]{3,2,1,0:T(1,128)S(1)}, f32[2,16,1,130]{3,2,1,0:T(1,128)S(1)}, u32[]{:S(2)}, u32[]{:S(2)}) collective-permute-start(f32[2,16,1,130]{3,2,1,0:T(1,128)S(1)} %get-tuple-element.58), channel_id=1, source_target_pairs={{4,0},{5,1},{6,2},{7,3},{12,8},{13,9},{14,10},{15,11},{20,16},{21,... | collective-permute-start | bytes 49928 | tf_op jit(solution)/shard_map/ppermute | solution.py:19
  28.4 18.1 %collective-permute-start.4 = (f32[2,1,10,130]{3,2,1,0:T(8,128)S(1)}, f32[2,1,10,130]{3,2,1,0:T(8,128)S(1)}, u32[]{:S(2)}, u32[]{:S(2)}) collective-permute-start(f32[2,1,10,130]{3,2,1,0:T(8,128)S(1)} %get-tuple-element.55), channel_id=1, source_target_pairs={{0,1},{1,2},{2,3},{4,5},{5,6},{6,7},{8,9},{9,10},{10,11},{12,13},{... | collective-permute-start | bytes 31208 | tf_op jit(solution)/shard_map/ppermute | solution.py:16
  31.9 14.6 %collective-permute-start.5 = (f32[2,1,10,130]{3,2,1,0:T(8,128)S(1)}, f32[2,1,10,130]{3,2,1,0:T(8,128)S(1)}, u32[]{:S(2)}, u32[]{:S(2)}) collective-permute-start(f32[2,1,10,130]{3,2,1,0:T(8,128)S(1)} %get-tuple-element.56), channel_id=1, source_target_pairs={{1,0},{2,1},{3,2},{5,4},{6,5},{7,6},{9,8},{10,9},{11,10},{13,12},{... | collective-permute-start | bytes 31208 | tf_op jit(solution)/shard_map/ppermute | solution.py:19
  42.0 8.7 %all-to-all-start.1 = ((f32[16,8,128]{2,1,0:T(8,128)}), f32[16,8,128]{2,1,0:T(8,128)S(1)}, u32[]{:S(2)}, u32[]{:S(2)}) async-start(f32[16,8,128]{2,1,0:T(8,128)} %select_add_fusion), calls=%async_computation.1 | async-start | bytes 131072 | tf_op jit(solution)/shard_map/all_to_all | solution.py:129
  47.2 0.7 copy-start.2
  50.6 7.4 %all-to-all-start = ((f32[16,8,128]{2,1,0:T(8,128)}), f32[16,8,128]{2,1,0:T(8,128)S(1)}, u32[]{:S(2)}, u32[]{:S(2)}) async-start(f32[16,8,128]{2,1,0:T(8,128)} %get-tuple-element.46), calls=%async_computation | async-start | bytes 131072 | tf_op jit(solution)/shard_map/all_to_all | solution.py:130
  58.0 7.4 %all-to-all-start.2 = ((f32[16,8,128]{2,1,0:T(8,128)}), f32[16,8,128]{2,1,0:T(8,128)S(1)}, u32[]{:S(2)}, u32[]{:S(2)}) async-start(f32[16,8,128]{2,1,0:T(8,128)} %get-tuple-element.47), calls=%async_computation.2 | async-start | bytes 131072 | tf_op jit(solution)/shard_map/all_to_all | solution.py:131
  65.4 7.4 %all-to-all-start.7 = ((f32[16,8,128]{2,1,0:T(8,128)}), f32[16,8,128]{2,1,0:T(8,128)S(1)}, u32[]{:S(2)}, u32[]{:S(2)}) async-start(f32[16,8,128]{2,1,0:T(8,128)} %get-tuple-element.48), calls=%async_computation.7 | async-start | bytes 131072 | tf_op jit(solution)/shard_map/all_to_all | solution.py:132
  72.8 7.4 %all-to-all-start.5 = ((f32[4,1,4096]{2,1,0:T(1,128)}), f32[4,1,4096]{2,1,0:T(1,128)S(1)}, u32[]{:S(2)}, u32[]{:S(2)}) async-start(f32[4,1,4096]{2,1,0:T(1,128)} %reshape.12), calls=%async_computation.5 | async-start | bytes 131072 | tf_op jit(solution)/shard_map/all_to_all | solution.py:150
  80.2 7.4 %all-to-all-start.3 = ((f32[4,1,4096]{2,1,0:T(1,128)}), f32[4,1,4096]{2,1,0:T(1,128)S(1)}, u32[]{:S(2)}, u32[]{:S(2)}) async-start(f32[4,1,4096]{2,1,0:T(1,128)} %reshape.16), calls=%async_computation.3 | async-start | bytes 131072 | tf_op jit(solution)/shard_map/all_to_all | solution.py:137
  87.6 7.4 %all-to-all-start.8 = ((f32[4,1,4096]{2,1,0:T(1,128)}), f32[4,1,4096]{2,1,0:T(1,128)S(1)}, u32[]{:S(2)}, u32[]{:S(2)}) async-start(f32[4,1,4096]{2,1,0:T(1,128)} %reshape.14), calls=%async_computation.8 | async-start | bytes 131072 | tf_op jit(solution)/shard_map/all_to_all | solution.py:157
  95.0 9.4 %all-to-all-start.6 = ((f32[16,8,128]{2,1,0:T(8,128)}), f32[16,8,128]{2,1,0:T(8,128)S(1)}, u32[]{:S(2)}, u32[]{:S(2)}) async-start(f32[16,8,128]{2,1,0:T(8,128)} %bitcast.37), calls=%async_computation.6 | async-start | bytes 131072 | tf_op jit(solution)/shard_map/all_to_all | solution.py:149
  104.4 7.4 %all-to-all-start.4 = ((f32[16,8,128]{2,1,0:T(8,128)}), f32[16,8,128]{2,1,0:T(8,128)S(1)}, u32[]{:S(2)}, u32[]{:S(2)}) async-start(f32[16,8,128]{2,1,0:T(8,128)} %bitcast.31), calls=%async_computation.4 | async-start | bytes 131072 | tf_op jit(solution)/shard_map/all_to_all | solution.py:136
  111.8 7.4 %all-to-all-start.9 = ((f32[16,8,128]{2,1,0:T(8,128)}), f32[16,8,128]{2,1,0:T(8,128)S(1)}, u32[]{:S(2)}, u32[]{:S(2)}) async-start(f32[16,8,128]{2,1,0:T(8,128)} %bitcast.47), calls=%async_computation.9 | async-start | bytes 131072 | tf_op jit(solution)/shard_map/all_to_all | solution.py:156
  119.2 7.4 %all-to-all-start.12 = ((f32[8,16,128]{2,0,1:T(8,128)}), f32[8,16,128]{2,0,1:T(8,128)S(1)}, u32[]{:S(2)}, u32[]{:S(2)}) async-start(f32[8,16,128]{2,0,1:T(8,128)} %copy.75), calls=%async_computation.12 | async-start | bytes 131072 | tf_op jit(solution)/shard_map/all_to_all | solution.py:176
  126.6 7.4 %all-to-all-start.10 = ((f32[8,16,128]{2,0,1:T(8,128)}), f32[8,16,128]{2,0,1:T(8,128)S(1)}, u32[]{:S(2)}, u32[]{:S(2)}) async-start(f32[8,16,128]{2,0,1:T(8,128)} %copy.70), calls=%async_computation.10 | async-start | bytes 131072 | tf_op jit(solution)/shard_map/all_to_all | solution.py:167
  134.0 11.7 %all-to-all-start.13 = ((f32[16,8,128]{2,0,1:T(8,128)}), f32[16,8,128]{2,0,1:T(8,128)S(1)}, u32[]{:S(2)}, u32[]{:S(2)}) async-start(f32[16,8,128]{2,0,1:T(8,128)} %copy.78), calls=%async_computation.13 | async-start | bytes 131072 | tf_op jit(solution)/shard_map/all_to_all | solution.py:175
  145.7 9.1 %all-to-all-start.11 = ((f32[16,8,128]{2,0,1:T(8,128)}), f32[16,8,128]{2,0,1:T(8,128)S(1)}, u32[]{:S(2)}, u32[]{:S(2)}) async-start(f32[16,8,128]{2,0,1:T(8,128)} %copy.73), calls=%async_computation.11 | async-start | bytes 131072 | tf_op jit(solution)/shard_map/all_to_all | solution.py:166
where the time goes:
time: 167 us; the launch traced here: 165 us
  starting transfers between devices  63.4 us (38%)
  waiting for transfers between devices  44.1 us (26%)
  other arithmetic  25.7 us (15%)
  local copies, waits for them, and re-layouts  22.3 us (13%)
  blocking collectives  8.11 us (5%)
    unnamed x12, local copies, waits for them, and re-layouts  9.75 us
    ppermute x3, starting transfers between devices, with_halo(): lax.ppermute(lax.slice_in_dim(block, block.shape[dim] - width, None, axis...  9.27 us
    another operation x2, other arithmetic, local(): jnp.stack([thermal_anomaly, local_thermal_rate])  9.09 us
    add x1, other arithmetic, local(): local_thermal_rate + jnp.where(material_label == table_entry, label_therm...  8.75 us
    ppermute x3, waiting for transfers between devices, with_halo(): lax.ppermute(lax.slice_in_dim(block, 0, width, axis=dim), axis, backward)  8.41 us
    all_to_all x1, blocking collectives, local(): lax.all_to_all(vertical_solve(conduct_z, source_z, bottom_edge_option), '...  8.11 us
    all_to_all x1, starting transfers between devices, local(): lax.all_to_all(lax.all_to_all(conduct_y, 'gy', split_axis=1, concat_axis=...  5.94 us
    all_to_all x1, waiting for transfers between devices, local(): lax.all_to_all(lax.all_to_all(after_y - THETA_FACTOR * across_z_y, 'gy',...  5.69 us
  transfers between devices with their start and end apart: 20, of which 15 were waited for; matrix products, arithmetic and copies ran while one was open for 21% of the time, Pallas kernels for 0%

commit v1 on v0

v1 whole, which is shorter than its diff:
```python
import functools

import jax
import jax.numpy as jnp
from jax import lax
from jax.experimental import pallas as pl
from jax.experimental.pallas import tpu as pltpu
from jax.sharding import PartitionSpec as P

FLAT_SCALE = 1000.0
UPWARD_SCALE = 200.0
F32 = jnp.float32


def link_of(scale, one, other):
    return scale * one * other / (one + other)


def roll(values, offset, axis):
    if axis == 0 and values.ndim == 3:
        offset = offset % values.shape[0]
        return jnp.concatenate([values[-offset:], values[:-offset]], 0)
    return pltpu.roll(values, offset % values.shape[axis], axis)


def steps_of(length):
    steps, distance = [], 1
    while distance < length - 1:
        steps.append(distance)
        distance *= 2
    return steps


def reduce_interior(link, axis, left_ref, right_ref):
    length = link.shape[axis]
    row = lax.broadcasted_iota(jnp.int32, link.shape, axis)
    low, high, own = link, roll(link, -1, axis), jnp.ones_like(link)
    high = jnp.where(row == length - 1, 0.0, high)
    for step, distance in enumerate(steps_of(length)):
        inverse = 1.0 / (own + low + high)
        open_low, open_high = row > distance, row < length - 1 - distance
        left = jnp.where(open_low, low * roll(inverse, distance, axis), 0.0)
        right = jnp.where(open_high, high * roll(inverse, -distance, axis), 0.0)
        left_ref[step], right_ref[step] = left, right
        own = own + left * roll(own, distance, axis) + right * roll(own, -distance, axis)
        low = jnp.where(open_low, left * roll(low, distance, axis), low)
        high = jnp.where(open_high, right * roll(high, -distance, axis), high)
    inverse = 1.0 / (own + low + high)
    inner = (row > 0) & (row < length - 1)
    share_low = jnp.where(inner, low * inverse, jnp.where(row == 0, 1.0, 0.0))
    share_high = jnp.where(inner, high * inverse, jnp.where(row == 0, 0.0, 1.0))
    return share_low, share_high, jnp.where(inner, inverse, 0.0), own * inverse


def reduce_source(source, axis, left_ref, right_ref, inverse):
    length = source.shape[axis]
    for step, distance in enumerate(steps_of(length)):
        source = (
            source
            + left_ref[step] * roll(source, distance, axis)
            + right_ref[step] * roll(source, -distance, axis)
        )
    return source * inverse


def chain(blocks, count, index, state):
    own = [blocks[k][3] + (blocks[k + 1][1] if k + 1 < count else 0.0) for k in range(count)]
    source = [blocks[k][4] + (blocks[k + 1][2] if k + 1 < count else 0.0) for k in range(count)]
    shape = own[0].shape
    state[0, 0], state[1, 0] = jnp.ones(shape, F32), jnp.zeros(shape, F32)
    up_own, up_source = own[0], source[0]
    for k in range(1, count):
        state[0, k], state[1, k] = up_own, up_source
        factor = blocks[k][0] / (up_own + blocks[k][0])
        up_own, up_source = own[k] + factor * up_own, source[k] + factor * up_source
    down_own, down_source = own[count - 1], source[count - 1]
    state[2, count - 1], state[3, count - 1] = down_own, down_source
    for k in range(count - 2, -1, -1):
        factor = blocks[k + 1][0] / (down_own + blocks[k + 1][0])
        down_own, down_source = own[k] + factor * down_own, source[k] + factor * down_source
        state[2, k], state[3, k] = down_own, down_source
    for k in range(count):
        state[4, k] = blocks[k][0]
    up_own, up_source, down_own, down_source, link = (state[i, index] for i in range(5))
    inverse = 1.0 / (up_own * down_own + link * (up_own + down_own))
    below = ((down_own + link) * up_source + link * down_source) * inverse
    here = ((up_own + link) * down_source + link * up_source) * inverse
    return below, here


def pick_halo(name, received, odd):
    first = received[0][...]
    second = received[1][...] if len(received) > 1 else jnp.zeros_like(first)
    index, count = lax.axis_index(name), lax.axis_size(name)
    below = jnp.where(odd, first, second)
    above = jnp.where(odd, second, first)
    return jnp.where(index > 0, below, 0.0), jnp.where(index < count - 1, above, 0.0)


def start_kernel(heat_ref, label_ref, table_ref, conduct_ref, za_ref, zb_ref, ya_ref, yb_ref):
    label = label_ref[...]
    conduct = jnp.full(label.shape, table_ref[0], F32)
    for entry in range(1, table_ref.shape[0]):
        conduct = jnp.where(label == entry, table_ref[entry], conduct)
    conduct_ref[...] = conduct
    odd_z = lax.axis_index("gz") % 2 == 1
    odd_y = lax.axis_index("gy") % 2 == 1
    for i, ref in enumerate((heat_ref, conduct_ref)):
        low, high = ref[0], ref[ref.shape[0] - 1]
        za_ref[i] = jnp.where(odd_z, low, high)
        zb_ref[i] = jnp.where(odd_z, high, low)
        low, high = ref[:, 0, :], ref[:, ref.shape[1] - 1, :]
        ya_ref[i] = jnp.where(odd_y, low, high)
        yb_ref[i] = jnp.where(odd_y, high, low)


def x_bands_kernel(
    heat_ref, conduct_ref, left_ref, right_ref, low_ref, high_ref, inverse_ref, ends_ref, local_ref
):
    nz, ny, nx = conduct_ref.shape
    conduct = conduct_ref[...]
    heat = heat_ref[...]
    local = 2.0 * heat
    across = 2.0 * link_of(UPWARD_SCALE, conduct[1:], conduct[:-1]) * (heat[1:] - heat[:-1])
    nothing = jnp.zeros_like(heat[:1])
    local = local + jnp.concatenate([across, nothing], 0) - jnp.concatenate([nothing, across], 0)
    row = lax.broadcasted_iota(jnp.int32, conduct.shape, 1)
    across = 2.0 * link_of(FLAT_SCALE, conduct, roll(conduct, 1, 1)) * (heat - roll(heat, 1, 1))
    across = jnp.where(row > 0, across, 0.0)
    local_ref[...] = local - across + roll(across, -1, 1)
    lines = conduct.reshape(nz * ny, nx).T
    row = lax.broadcasted_iota(jnp.int32, lines.shape, 0)
    link = jnp.where(row > 0, link_of(FLAT_SCALE, lines, roll(lines, 1, 0)), 0.0)
    low, high, inverse, own = reduce_interior(link, 0, left_ref, right_ref)
    low_ref[...], high_ref[...], inverse_ref[...] = low, high, inverse
    first, last = link[1:2], link[nx - 1 :]
    ends_ref[...] = jnp.concatenate(
        [
            first,
            last,
            1.0 + first * own[1:2],
            1.0 + last * own[nx - 2 : nx - 1],
            first * high[1:2],
            lines[:1],
            lines[nx - 1 :],
            jnp.zeros_like(first),
        ],
        0,
    )


def x_source_kernel(
    halo_counts, heat_ref, conduct_ref, edge_ref, local_ref, left_ref, right_ref, inverse_ref,
    ends_ref, *refs
):
    z_halo, y_halo = refs[: halo_counts[0]], refs[halo_counts[0] : sum(halo_counts)]
    part_ref, message_ref, source_ref = refs[sum(halo_counts) :]
    nz, ny, nx = conduct_ref.shape
    index_z, index_y = lax.axis_index("gz"), lax.axis_index("gy")
    below, above = pick_halo("gz", z_halo, index_z % 2 == 1)
    source_ref[...] = local_ref[...]
    ground = UPWARD_SCALE * conduct_ref[0] * edge_ref[...].astype(F32)
    ground = jnp.where(index_z == 0, ground, 0.0)
    flow = link_of(UPWARD_SCALE, conduct_ref[0], below[1]) * (below[0] - heat_ref[0])
    source_ref[0] += 2.0 * (flow - ground * heat_ref[0])
    flow = link_of(UPWARD_SCALE, conduct_ref[nz - 1], above[1]) * (above[0] - heat_ref[nz - 1])
    source_ref[nz - 1] += 2.0 * flow
    below, above = pick_halo("gy", y_halo, index_y % 2 == 1)
    flow = link_of(FLAT_SCALE, conduct_ref[:, 0, :], below[1]) * (below[0] - heat_ref[:, 0, :])
    source_ref[:, 0, :] += 2.0 * flow
    flow = link_of(FLAT_SCALE, conduct_ref[:, ny - 1, :], above[1])
    source_ref[:, ny - 1, :] += 2.0 * flow * (above[0] - heat_ref[:, ny - 1, :])
    source = source_ref[...].reshape(nz * ny, nx).T
    part = reduce_source(source, 0, left_ref, right_ref, inverse_ref[...])
    part_ref[...] = part
    message_ref[...] = jnp.concatenate(
        [
            source[:1] + ends_ref[0:1] * part[1:2],
            source[nx - 1 :] + ends_ref[1:2] * part[nx - 2 : nx - 1],
            ends_ref[2:8],
        ],
        0,
    )


def end_bands(link, first, last, axis, high, own):
    length = high.shape[axis]
    at = lambda values, i: lax.index_in_dim(values, i, axis, keepdims=False)
    return (
        1.0 + first * at(own, 1),
        1.0 + last * at(own, length - 2),
        first * at(high, 1),
    )


def yz_bands_kernel(
    halo_counts, conduct_ref, edge_ref, *refs
):
    z_halo, y_halo = refs[: halo_counts[0]], refs[halo_counts[0] : sum(halo_counts)]
    (
        yl_ref, yr_ref, ylow_ref, yhigh_ref, yinv_ref, yends_ref,
        zl_ref, zr_ref, zlow_ref, zhigh_ref, zinv_ref, zends_ref,
    ) = refs[sum(halo_counts) :]
    nz, ny, nx = conduct_ref.shape
    index_z, index_y = lax.axis_index("gz"), lax.axis_index("gy")
    conduct = conduct_ref[...]
    row = lax.broadcasted_iota(jnp.int32, conduct.shape, 1)
    link = jnp.where(row > 0, link_of(FLAT_SCALE, conduct, roll(conduct, 1, 1)), 0.0)
    low, high, inverse, own = reduce_interior(link, 1, yl_ref, yr_ref)
    ylow_ref[...], yhigh_ref[...], yinv_ref[...] = low, high, inverse
    below, above = pick_halo("gy", y_halo, index_y % 2 == 1)
    first = link_of(FLAT_SCALE, conduct_ref[:, 0, :], conduct_ref[:, 1, :])
    last = link_of(FLAT_SCALE, conduct_ref[:, ny - 1, :], conduct_ref[:, ny - 2, :])
    own_first, own_last, between = end_bands(link, first, last, 1, high, own)
    outer_low = link_of(FLAT_SCALE, conduct_ref[:, 0, :], below[1])
    outer_high = link_of(FLAT_SCALE, conduct_ref[:, ny - 1, :], above[1])
    for i, value in enumerate((first, last, own_first, own_last, between, outer_low, outer_high)):
        yends_ref[i] = value
    link = link_of(UPWARD_SCALE, conduct[1:], conduct[:-1])
    link = jnp.concatenate([jnp.zeros_like(conduct[:1]), link], 0)
    low, high, inverse, own = reduce_interior(link, 0, zl_ref, zr_ref)
    zlow_ref[...], zhigh_ref[...], zinv_ref[...] = low, high, inverse
    below, above = pick_halo("gz", z_halo, index_z % 2 == 1)
    own_first, own_last, between = end_bands(link, link[1], link[nz - 1], 0, high, own)
    ground = UPWARD_SCALE * conduct[0] * edge_ref[...].astype(F32)
    own_first = own_first + jnp.where(index_z == 0, ground, 0.0)
    outer = link_of(UPWARD_SCALE, conduct[0], below[1])
    for i, value in enumerate((link[1], link[nz - 1], own_first, own_last, between, outer)):
        zends_ref[i] = value


def chain_message(ends_ref, source_first, source_last, message_ref):
    own_first, own_last, between, outer = (ends_ref[i] for i in range(2, 6))
    inverse = 1.0 / (own_first + between + outer)
    message_ref[0] = outer * between * inverse
    message_ref[1] = outer * own_first * inverse
    message_ref[2] = outer * inverse * source_first
    message_ref[3] = own_last + between * own_first * inverse
    message_ref[4] = source_last + between * inverse * source_first


def chain_ends(name, messages, ends_ref, source_first, blocks_ref, state_ref):
    count, index = lax.axis_size(name), lax.axis_index(name)
    for mask, message in enumerate(messages):
        blocks_ref[index ^ mask] = message[...]
    blocks = [tuple(blocks_ref[k, i] for i in range(5)) for k in range(count)]
    below, last = chain(blocks, count, index, state_ref)
    own_first, between, outer = ends_ref[2], ends_ref[4], ends_ref[5]
    first = (source_first + outer * below + between * last) / (own_first + between + outer)
    return first, last


def y_source_kernel(
    count_x, count_y, heat_ref, part_ref, low_ref, high_ref, yl_ref, yr_ref, yinv_ref, yends_ref,
    *refs
):
    messages, (ypart_ref, ysource_ref, message_ref, blocks_ref, rows_ref, state_ref, d_ref) = (
        refs[:count_x], refs[count_x:]
    )
    nz, ny, nx = heat_ref.shape
    index = lax.axis_index("gx")
    for mask, message in enumerate(messages):
        blocks_ref[index ^ mask] = message[...]
    first, last, own_first, own_last, between, c_first, c_last = (
        blocks_ref[:, i, :] for i in range(7)
    )
    before = jnp.concatenate([jnp.zeros_like(c_last[:1]), c_last[:-1]], 0)
    outer = link_of(FLAT_SCALE, c_first, before)
    inverse = 1.0 / (own_first + between + outer)
    rows = (
        outer * between * inverse,
        outer * own_first * inverse,
        outer * inverse * first,
        own_last + between * own_first * inverse,
        last + between * inverse * first,
        first * inverse,
        outer * inverse,
        between * inverse,
    )
    for i, value in enumerate(rows):
        rows_ref[i] = value
    whole = lambda i, k: jnp.broadcast_to(rows_ref[i, pl.ds(k, 1), :], (8, rows_ref.shape[2]))
    blocks = [tuple(whole(i, k) for i in range(5)) for k in range(count_x)]
    below, last = chain(blocks, count_x, index, state_ref)
    first = whole(5, index) + whole(6, index) * below + whole(7, index) * last
    lines = part_ref[...] + low_ref[...] * first[:1] + high_ref[...] * last[:1]
    source = lines.T.reshape(nz, ny, nx) - 2.0 * heat_ref[...]
    d_ref[...] = source
    part = reduce_source(source, 1, yl_ref, yr_ref, yinv_ref[...])
    ypart_ref[...] = part
    source_first = d_ref[:, 0, :] + yends_ref[0] * ypart_ref[:, 1, :]
    source_last = d_ref[:, ny - 1, :] + yends_ref[1] * ypart_ref[:, ny - 2, :]
    ysource_ref[0], ysource_ref[1] = source_first, source_last
    if count_y > 2:
        chain_message(yends_ref, source_first, source_last, message_ref)
        return
    odd = lax.axis_index("gy") % 2 == 1
    near_own = jnp.where(odd, yends_ref[2], yends_ref[3])
    far_own = jnp.where(odd, yends_ref[3], yends_ref[2])
    share = yends_ref[4] / (far_own + yends_ref[4])
    message_ref[0] = near_own + share * far_own
    message_ref[1] = jnp.where(odd, source_first, source_last) + share * jnp.where(
        odd, source_last, source_first
    )


def z_source_kernel(
    count_y, ypart_ref, ylow_ref, yhigh_ref, yends_ref, ysource_ref, zl_ref, zr_ref, zinv_ref,
    zends_ref, *refs
):
    messages, (zpart_ref, zsource_ref, message_ref, ends_ref, blocks_ref, state_ref) = (
        refs[:count_y], refs[count_y:]
    )
    nz, ny, nx = ypart_ref.shape
    if count_y > 2:
        first, last = chain_ends("gy", messages, yends_ref, ysource_ref[0], blocks_ref, state_ref)
    else:
        odd = lax.axis_index("gy") % 2 == 1
        mine, other = messages
        outer = jnp.where(odd, yends_ref[5], yends_ref[6])
        between = yends_ref[4]
        factor = outer / (other[0] + outer)
        near = (mine[1] + factor * other[1]) / (mine[0] + factor * other[0])
        far_own = jnp.where(odd, yends_ref[3], yends_ref[2])
        far_source = jnp.where(odd, ysource_ref[1], ysource_ref[0])
        far = (far_source + between * near) / (far_own + between)
        first, last = jnp.where(odd, near, far), jnp.where(odd, far, near)
    ends_ref[0], ends_ref[1] = first, last
    source = jnp.stack(
        [
            ypart_ref[k]
            + ylow_ref[k] * ends_ref[0, pl.ds(k, 1), :]
            + yhigh_ref[k] * ends_ref[1, pl.ds(k, 1), :]
            for k in range(nz)
        ],
        0,
    )
    part = reduce_source(source, 0, zl_ref, zr_ref, zinv_ref[...])
    zpart_ref[...] = part
    source_first = source[0] + zends_ref[0] * part[1]
    source_last = source[nz - 1] + zends_ref[1] * part[nz - 2]
    zsource_ref[...] = source_first
    chain_message(zends_ref, source_first, source_last, message_ref)


def finish_kernel(
    count_z, heat_ref, zpart_ref, zlow_ref, zhigh_ref, zends_ref, zsource_ref, *refs
):
    messages, (out_ref, blocks_ref, state_ref) = refs[:count_z], refs[count_z:]
    first, last = chain_ends("gz", messages, zends_ref, zsource_ref[...], blocks_ref, state_ref)
    out_ref[...] = heat_ref[...] + zpart_ref[...] + zlow_ref[...] * first + zhigh_ref[...] * last


VMEM = pl.BlockSpec(memory_space=pltpu.VMEM)
SMEM = pl.BlockSpec(memory_space=pltpu.SMEM)


def call(kernel, outs, operands, scratch=(), specs=None, ops=200_000):
    return pl.pallas_call(
        kernel,
        out_shape=[jax.ShapeDtypeStruct(shape, F32) for shape in outs],
        in_specs=specs or [VMEM] * len(operands),
        out_specs=[VMEM] * len(outs),
        scratch_shapes=[pltpu.VMEM(shape, F32) for shape in scratch],
        compiler_params=pltpu.CompilerParams(vmem_limit_bytes=32 * 1024 * 1024),
        cost_estimate=pl.CostEstimate(flops=ops, bytes_accessed=ops, transcendentals=0),
    )(*operands)


def neighbour_swaps(name, other, low_first, second):
    count, width = lax.axis_size(name), lax.axis_size(other)
    received = [lax.ppermute(low_first, name, [(i, i ^ 1) for i in range(count)])]
    if count > 2:
        pairs = []
        for j in range(width):
            for i in range(count):
                at = (j ^ 1, i) if i in (0, count - 1) else (j, ((i + 1) ^ 1) - 1)
                pairs.append(((j, i), at))
        if (other, name) == ("gy", "gz"):
            axes, place = (other, name), lambda at: at[0] * count + at[1]
        else:
            axes, place = (name, other), lambda at: at[1] * width + at[0]
        pairs = [(place(source), place(target)) for source, target in pairs]
        received.append(lax.ppermute(second, axes, pairs))
    return received


def swap_all(name, message):
    count = lax.axis_size(name)
    return [message] + [
        lax.ppermute(message, name, [(i, i ^ mask) for i in range(count)])
        for mask in range(1, count)
    ]


def local(heat, label, table, edge):
    nz, ny, nx = heat.shape
    block, lines, layer, rows = (nz, ny, nx), (nx, nz * ny), (ny, nx), (nz, nx)
    count_x, count_y, count_z = (lax.axis_size(name) for name in ("gx", "gy", "gz"))
    x_steps, y_steps, z_steps = (len(steps_of(length)) for length in (nx, ny, nz))

    conduct, za, zb, ya, yb = call(
        start_kernel,
        [block, (2, *layer), (2, *layer), (2, *rows), (2, *rows)],
        [heat, label, table],
        specs=[VMEM, VMEM, SMEM],
    )
    z_halo = neighbour_swaps("gz", "gy", za, zb)
    y_halo = neighbour_swaps("gy", "gz", ya, yb)
    halo_counts = (len(z_halo), len(y_halo))

    x_left, x_right, x_low, x_high, x_inverse, x_ends, source = call(
        x_bands_kernel,
        [(x_steps, *lines)] * 2 + [lines] * 3 + [(8, lines[1]), block],
        [heat, conduct],
    )
    x_part, x_message = call(
        functools.partial(x_source_kernel, halo_counts),
        [lines, (8, lines[1])],
        [heat, conduct, edge, source, x_left, x_right, x_inverse, x_ends, *z_halo, *y_halo],
        [block],
    )
    x_messages = swap_all("gx", x_message)
    (
        y_left, y_right, y_low, y_high, y_inverse, y_ends,
        z_left, z_right, z_low, z_high, z_inverse, z_ends,
    ) = call(
        functools.partial(yz_bands_kernel, halo_counts),
        [(y_steps, *block)] * 2 + [block] * 3 + [(7, *rows)]
        + [(z_steps, *block)] * 2 + [block] * 3 + [(6, *layer)],
        [conduct, edge, *z_halo, *y_halo],
    )
    y_rows = 5 if count_y > 2 else 2
    y_part, y_source, y_message = call(
        functools.partial(y_source_kernel, count_x, count_y),
        [block, (2, *rows), (y_rows, *rows)],
        [heat, x_part, x_low, x_high, y_left, y_right, y_inverse, y_ends, *x_messages],
        [(count_x, 8, lines[1]), (8, count_x, lines[1]), (5, count_x, 8, lines[1]), block],
    )
    y_messages = swap_all("gy", y_message)
    z_part, z_source, z_message = call(
        functools.partial(z_source_kernel, count_y),
        [block, layer, (5, *layer)],
        [y_part, y_low, y_high, y_ends, y_source, z_left, z_right, z_inverse, z_ends, *y_messages],
        [(2, *rows), (count_y, y_rows, *rows), (5, count_y, *rows)],
    )
    z_messages = swap_all("gz", z_message)
    (heated,) = call(
        functools.partial(finish_kernel, count_z),
        [block],
        [heat, z_part, z_low, z_high, z_ends, z_source, *z_messages],
        [(count_z, 5, *layer), (5, count_z, *layer)],
    )
    return heated


def solution(mesh):
    return jax.shard_map(
        local,
        mesh=mesh,
        in_specs=(P("gz", "gy", "gx"), P("gz", "gy", "gx"), P(), P("gy", "gx")),
        out_specs=P("gz", "gy", "gx"),
        check_vma=False,
    )
```

time: 167 us -> 29 us (0.17); the launches traced: 165 us -> 28.8 us
  starting transfers between devices: 63.4 us -> 12 us
  waiting for transfers between devices: 44.1 us -> 10.4 us
  other arithmetic: 25.7 us -> 0 us
  local copies, waits for them, and re-layouts: 22.3 us -> 3.03 us
  blocking collectives: 8.11 us -> 0 us
  Pallas kernels: 0 us -> 3.25 us
    all_to_all x14 -> x0, starting transfers between devices: 50.2 us -> none  [the longest x1 5.94 us: local(): lax.all_to_all(lax.all_to_all(conduct_y, 'gy', split_axis=1, concat_axis=...]
    all_to_all x14 -> x0, waiting for transfers between devices: 35.6 us -> none  [the longest x1 5.69 us: local(): lax.all_to_all(lax.all_to_all(after_y - THETA_FACTOR * across_z_y, 'gy',...]
    add x3 -> x0, other arithmetic: 9.63 us -> none  [the longest x1 8.75 us: local(): local_thermal_rate + jnp.where(material_label == table_entry, label_therm...]
    another operation x2 -> x0, other arithmetic: 9.09 us -> none  [local(): jnp.stack([thermal_anomaly, local_thermal_rate])]
    all_to_all x1 -> x0, blocking collectives: 8.11 us -> none  [local(): lax.all_to_all(vertical_solve(conduct_z, source_z, bottom_edge_option), '...]
    all_to_all x22 -> x0, local copies, waits for them, and re-layouts: 6.83 us -> none  [the longest x3 1.48 us: local(): lax.all_to_all(lines_across_z, 'gx', split_axis=2, concat_axis=0, tiled=T...]
    unnamed x12 -> x10, local copies, waits for them, and re-layouts: 9.75 us -> 3.03 us
    slice x79 -> x0, local copies, waits for them, and re-layouts: 4.54 us -> none  [the longest x1 1.82 us: local(): label_thermal_table[table_entry]]
  transfers between devices with their start and end apart: 20 -> 10, of which waited for: 15 -> 7; matrix products, arithmetic and copies ran while one was open for 21% -> 0% of each run, Pallas kernels for 0% -> 3%
where the time goes in v1:
time: 29 us; the launch traced here: 28.8 us
  starting transfers between devices  12 us (41%)
  waiting for transfers between devices  10.4 us (36%)
  Pallas kernels  3.25 us (11%)
  local copies, waits for them, and re-layouts  3.03 us (10%)
    ppermute x7, waiting for transfers between devices, swap_all(): lax.ppermute(message, name, [(i, i ^ mask) for i in range(count)])  7.67 us
    ppermute x7, starting transfers between devices, swap_all(): lax.ppermute(message, name, [(i, i ^ mask) for i in range(count)])  6.96 us
    ppermute x2, starting transfers between devices, neighbour_swaps(): lax.ppermute(low_first, name, [(i, i ^ 1) for i in range(count)])  4.54 us
    pallas_call x7, Pallas kernels, call(): pl.pallas_call(kernel, out_shape=[jax.ShapeDtypeStruct(shape, F32) for sh...  3.25 us
    unnamed x10, local copies, waits for them, and re-layouts  3.03 us
    ppermute x1, waiting for transfers between devices, neighbour_swaps(): received.append(lax.ppermute(second, axes, pairs))  1.58 us
    ppermute x2, waiting for transfers between devices, neighbour_swaps(): lax.ppermute(low_first, name, [(i, i ^ 1) for i in range(count)])  1.18 us
  transfers between devices with their start and end apart: 10, of which 7 were waited for; matrix products, arithmetic and copies ran while one was open for 0% of the time, Pallas kernels for 3%

profile of v1, /device:TPU:0, one launch (start us, length us, event | category | flops | bytes accessed | tf_op | source)
XLA Modules:
  0.0 28.8 jit_solution(17514549399340376071)
XLA Ops:
  0.0 0.8 %copy-done = f32[16,8,128]{2,1,0:T(8,128)S(1)} copy-done((f32[16,8,128]{2,1,0:T(8,128)S(1)}, f32[16,8,128]{2,1,0:T(8,128)}, u32[]{:S(2)}) %copy-start) | copy-done | bytes 65560
  0.8 0.8 %copy-done.2 = s32[16,8,128]{2,1,0:T(8,128)S(1)} copy-done((s32[16,8,128]{2,1,0:T(8,128)S(1)}, s32[16,8,128]{2,1,0:T(8,128)}, u32[]{:S(2)}) %copy-start.2) | copy-done | bytes 65560
  1.7 0.7 %copy-done.4 = f32[13]{0:T(128)S(1)} copy-done((f32[13]{0:T(128)S(1)}, f32[13]{0:T(128)}, u32[]{:S(2)}) %copy-start.4) | copy-done | bytes 76
  2.3 1.2 %shard_map.46 = (f32[16,8,128]{2,1,0:T(8,128)S(1)}, f32[2,8,128]{2,1,0:T(8,128)S(1)}, f32[2,8,128]{2,1,0:T(8,128)S(1)}, f32[2,16,128]{2,1,0:T(8,128)S(1)}, f32[2,16,128]{2,1,0:T(8,128)}) custom-call(f32[16,8,128]{2,1,0:T(8,128)S(1)} %copy-done, s32[16,8,128]{2,1,0:T(8,128)S(1)} %copy-done.2, f32[13]{0:T(128)S(1)} %copy-done.4), custom_call_target="tpu_custom_call" | custom-call | flops 200000 | bytes 200000 | tf_op jit(solution)/shard_map/pallas_call | solution.py:359
  3.6 3.0 %collective-permute-start.2 = (f32[2,16,128]{2,1,0:T(8,128)S(1)}, f32[2,16,128]{2,1,0:T(8,128)S(1)}, u32[]{:S(2)}, u32[]{:S(2)}) collective-permute-start(f32[2,16,128]{2,1,0:T(8,128)S(1)} %get-tuple-element.44), channel_id=1, source_target_pairs={{0,4},{4,0},{1,5},{5,1},{2,6},{6,2},{3,7},{7,3},{8,12},{12,8},{9,1... | collective-permute-start | bytes 49160 | tf_op jit(solution)/shard_map/ppermute | solution.py:372
  6.5 1.6 %collective-permute-start = (f32[2,8,128]{2,1,0:T(8,128)S(1)}, f32[2,8,128]{2,1,0:T(8,128)S(1)}, u32[]{:S(2)}, u32[]{:S(2)}) collective-permute-start(f32[2,8,128]{2,1,0:T(8,128)S(1)} %get-tuple-element.42), channel_id=1, source_target_pairs={{0,1},{1,0},{2,3},{3,2},{4,5},{5,4},{6,7},{7,6},{8,9},{9,8},{10,11... | collective-permute-start | bytes 24584 | tf_op jit(solution)/shard_map/ppermute | solution.py:372
  8.1 0.5 %collective-permute-start.1 = (f32[2,8,128]{2,1,0:T(8,128)S(1)}, f32[2,8,128]{2,1,0:T(8,128)S(1)}, u32[]{:S(2)}, u32[]{:S(2)}) collective-permute-start(f32[2,8,128]{2,1,0:T(8,128)S(1)} %get-tuple-element.43), channel_id=1, source_target_pairs={{0,4},{1,2},{2,1},{3,7},{4,0},{5,6},{6,5},{7,3},{8,12},{9,10},{10,... | collective-permute-start | bytes 24584 | tf_op jit(solution)/shard_map/ppermute | solution.py:384
  8.6 0.4 %shard_map.47 = (f32[7,128,128]{2,1,0:T(8,128)S(1)}, f32[7,128,128]{2,1,0:T(8,128)S(1)}, f32[128,128]{1,0:T(8,128)S(1)}, f32[128,128]{1,0:T(8,128)S(1)}, f32[128...) custom-call(f32[16,8,128]{2,1,0:T(8,128)S(1)} %copy-done, ...), custom_call_target="tpu_custom_call" | custom-call | flops 200000 | bytes 200000 | tf_op jit(solution)/shard_map/pallas_call | solution.py:359
  9.0 1.2 %collective-permute-done.refs_0_ = f32[2,8,128]{2,1,0:T(8,128)S(1)} collective-permute-done((f32[2,8,128]{2,1,0:T(8,128)S(1)}, f32[2,8,128]{2,1,0:T(8,128)S(1)}, u32[]{:S(2)}, u32[]{:S(2)}) %collective-permute-start) | collective-permute-done | bytes 8224 | tf_op jit(solution)/shard_map/ppermute | solution.py:372
  10.2 1.6 %collective-permute-done.1.refs_1_ = f32[2,8,128]{2,1,0:T(8,128)S(1)} collective-permute-done((f32[2,8,128]{2,1,0:T(8,128)S(1)}, f32[2,8,128]{2,1,0:T(8,128)S(1)}, u32[]{:S(2)}, u32[]{:S(2)}) %collective-permute-start.1) | collective-permute-done | bytes 8224 | tf_op jit(solution)/shard_map/ppermute | solution.py:384
  11.8 0.0 collective-permute-done.2.refs_2_
  11.8 0.7 %copy-done.3 = s32[8,128]{1,0:T(8,128)S(1)} copy-done((s32[8,128]{1,0:T(8,128)S(1)}, s32[8,128]{1,0:T(8,128)}, u32[]{:S(2)}) %copy-start.3) | copy-done | bytes 4120
  12.5 0.2 shard_map.48
  12.7 0.0 copy-start.1
  12.7 0.1 collective-permute-start.5
  12.8 1.6 %collective-permute-start.4 = (f32[8,128]{1,0:T(8,128)S(1)}, f32[8,128]{1,0:T(8,128)S(1)}, u32[]{:S(2)}, u32[]{:S(2)}) collective-permute-start(f32[8,128]{1,0:T(8,128)S(1)} %get-tuple-element.52.refs_0_), channel_id=1, source_target_pairs={{0,16},{8,24},{16,0},{24,8},{1,17},{9,25},{17,1},{25,9},{2,18},{10... | collective-permute-start | bytes 12296 | tf_op jit(solution)/shard_map/ppermute | solution.py:391
  14.3 0.3 %collective-permute-start.3 = (f32[8,128]{1,0:T(8,128)S(1)}, f32[8,128]{1,0:T(8,128)S(1)}, u32[]{:S(2)}, u32[]{:S(2)}) collective-permute-start(f32[8,128]{1,0:T(8,128)S(1)} %get-tuple-element.52.refs_0_), channel_id=1, source_target_pairs={{0,8},{8,0},{16,24},{24,16},{1,9},{9,1},{17,25},{25,17},{2,10},{10... | collective-permute-start | bytes 12296 | tf_op jit(solution)/shard_map/ppermute | solution.py:391
  14.6 0.4 %shard_map.49 = (f32[3,16,8,128]{3,2,1,0:T(8,128)S(1)}, f32[3,16,8,128]{3,2,1,0:T(8,128)S(1)}, f32[16,8,128]{2,1,0:T(8,128)S(1)}, f32[16,8,128]{2,1,0:T(8,128)S(...) custom-call(f32[16,8,128]{2,1,0:T(8,128)S(1)} %get-tuple-element.36., ...), custom_call_target="tpu_custom_call" | custom-call | flops 200000 | bytes 200000 | tf_op jit(solution)/shard_map/pallas_call | solution.py:359
  15.0 0.8 %collective-permute-done.5.refs_3_ = f32[8,128]{1,0:T(8,128)S(1)} collective-permute-done((f32[8,128]{1,0:T(8,128)S(1)}, f32[8,128]{1,0:T(8,128)S(1)}, u32[]{:S(2)}, u32[]{:S(2)}) %collective-permute-start.5) | collective-permute-done | bytes 4128 | tf_op jit(solution)/shard_map/ppermute | solution.py:391
  15.8 0.7 %collective-permute-done.4.refs_2_ = f32[8,128]{1,0:T(8,128)S(1)} collective-permute-done((f32[8,128]{1,0:T(8,128)S(1)}, f32[8,128]{1,0:T(8,128)S(1)}, u32[]{:S(2)}, u32[]{:S(2)}) %collective-permute-start.4) | collective-permute-done | bytes 4128 | tf_op jit(solution)/shard_map/ppermute | solution.py:391
  16.4 0.0 collective-permute-done.3.refs_1_
  16.4 0.2 shard_map.50
  16.7 0.6 %collective-permute-start.6 = (f32[2,16,128]{2,1,0:T(8,128)S(1)}, f32[2,16,128]{2,1,0:T(8,128)S(1)}, u32[]{:S(2)}, u32[]{:S(2)}) collective-permute-start(f32[2,16,128]{2,1,0:T(8,128)S(1)} %get-tuple-element.61.refs_0_), channel_id=1, source_target_pairs={{0,4},{4,0},{1,5},{5,1},{2,6},{6,2},{3,7},{7,3},{8,12},{12,8},{9,1... | collective-permute-start | bytes 49160 | tf_op jit(solution)/shard_map/ppermute | solution.py:391
  17.3 3.2 %collective-permute-done.6.refs_1_ = f32[2,16,128]{2,1,0:T(8,128)S(1)} collective-permute-done((f32[2,16,128]{2,1,0:T(8,128)S(1)}, f32[2,16,128]{2,1,0:T(8,128)S(1)}, u32[]{:S(2)}, u32[]{:S(2)}) %collective-permute-start.6) | collective-permute-done | bytes 16416 | tf_op jit(solution)/shard_map/ppermute | solution.py:391
  20.5 0.1 shard_map.51
  20.6 2.5 %collective-permute-start.9 = (f32[5,8,128]{2,1,0:T(8,128)S(1)}, f32[5,8,128]{2,1,0:T(8,128)S(1)}, u32[]{:S(2)}, u32[]{:S(2)}) collective-permute-start(f32[5,8,128]{2,1,0:T(8,128)S(1)} %get-tuple-element.66.refs_0_), channel_id=1, source_target_pairs={{0,3},{1,2},{2,1},{3,0},{4,7},{5,6},{6,5},{7,4},{8,11},{9,10},{10,... | collective-permute-start | bytes 61448 | tf_op jit(solution)/shard_map/ppermute | solution.py:391
  23.2 0.2 collective-permute-start.8
  23.4 1.7 %collective-permute-start.7 = (f32[5,8,128]{2,1,0:T(8,128)S(1)}, f32[5,8,128]{2,1,0:T(8,128)S(1)}, u32[]{:S(2)}, u32[]{:S(2)}) collective-permute-start(f32[5,8,128]{2,1,0:T(8,128)S(1)} %get-tuple-element.66.refs_0_), channel_id=1, source_target_pairs={{0,1},{1,0},{2,3},{3,2},{4,5},{5,4},{6,7},{7,6},{8,9},{9,8},{10,11... | collective-permute-start | bytes 61448 | tf_op jit(solution)/shard_map/ppermute | solution.py:391
  25.1 1.2 %collective-permute-done.9.refs_3_ = f32[5,8,128]{2,1,0:T(8,128)S(1)} collective-permute-done((f32[5,8,128]{2,1,0:T(8,128)S(1)}, f32[5,8,128]{2,1,0:T(8,128)S(1)}, u32[]{:S(2)}, u32[]{:S(2)}) %collective-permute-start.9) | collective-permute-done | bytes 20512 | tf_op jit(solution)/shard_map/ppermute | solution.py:391
  26.3 1.8 %collective-permute-done.8.refs_2_ = f32[5,8,128]{2,1,0:T(8,128)S(1)} collective-permute-done((f32[5,8,128]{2,1,0:T(8,128)S(1)}, f32[5,8,128]{2,1,0:T(8,128)S(1)}, u32[]{:S(2)}, u32[]{:S(2)}) %collective-permute-start.8) | collective-permute-done | bytes 20512 | tf_op jit(solution)/shard_map/ppermute | solution.py:391
  28.1 0.0 collective-permute-done.7.refs_1_
  28.1 0.7 %shard_map.52 = f32[16,8,128]{2,1,0:T(8,128)} custom-call(f32[16,8,128]{2,1,0:T(8,128)S(1)} %copy-done.1, f32[16,8,128]{2,1,0:T(8,128)S(1)} %get-tuple-element.62.zpart_ref, f32[16,8,128]{2,1,0:T(8,128)S(1)} %get-tuple-element.63.zlow_ref, f32[16,8,128]{2,1,0:T(8,128)S(1)} %get-tuple-element.64.zhigh_ref, f32[6,8,128]{2,1,0:T(8,128)S(1)} %get-tuple-element.60.zends_ref, ...), custom_call_target="tpu_custom_call" | custom-call | flops 200000 | bytes 200000 | tf_op jit(solution)/shard_map/pallas_call | solution.py:359
  (5 shorter events, 0.0 us)
Async XLA Ops:
  0.0 0.8 %copy-start = (f32[16,8,128]{2,1,0:T(8,128)S(1)}, f32[16,8,128]{2,1,0:T(8,128)}, u32[]{:S(2)}) copy-start(f32[16,8,128]{2,1,0:T(8,128)} %heat_ref.9) | copy-start | bytes 196612
  0.8 0.8 %copy-start.2 = (s32[16,8,128]{2,1,0:T(8,128)S(1)}, s32[16,8,128]{2,1,0:T(8,128)}, u32[]{:S(2)}) copy-start(s32[16,8,128]{2,1,0:T(8,128)} %label_ref.1) | copy-start | bytes 196612
  1.7 0.7 %copy-start.4 = (f32[13]{0:T(128)S(1)}, f32[13]{0:T(128)}, u32[]{:S(2)}) copy-start(f32[13]{0:T(128)} %table_ref.1) | copy-start | bytes 160
  3.6 8.2 %collective-permute-start.2 = (f32[2,16,128]{2,1,0:T(8,128)S(1)}, f32[2,16,128]{2,1,0:T(8,128)S(1)}, u32[]{:S(2)}, u32[]{:S(2)}) collective-permute-start(f32[2,16,128]{2,1,0:T(8,128)S(1)} %get-tuple-element.44), channel_id=1, source_target_pairs={{0,4},{4,0},{1,5},{5,1},{2,6},{6,2},{3,7},{7,3},{8,12},{12,8},{9,1... | collective-permute-start | bytes 49160 | tf_op jit(solution)/shard_map/ppermute | solution.py:372
  6.5 3.7 %collective-permute-start = (f32[2,8,128]{2,1,0:T(8,128)S(1)}, f32[2,8,128]{2,1,0:T(8,128)S(1)}, u32[]{:S(2)}, u32[]{:S(2)}) collective-permute-start(f32[2,8,128]{2,1,0:T(8,128)S(1)} %get-tuple-element.42), channel_id=1, source_target_pairs={{0,1},{1,0},{2,3},{3,2},{4,5},{5,4},{6,7},{7,6},{8,9},{9,8},{10,11... | collective-permute-start | bytes 24584 | tf_op jit(solution)/shard_map/ppermute | solution.py:372
  8.1 3.7 %collective-permute-start.1 = (f32[2,8,128]{2,1,0:T(8,128)S(1)}, f32[2,8,128]{2,1,0:T(8,128)S(1)}, u32[]{:S(2)}, u32[]{:S(2)}) collective-permute-start(f32[2,8,128]{2,1,0:T(8,128)S(1)} %get-tuple-element.43), channel_id=1, source_target_pairs={{0,4},{1,2},{2,1},{3,7},{4,0},{5,6},{6,5},{7,3},{8,12},{9,10},{10,... | collective-permute-start | bytes 24584 | tf_op jit(solution)/shard_map/ppermute | solution.py:384
  11.8 0.7 %copy-start.3 = (s32[8,128]{1,0:T(8,128)S(1)}, s32[8,128]{1,0:T(8,128)}, u32[]{:S(2)}) copy-start(s32[8,128]{1,0:T(8,128)} %edge_ref.3) | copy-start | bytes 12292
  12.7 3.8 %copy-start.1 = (f32[16,8,128]{2,1,0:T(8,128)S(1)}, f32[16,8,128]{2,1,0:T(8,128)}, u32[]{:S(2)}) copy-start(f32[16,8,128]{2,1,0:T(8,128)} %heat_ref.9) | copy-start | bytes 196612
  12.7 3.1 %collective-permute-start.5 = (f32[8,128]{1,0:T(8,128)S(1)}, f32[8,128]{1,0:T(8,128)S(1)}, u32[]{:S(2)}, u32[]{:S(2)}) collective-permute-start(f32[8,128]{1,0:T(8,128)S(1)} %get-tuple-element.52.refs_0_), channel_id=1, source_target_pairs={{0,24},{8,16},{16,8},{24,0},{1,25},{9,17},{17,9},{25,1},{2,26},{10... | collective-permute-start | bytes 12296 | tf_op jit(solution)/shard_map/ppermute | solution.py:391
  12.8 3.7 %collective-permute-start.4 = (f32[8,128]{1,0:T(8,128)S(1)}, f32[8,128]{1,0:T(8,128)S(1)}, u32[]{:S(2)}, u32[]{:S(2)}) collective-permute-start(f32[8,128]{1,0:T(8,128)S(1)} %get-tuple-element.52.refs_0_), channel_id=1, source_target_pairs={{0,16},{8,24},{16,0},{24,8},{1,17},{9,25},{17,1},{25,9},{2,18},{10... | collective-permute-start | bytes 12296 | tf_op jit(solution)/shard_map/ppermute | solution.py:391
  14.3 2.1 %collective-permute-start.3 = (f32[8,128]{1,0:T(8,128)S(1)}, f32[8,128]{1,0:T(8,128)S(1)}, u32[]{:S(2)}, u32[]{:S(2)}) collective-permute-start(f32[8,128]{1,0:T(8,128)S(1)} %get-tuple-element.52.refs_0_), channel_id=1, source_target_pairs={{0,8},{8,0},{16,24},{24,16},{1,9},{9,1},{17,25},{25,17},{2,10},{10... | collective-permute-start | bytes 12296 | tf_op jit(solution)/shard_map/ppermute | solution.py:391
  16.7 3.8 %collective-permute-start.6 = (f32[2,16,128]{2,1,0:T(8,128)S(1)}, f32[2,16,128]{2,1,0:T(8,128)S(1)}, u32[]{:S(2)}, u32[]{:S(2)}) collective-permute-start(f32[2,16,128]{2,1,0:T(8,128)S(1)} %get-tuple-element.61.refs_0_), channel_id=1, source_target_pairs={{0,4},{4,0},{1,5},{5,1},{2,6},{6,2},{3,7},{7,3},{8,12},{12,8},{9,1... | collective-permute-start | bytes 49160 | tf_op jit(solution)/shard_map/ppermute | solution.py:391
  20.6 5.6 %collective-permute-start.9 = (f32[5,8,128]{2,1,0:T(8,128)S(1)}, f32[5,8,128]{2,1,0:T(8,128)S(1)}, u32[]{:S(2)}, u32[]{:S(2)}) collective-permute-start(f32[5,8,128]{2,1,0:T(8,128)S(1)} %get-tuple-element.66.refs_0_), channel_id=1, source_target_pairs={{0,3},{1,2},{2,1},{3,0},{4,7},{5,6},{6,5},{7,4},{8,11},{9,10},{10,... | collective-permute-start | bytes 61448 | tf_op jit(solution)/shard_map/ppermute | solution.py:391
  23.2 4.9 %collective-permute-start.8 = (f32[5,8,128]{2,1,0:T(8,128)S(1)}, f32[5,8,128]{2,1,0:T(8,128)S(1)}, u32[]{:S(2)}, u32[]{:S(2)}) collective-permute-start(f32[5,8,128]{2,1,0:T(8,128)S(1)} %get-tuple-element.66.refs_0_), channel_id=1, source_target_pairs={{0,2},{1,3},{2,0},{3,1},{4,6},{5,7},{6,4},{7,5},{8,10},{9,11},{10,... | collective-permute-start | bytes 61448 | tf_op jit(solution)/shard_map/ppermute | solution.py:391
  23.4 4.7 %collective-permute-start.7 = (f32[5,8,128]{2,1,0:T(8,128)S(1)}, f32[5,8,128]{2,1,0:T(8,128)S(1)}, u32[]{:S(2)}, u32[]{:S(2)}) collective-permute-start(f32[5,8,128]{2,1,0:T(8,128)S(1)} %get-tuple-element.66.refs_0_), channel_id=1, source_target_pairs={{0,1},{1,0},{2,3},{3,2},{4,5},{5,4},{6,7},{7,6},{8,9},{9,8},{10,11... | collective-permute-start | bytes 61448 | tf_op jit(solution)/shard_map/ppermute | solution.py:391

commit v2 on v1

--- a/solution.py
+++ b/solution.py
@@ -97,12 +97,47 @@
     return jnp.where(index > 0, below, 0.0), jnp.where(index < count - 1, above, 0.0)
 
 
-def start_kernel(heat_ref, label_ref, table_ref, conduct_ref, za_ref, zb_ref, ya_ref, yb_ref):
-    label = label_ref[...]
-    conduct = jnp.full(label.shape, table_ref[0], F32)
+def look_up(label, table_ref):
+    conduct = jnp.broadcast_to(table_ref[0], label.shape)
     for entry in range(1, table_ref.shape[0]):
         conduct = jnp.where(label == entry, table_ref[entry], conduct)
-    conduct_ref[...] = conduct
+    return conduct
+
+
+def stage_kernel(
+    heat_in, label_in, table_in, edge_in, heat_ref, conduct_ref, table_ref, edge_ref, label_ref,
+    entries_ref, sems
+):
+    copies = [
+        pltpu.make_async_copy(source, target, sems.at[i])
+        for i, (source, target) in enumerate(
+            (
+                (table_in, entries_ref), (label_in, label_ref), (heat_in, heat_ref),
+                (edge_in, edge_ref),
+            )
+        )
+    ]
+    for copy in copies:
+        copy.start()
+    copies[0].wait()
+    for entry in range(table_ref.shape[0]):
+        table_ref[entry] = jnp.full(table_ref.shape[1:], entries_ref[entry], F32)
+    copies[1].wait()
+    conduct_ref[...] = look_up(label_ref[...], table_ref)
+    copies[2].wait()
+    copies[3].wait()
+
+
+def start_kernel(
+    heat_a_ref, label_a_ref, edge_a_ref, heat_b_ref, conduct_b_ref, edge_b_ref, table_ref,
+    heat_ref, conduct_ref, edge_ref, za_ref, zb_ref, ya_ref, yb_ref
+):
+    nx = heat_a_ref.shape[-1]
+    heat_ref[:, :, :nx], heat_ref[:, :, nx:] = heat_a_ref[...], heat_b_ref[...]
+    conduct_ref[:, :, :nx] = look_up(label_a_ref[...], table_ref)
+    conduct_ref[:, :, nx:] = conduct_b_ref[...]
+    edge_ref[:, :nx] = edge_a_ref[...].astype(F32)
+    edge_ref[:, nx:] = edge_b_ref[...].astype(F32)
     odd_z = lax.axis_index("gz") % 2 == 1
     odd_y = lax.axis_index("gy") % 2 == 1
     for i, ref in enumerate((heat_ref, conduct_ref)):
@@ -159,7 +194,7 @@
     index_z, index_y = lax.axis_index("gz"), lax.axis_index("gy")
     below, above = pick_halo("gz", z_halo, index_z % 2 == 1)
     source_ref[...] = local_ref[...]
-    ground = UPWARD_SCALE * conduct_ref[0] * edge_ref[...].astype(F32)
+    ground = UPWARD_SCALE * conduct_ref[0] * edge_ref[...]
     ground = jnp.where(index_z == 0, ground, 0.0)
     flow = link_of(UPWARD_SCALE, conduct_ref[0], below[1]) * (below[0] - heat_ref[0])
     source_ref[0] += 2.0 * (flow - ground * heat_ref[0])
@@ -222,7 +257,7 @@
     zlow_ref[...], zhigh_ref[...], zinv_ref[...] = low, high, inverse
     below, above = pick_halo("gz", z_halo, index_z % 2 == 1)
     own_first, own_last, between = end_bands(link, link[1], link[nz - 1], 0, high, own)
-    ground = UPWARD_SCALE * conduct[0] * edge_ref[...].astype(F32)
+    ground = UPWARD_SCALE * conduct[0] * edge_ref[...]
     own_first = own_first + jnp.where(index_z == 0, ground, 0.0)
     outer = link_of(UPWARD_SCALE, conduct[0], below[1])
     for i, value in enumerate((link[1], link[nz - 1], own_first, own_last, between, outer)):
@@ -258,7 +293,7 @@
         refs[:count_x], refs[count_x:]
     )
     nz, ny, nx = heat_ref.shape
-    index = lax.axis_index("gx")
+    index = lax.axis_index("gx") // 2
     for mask, message in enumerate(messages):
         blocks_ref[index ^ mask] = message[...]
     first, last, own_first, own_last, between, c_first, c_last = (
@@ -346,23 +381,25 @@
 def finish_kernel(
     count_z, heat_ref, zpart_ref, zlow_ref, zhigh_ref, zends_ref, zsource_ref, *refs
 ):
-    messages, (out_ref, blocks_ref, state_ref) = refs[:count_z], refs[count_z:]
+    messages, (theirs_ref, mine_ref, blocks_ref, state_ref) = refs[:count_z], refs[count_z:]
     first, last = chain_ends("gz", messages, zends_ref, zsource_ref[...], blocks_ref, state_ref)
-    out_ref[...] = heat_ref[...] + zpart_ref[...] + zlow_ref[...] * first + zhigh_ref[...] * last
+    nx = theirs_ref.shape[-1]
+    heated = heat_ref[...] + zpart_ref[...] + zlow_ref[...] * first + zhigh_ref[...] * last
+    theirs_ref[...], mine_ref[...] = heated[:, :, :nx], heated[:, :, nx:]
 
 
 VMEM = pl.BlockSpec(memory_space=pltpu.VMEM)
-SMEM = pl.BlockSpec(memory_space=pltpu.SMEM)
-
-
-def call(kernel, outs, operands, scratch=(), specs=None, ops=200_000):
+HBM = pl.BlockSpec(memory_space=pltpu.HBM)
+
+
+def call(kernel, outs, operands, scratch=(), specs=None, ops=200_000, vmem=32):
     return pl.pallas_call(
         kernel,
-        out_shape=[jax.ShapeDtypeStruct(shape, F32) for shape in outs],
+        out_shape=[jax.ShapeDtypeStruct(out, F32) if isinstance(out, tuple) else out for out in outs],
         in_specs=specs or [VMEM] * len(operands),
         out_specs=[VMEM] * len(outs),
-        scratch_shapes=[pltpu.VMEM(shape, F32) for shape in scratch],
-        compiler_params=pltpu.CompilerParams(vmem_limit_bytes=32 * 1024 * 1024),
+        scratch_shapes=[pltpu.VMEM(item, F32) if isinstance(item, tuple) else item for item in scratch],
+        compiler_params=pltpu.CompilerParams(vmem_limit_bytes=vmem * 1024 * 1024),
         cost_estimate=pl.CostEstimate(flops=ops, bytes_accessed=ops, transcendentals=0),
     )(*operands)
 
@@ -385,25 +422,31 @@
     return received
 
 
-def swap_all(name, message):
+def swap_all(name, message, stride=1):
     count = lax.axis_size(name)
     return [message] + [
         lax.ppermute(message, name, [(i, i ^ mask) for i in range(count)])
-        for mask in range(1, count)
+        for mask in range(stride, count, stride)
     ]
 
 
-def local(heat, label, table, edge):
-    nz, ny, nx = heat.shape
+def other_core(values):
+    count = lax.axis_size("gx")
+    return lax.ppermute(values, "gx", [(i, i ^ 1) for i in range(count)])
+
+
+def chip_step(heat_a, label_a, edge_a, heat_b, conduct_b, edge_b, table):
+    nz, ny, half = heat_a.shape
+    nx = 2 * half
     block, lines, layer, rows = (nz, ny, nx), (nx, nz * ny), (ny, nx), (nz, nx)
     count_x, count_y, count_z = (lax.axis_size(name) for name in ("gx", "gy", "gz"))
+    count_x = count_x // 2
     x_steps, y_steps, z_steps = (len(steps_of(length)) for length in (nx, ny, nz))
 
-    conduct, za, zb, ya, yb = call(
+    heat, conduct, edge, za, zb, ya, yb = call(
         start_kernel,
-        [block, (2, *layer), (2, *layer), (2, *rows), (2, *rows)],
-        [heat, label, table],
-        specs=[VMEM, VMEM, SMEM],
+        [block, block, layer, (2, *layer), (2, *layer), (2, *rows), (2, *rows)],
+        [heat_a, label_a, edge_a, heat_b, conduct_b, edge_b, table],
     )
     z_halo = neighbour_swaps("gz", "gy", za, zb)
     y_halo = neighbour_swaps("gy", "gz", ya, yb)
@@ -420,7 +463,7 @@
         [heat, conduct, edge, source, x_left, x_right, x_inverse, x_ends, *z_halo, *y_halo],
         [block],
     )
-    x_messages = swap_all("gx", x_message)
+    x_messages = swap_all("gx", x_message, 2)
     (
         y_left, y_right, y_low, y_high, y_inverse, y_ends,
         z_left, z_right, z_low, z_high, z_inverse, z_ends,
@@ -445,13 +488,36 @@
         [(2, *rows), (count_y, y_rows, *rows), (5, count_y, *rows)],
     )
     z_messages = swap_all("gz", z_message)
-    (heated,) = call(
+    return call(
         functools.partial(finish_kernel, count_z),
-        [block],
+        [heat_a.shape] * 2,
         [heat, z_part, z_low, z_high, z_ends, z_source, *z_messages],
         [(count_z, 5, *layer), (5, count_z, *layer)],
     )
-    return heated
+
+
+def local(heat, label, table, edge):
+    others = [other_core(values) for values in (label, heat, edge)]
+    entries = table.shape[0]
+    own_heat, own_conduct, rows, own_edge = call(
+        stage_kernel,
+        [heat.shape, heat.shape, (entries, 8, heat.shape[-1]),
+         jax.ShapeDtypeStruct(edge.shape, edge.dtype)],
+        [heat, label, table, edge],
+        [pltpu.VMEM(label.shape, label.dtype), pltpu.SMEM(table.shape, F32),
+         pltpu.SemaphoreType.DMA((4,))],
+        [HBM] * 4,
+        vmem=60,
+    )
+    label_a, heat_a, edge_a = others
+    second = lax.axis_index("gx") % 2 == 1
+    theirs, mine = lax.cond(
+        second,
+        chip_step,
+        lambda heat_a, label_a, edge_a, heat_b, *rest: (heat_a, heat_b),
+        heat_a, label_a, edge_a, own_heat, own_conduct, own_edge, rows,
+    )
+    return jnp.where(second, mine, other_core(theirs))
 
 
 def solution(mesh):

time: 29 us -> 24.6 us (0.85)
  starting transfers between devices: 12 us -> 21.9 us
  waiting for transfers between devices: 10.4 us -> 0.98 us
  local copies, waits for them, and re-layouts: 3.03 us -> 0 us
  Pallas kernels: 3.25 us -> 0.93 us
  other arithmetic: 0 us -> 0.64 us
    ppermute x10 -> x4, starting transfers between devices: 12 us -> 21.9 us  [other_core(): return lax.ppermute(values, 'gx', [(i, i ^ 1) for i in range(count)])]
    ppermute x10 -> x4, waiting for transfers between devices: 10.4 us -> 0.98 us  [other_core(): return lax.ppermute(values, 'gx', [(i, i ^ 1) for i in range(count)])]
    unnamed x10 -> x0, local copies, waits for them, and re-layouts: 3.03 us -> none
    pallas_call x7 -> x1, Pallas kernels: 3.25 us -> 0.93 us  [call(): pl.pallas_call(kernel, out_shape=[jax.ShapeDtypeStruct(out, F32) if isins...]
    select_n x0 -> x1, other arithmetic: none -> 0.64 us  [local(): return jnp.where(second, mine, other_core(theirs))]
  transfers between devices with their start and end apart: 10 -> 4, of which waited for: 7 -> 2; matrix products, arithmetic and copies ran while one was open for 0% -> 0% of each run, Pallas kernels for 3% -> 4%
where the time goes in v2:
time: 24.6 us; the launch traced here: 24.5 us
  starting transfers between devices  21.9 us (89%)
  waiting for transfers between devices  0.98 us (4%)
  Pallas kernels  0.93 us (4%)
  other arithmetic  0.64 us (3%)
    ppermute x4, starting transfers between devices, other_core(): return lax.ppermute(values, 'gx', [(i, i ^ 1) for i in range(count)])  21.9 us
    ppermute x4, waiting for transfers between devices, other_core(): return lax.ppermute(values, 'gx', [(i, i ^ 1) for i in range(count)])  0.98 us
    pallas_call x1, Pallas kernels, call(): pl.pallas_call(kernel, out_shape=[jax.ShapeDtypeStruct(out, F32) if isins...  0.93 us
    select_n x1, other arithmetic, local(): return jnp.where(second, mine, other_core(theirs))  0.64 us
  transfers between devices with their start and end apart: 4, of which 2 were waited for; matrix products, arithmetic and copies ran while one was open for 0% of the time, Pallas kernels for 4%

profile of v2, /device:TPU:0, one launch (start us, length us, event | category | flops | bytes accessed | tf_op | source)
XLA Modules:
  0.0 24.5 jit_solution(10081960798886363999)
XLA Ops:
  0.0 0.5 %collective-permute-start.8 = (f32[16,8,128]{2,1,0:T(8,128)}, f32[16,8,128]{2,1,0:T(8,128)S(1)}, u32[]{:S(2)}, u32[]{:S(2)}) collective-permute-start(f32[16,8,128]{2,1,0:T(8,128)} %heat_in.1), channel_id=1, source_target_pairs={{0,8},{8,0},{16,24},{24,16},{1,9},{9,1},{17,25},{25,17},{2,10},{10... | collective-permute-start | bytes 196616 | tf_op jit(solution)/shard_map/ppermute | solution.py:435
  0.5 0.1 collective-permute-start.9
  0.5 0.5 %collective-permute-start.10 = (s32[8,128]{1,0:T(8,128)}, s32[8,128]{1,0:T(8,128)S(1)}, u32[]{:S(2)}, u32[]{:S(2)}) collective-permute-start(s32[8,128]{1,0:T(8,128)} %edge_in.1), channel_id=1, source_target_pairs={{0,8},{8,0},{16,24},{24,16},{1,9},{9,1},{17,25},{25,17},{2,10},{10... | collective-permute-start | bytes 12296 | tf_op jit(solution)/shard_map/ppermute | solution.py:435
  1.0 0.9 %shard_map.46 = (f32[16,8,128]{2,1,0:T(8,128)S(1)}, f32[16,8,128]{2,1,0:T(8,128)S(1)}, f32[13,8,128]{2,1,0:T(8,128)S(1)}, s32[8,128]{1,0:T(8,128)S(1)}) custom-call(f32[16,8,128]{2,1,0:T(8,128)} %heat_in.1, s32[16,8,128]{2,1,0:T(8,128)} %label_in.1, f32[13]{0:T(128)} %table_in.1, s32[8,128]{1,0:T(8,128)} %edge_in.1), custom_call_target="tpu_custom_call" | custom-call | flops 200000 | bytes 200000 | tf_op jit(solution)/shard_map/pallas_call | solution.py:396
  1.9 0.0 collective-permute-done.8
  1.9 0.1 collective-permute-done.10
  2.0 0.0 collective-permute-done.9
  2.0 20.9 %collective-permute-start.11 = (f32[16,8,128]{2,1,0:T(8,128)S(1)}, f32[16,8,128]{2,1,0:T(8,128)S(1)}, u32[]{:S(2)}, u32[]{:S(2)}) collective-permute-start(f32[16,8,128]{2,1,0:T(8,128)S(1)} %get-tuple-element.74), channel_id=1, source_target_pairs={{0,8},{8,0},{16,24},{24,16},{1,9},{9,1},{17,25},{25,17},{2,10},{10... | collective-permute-start | bytes 196616 | tf_op jit(solution)/shard_map/ppermute | solution.py:435
  22.9 0.9 %collective-permute-done.11 = f32[16,8,128]{2,1,0:T(8,128)S(1)} collective-permute-done((f32[16,8,128]{2,1,0:T(8,128)S(1)}, f32[16,8,128]{2,1,0:T(8,128)S(1)}, u32[]{:S(2)}, u32[]{:S(2)}) %collective-permute-start.11) | collective-permute-done | bytes 65568 | tf_op jit(solution)/shard_map/ppermute | solution.py:435
  23.8 0.6 %broadcast_select_fusion = f32[16,8,128]{2,1,0:T(8,128)} fusion(f32[16,8,128]{2,1,0:T(8,128)S(1)} %get-tuple-element.73, f32[16,8,128]{2,1,0:T(8,128)S(1)} %collective-permute-done.11, pred[]{:T(512)S(6)} %eq.5), kind=kLoop, calls=%fused_computation | loop fusion | flops 16384 | bytes 196609 | tf_op jit(solution)/shard_map/jit(_where)/select_n | solution.py:520
  (1 shorter events, 0.0 us)
Async XLA Ops:
  0.0 1.9 %collective-permute-start.8 = (f32[16,8,128]{2,1,0:T(8,128)}, f32[16,8,128]{2,1,0:T(8,128)S(1)}, u32[]{:S(2)}, u32[]{:S(2)}) collective-permute-start(f32[16,8,128]{2,1,0:T(8,128)} %heat_in.1), channel_id=1, source_target_pairs={{0,8},{8,0},{16,24},{24,16},{1,9},{9,1},{17,25},{25,17},{2,10},{10... | collective-permute-start | bytes 196616 | tf_op jit(solution)/shard_map/ppermute | solution.py:435
  0.5 1.5 %collective-permute-start.9 = (s32[16,8,128]{2,1,0:T(8,128)}, s32[16,8,128]{2,1,0:T(8,128)S(1)}, u32[]{:S(2)}, u32[]{:S(2)}) collective-permute-start(s32[16,8,128]{2,1,0:T(8,128)} %label_in.1), channel_id=1, source_target_pairs={{0,8},{8,0},{16,24},{24,16},{1,9},{9,1},{17,25},{25,17},{2,10},{10... | collective-permute-start | bytes 196616 | tf_op jit(solution)/shard_map/ppermute | solution.py:435
  0.5 1.5 %collective-permute-start.10 = (s32[8,128]{1,0:T(8,128)}, s32[8,128]{1,0:T(8,128)S(1)}, u32[]{:S(2)}, u32[]{:S(2)}) collective-permute-start(s32[8,128]{1,0:T(8,128)} %edge_in.1), channel_id=1, source_target_pairs={{0,8},{8,0},{16,24},{24,16},{1,9},{9,1},{17,25},{25,17},{2,10},{10... | collective-permute-start | bytes 12296 | tf_op jit(solution)/shard_map/ppermute | solution.py:435
  2.0 21.8 %collective-permute-start.11 = (f32[16,8,128]{2,1,0:T(8,128)S(1)}, f32[16,8,128]{2,1,0:T(8,128)S(1)}, u32[]{:S(2)}, u32[]{:S(2)}) collective-permute-start(f32[16,8,128]{2,1,0:T(8,128)S(1)} %get-tuple-element.74), channel_id=1, source_target_pairs={{0,8},{8,0},{16,24},{24,16},{1,9},{9,1},{17,25},{25,17},{2,10},{10... | collective-permute-start | bytes 196616 | tf_op jit(solution)/shard_map/ppermute | solution.py:435

commit v3 on v2

--- a/solution.py
+++ b/solution.py
@@ -97,6 +97,10 @@
     return jnp.where(index > 0, below, 0.0), jnp.where(index < count - 1, above, 0.0)
 
 
+def swaps_along(name):
+    return min(lax.axis_size(name) - 1, 2)
+
+
 def look_up(label, table_ref):
     conduct = jnp.broadcast_to(table_ref[0], label.shape)
     for entry in range(1, table_ref.shape[0]):
@@ -128,9 +132,18 @@
     copies[3].wait()
 
 
+def join_halos(z_halo, y_halo):
+    return [*z_halo[1:], *y_halo, z_halo[0]]
+
+
+def split_halos(counts, refs):
+    halos = refs[: sum(counts)]
+    return [halos[-1], *halos[: counts[0] - 1]], halos[counts[0] - 1 : -1]
+
+
 def start_kernel(
     heat_a_ref, label_a_ref, edge_a_ref, heat_b_ref, conduct_b_ref, edge_b_ref, table_ref,
-    heat_ref, conduct_ref, edge_ref, za_ref, zb_ref, ya_ref, yb_ref
+    heat_ref, conduct_ref, edge_ref, *faces
 ):
     nx = heat_a_ref.shape[-1]
     heat_ref[:, :, :nx], heat_ref[:, :, nx:] = heat_a_ref[...], heat_b_ref[...]
@@ -138,15 +151,16 @@
     conduct_ref[:, :, nx:] = conduct_b_ref[...]
     edge_ref[:, :nx] = edge_a_ref[...].astype(F32)
     edge_ref[:, nx:] = edge_b_ref[...].astype(F32)
+    z_faces, y_faces = faces[: swaps_along("gz")], faces[swaps_along("gz") :]
     odd_z = lax.axis_index("gz") % 2 == 1
     odd_y = lax.axis_index("gy") % 2 == 1
     for i, ref in enumerate((heat_ref, conduct_ref)):
         low, high = ref[0], ref[ref.shape[0] - 1]
-        za_ref[i] = jnp.where(odd_z, low, high)
-        zb_ref[i] = jnp.where(odd_z, high, low)
+        for face_ref, pick in zip(z_faces, (odd_z, ~odd_z)):
+            face_ref[i] = jnp.where(pick, low, high)
         low, high = ref[:, 0, :], ref[:, ref.shape[1] - 1, :]
-        ya_ref[i] = jnp.where(odd_y, low, high)
-        yb_ref[i] = jnp.where(odd_y, high, low)
+        for face_ref, pick in zip(y_faces, (odd_y, ~odd_y)):
+            face_ref[i] = jnp.where(pick, low, high)
 
 
 def x_bands_kernel(
@@ -188,7 +202,7 @@
     halo_counts, heat_ref, conduct_ref, edge_ref, local_ref, left_ref, right_ref, inverse_ref,
     ends_ref, *refs
 ):
-    z_halo, y_halo = refs[: halo_counts[0]], refs[halo_counts[0] : sum(halo_counts)]
+    z_halo, y_halo = split_halos(halo_counts, refs)
     part_ref, message_ref, source_ref = refs[sum(halo_counts) :]
     nz, ny, nx = conduct_ref.shape
     index_z, index_y = lax.axis_index("gz"), lax.axis_index("gy")
@@ -231,7 +245,7 @@
 def yz_bands_kernel(
     halo_counts, conduct_ref, edge_ref, *refs
 ):
-    z_halo, y_halo = refs[: halo_counts[0]], refs[halo_counts[0] : sum(halo_counts)]
+    z_halo, y_halo = split_halos(halo_counts, refs)
     (
         yl_ref, yr_ref, ylow_ref, yhigh_ref, yinv_ref, yends_ref,
         zl_ref, zr_ref, zlow_ref, zhigh_ref, zinv_ref, zends_ref,
@@ -381,7 +395,8 @@
 def finish_kernel(
     count_z, heat_ref, zpart_ref, zlow_ref, zhigh_ref, zends_ref, zsource_ref, *refs
 ):
-    messages, (theirs_ref, mine_ref, blocks_ref, state_ref) = refs[:count_z], refs[count_z:]
+    messages = refs[:count_z][::-1]
+    theirs_ref, mine_ref, blocks_ref, state_ref = refs[count_z:]
     first, last = chain_ends("gz", messages, zends_ref, zsource_ref[...], blocks_ref, state_ref)
     nx = theirs_ref.shape[-1]
     heated = heat_ref[...] + zpart_ref[...] + zlow_ref[...] * first + zhigh_ref[...] * last
@@ -404,9 +419,9 @@
     )(*operands)
 
 
-def neighbour_swaps(name, other, low_first, second):
+def neighbour_swaps(name, other, faces):
     count, width = lax.axis_size(name), lax.axis_size(other)
-    received = [lax.ppermute(low_first, name, [(i, i ^ 1) for i in range(count)])]
+    received = [lax.ppermute(faces[0], name, [(i, i ^ 1) for i in range(count)])]
     if count > 2:
         pairs = []
         for j in range(width):
@@ -418,7 +433,7 @@
         else:
             axes, place = (name, other), lambda at: at[1] * width + at[0]
         pairs = [(place(source), place(target)) for source, target in pairs]
-        received.append(lax.ppermute(second, axes, pairs))
+        received.append(lax.ppermute(faces[1], axes, pairs))
     return received
 
 
@@ -443,14 +458,14 @@
     count_x = count_x // 2
     x_steps, y_steps, z_steps = (len(steps_of(length)) for length in (nx, ny, nz))
 
-    heat, conduct, edge, za, zb, ya, yb = call(
+    halo_counts = swaps_along("gz"), swaps_along("gy")
+    heat, conduct, edge, *faces = call(
         start_kernel,
-        [block, block, layer, (2, *layer), (2, *layer), (2, *rows), (2, *rows)],
+        [block, block, layer] + [(2, *layer)] * halo_counts[0] + [(2, *rows)] * halo_counts[1],
         [heat_a, label_a, edge_a, heat_b, conduct_b, edge_b, table],
     )
-    z_halo = neighbour_swaps("gz", "gy", za, zb)
-    y_halo = neighbour_swaps("gy", "gz", ya, yb)
-    halo_counts = (len(z_halo), len(y_halo))
+    z_halo = neighbour_swaps("gz", "gy", faces[: halo_counts[0]])
+    y_halo = neighbour_swaps("gy", "gz", faces[halo_counts[0] :])
 
     x_left, x_right, x_low, x_high, x_inverse, x_ends, source = call(
         x_bands_kernel,
@@ -460,7 +475,7 @@
     x_part, x_message = call(
         functools.partial(x_source_kernel, halo_counts),
         [lines, (8, lines[1])],
-        [heat, conduct, edge, source, x_left, x_right, x_inverse, x_ends, *z_halo, *y_halo],
+        [heat, conduct, edge, source, x_left, x_right, x_inverse, x_ends, *join_halos(z_halo, y_halo)],
         [block],
     )
     x_messages = swap_all("gx", x_message, 2)
@@ -471,7 +486,7 @@
         functools.partial(yz_bands_kernel, halo_counts),
         [(y_steps, *block)] * 2 + [block] * 3 + [(7, *rows)]
         + [(z_steps, *block)] * 2 + [block] * 3 + [(6, *layer)],
-        [conduct, edge, *z_halo, *y_halo],
+        [conduct, edge, *join_halos(z_halo, y_halo)],
     )
     y_rows = 5 if count_y > 2 else 2
     y_part, y_source, y_message = call(
@@ -491,7 +506,7 @@
     return call(
         functools.partial(finish_kernel, count_z),
         [heat_a.shape] * 2,
-        [heat, z_part, z_low, z_high, z_ends, z_source, *z_messages],
+        [heat, z_part, z_low, z_high, z_ends, z_source, *z_messages[::-1]],
         [(count_z, 5, *layer), (5, count_z, *layer)],
     )
 

time: 24.6 us -> 22.9 us (0.931)
  starting transfers between devices: 21.9 us -> 20.2 us
    ppermute x4, starting transfers between devices: 21.9 us -> 20.2 us  [other_core(): return lax.ppermute(values, 'gx', [(i, i ^ 1) for i in range(count)])]
where the time goes in v3:
time: 22.9 us; the launch traced here: 22.8 us
  starting transfers between devices  20.2 us (88%)
  waiting for transfers between devices  0.98 us (4%)
  Pallas kernels  0.93 us (4%)
  other arithmetic  0.64 us (3%)
    ppermute x4, starting transfers between devices, other_core(): return lax.ppermute(values, 'gx', [(i, i ^ 1) for i in range(count)])  20.2 us
    ppermute x4, waiting for transfers between devices, other_core(): return lax.ppermute(values, 'gx', [(i, i ^ 1) for i in range(count)])  0.98 us
    pallas_call x1, Pallas kernels, call(): pl.pallas_call(kernel, out_shape=[jax.ShapeDtypeStruct(out, F32) if isins...  0.93 us
    select_n x1, other arithmetic, local(): return jnp.where(second, mine, other_core(theirs))  0.64 us
  transfers between devices with their start and end apart: 4, of which 2 were waited for; matrix products, arithmetic and copies ran while one was open for 0% of the time, Pallas kernels for 4%

profile of v3, /device:TPU:0, one launch (start us, length us, event | category | flops | bytes accessed | tf_op | source)
XLA Modules:
  0.0 22.8 jit_solution(10612187460999675198)
XLA Ops:
  0.0 0.5 %collective-permute-start.8 = (f32[16,8,128]{2,1,0:T(8,128)}, f32[16,8,128]{2,1,0:T(8,128)S(1)}, u32[]{:S(2)}, u32[]{:S(2)}) collective-permute-start(f32[16,8,128]{2,1,0:T(8,128)} %heat_in.1), channel_id=1, source_target_pairs={{0,8},{8,0},{16,24},{24,16},{1,9},{9,1},{17,25},{25,17},{2,10},{10... | collective-permute-start | bytes 196616 | tf_op jit(solution)/shard_map/ppermute | solution.py:450
  0.5 0.1 collective-permute-start.9
  0.5 0.5 %collective-permute-start.10 = (s32[8,128]{1,0:T(8,128)}, s32[8,128]{1,0:T(8,128)S(1)}, u32[]{:S(2)}, u32[]{:S(2)}) collective-permute-start(s32[8,128]{1,0:T(8,128)} %edge_in.1), channel_id=1, source_target_pairs={{0,8},{8,0},{16,24},{24,16},{1,9},{9,1},{17,25},{25,17},{2,10},{10... | collective-permute-start | bytes 12296 | tf_op jit(solution)/shard_map/ppermute | solution.py:450
  1.0 0.9 %shard_map.46 = (f32[16,8,128]{2,1,0:T(8,128)S(1)}, f32[16,8,128]{2,1,0:T(8,128)S(1)}, f32[13,8,128]{2,1,0:T(8,128)S(1)}, s32[8,128]{1,0:T(8,128)S(1)}) custom-call(f32[16,8,128]{2,1,0:T(8,128)} %heat_in.1, s32[16,8,128]{2,1,0:T(8,128)} %label_in.1, f32[13]{0:T(128)} %table_in.1, s32[8,128]{1,0:T(8,128)} %edge_in.1), custom_call_target="tpu_custom_call" | custom-call | flops 200000 | bytes 200000 | tf_op jit(solution)/shard_map/pallas_call | solution.py:411
  1.9 0.0 collective-permute-done.8
  1.9 0.1 collective-permute-done.10
  2.0 0.0 collective-permute-done.9
  2.0 19.2 %collective-permute-start.11 = (f32[16,8,128]{2,1,0:T(8,128)S(1)}, f32[16,8,128]{2,1,0:T(8,128)S(1)}, u32[]{:S(2)}, u32[]{:S(2)}) collective-permute-start(f32[16,8,128]{2,1,0:T(8,128)S(1)} %get-tuple-element.74), channel_id=1, source_target_pairs={{0,8},{8,0},{16,24},{24,16},{1,9},{9,1},{17,25},{25,17},{2,10},{10... | collective-permute-start | bytes 196616 | tf_op jit(solution)/shard_map/ppermute | solution.py:450
  21.2 0.9 %collective-permute-done.11 = f32[16,8,128]{2,1,0:T(8,128)S(1)} collective-permute-done((f32[16,8,128]{2,1,0:T(8,128)S(1)}, f32[16,8,128]{2,1,0:T(8,128)S(1)}, u32[]{:S(2)}, u32[]{:S(2)}) %collective-permute-start.11) | collective-permute-done | bytes 65568 | tf_op jit(solution)/shard_map/ppermute | solution.py:450
  22.2 0.6 %broadcast_select_fusion = f32[16,8,128]{2,1,0:T(8,128)} fusion(f32[16,8,128]{2,1,0:T(8,128)S(1)} %get-tuple-element.73, f32[16,8,128]{2,1,0:T(8,128)S(1)} %collective-permute-done.11, pred[]{:T(512)S(6)} %eq.5), kind=kLoop, calls=%fused_computation | loop fusion | flops 16384 | bytes 196609 | tf_op jit(solution)/shard_map/jit(_where)/select_n | solution.py:535
  (1 shorter events, 0.0 us)
Async XLA Ops:
  0.0 1.9 %collective-permute-start.8 = (f32[16,8,128]{2,1,0:T(8,128)}, f32[16,8,128]{2,1,0:T(8,128)S(1)}, u32[]{:S(2)}, u32[]{:S(2)}) collective-permute-start(f32[16,8,128]{2,1,0:T(8,128)} %heat_in.1), channel_id=1, source_target_pairs={{0,8},{8,0},{16,24},{24,16},{1,9},{9,1},{17,25},{25,17},{2,10},{10... | collective-permute-start | bytes 196616 | tf_op jit(solution)/shard_map/ppermute | solution.py:450
  0.5 1.5 %collective-permute-start.9 = (s32[16,8,128]{2,1,0:T(8,128)}, s32[16,8,128]{2,1,0:T(8,128)S(1)}, u32[]{:S(2)}, u32[]{:S(2)}) collective-permute-start(s32[16,8,128]{2,1,0:T(8,128)} %label_in.1), channel_id=1, source_target_pairs={{0,8},{8,0},{16,24},{24,16},{1,9},{9,1},{17,25},{25,17},{2,10},{10... | collective-permute-start | bytes 196616 | tf_op jit(solution)/shard_map/ppermute | solution.py:450
  0.5 1.5 %collective-permute-start.10 = (s32[8,128]{1,0:T(8,128)}, s32[8,128]{1,0:T(8,128)S(1)}, u32[]{:S(2)}, u32[]{:S(2)}) collective-permute-start(s32[8,128]{1,0:T(8,128)} %edge_in.1), channel_id=1, source_target_pairs={{0,8},{8,0},{16,24},{24,16},{1,9},{9,1},{17,25},{25,17},{2,10},{10... | collective-permute-start | bytes 12296 | tf_op jit(solution)/shard_map/ppermute | solution.py:450
  2.0 20.1 %collective-permute-start.11 = (f32[16,8,128]{2,1,0:T(8,128)S(1)}, f32[16,8,128]{2,1,0:T(8,128)S(1)}, u32[]{:S(2)}, u32[]{:S(2)}) collective-permute-start(f32[16,8,128]{2,1,0:T(8,128)S(1)} %get-tuple-element.74), channel_id=1, source_target_pairs={{0,8},{8,0},{16,24},{24,16},{1,9},{9,1},{17,25},{25,17},{2,10},{10... | collective-permute-start | bytes 196616 | tf_op jit(solution)/shard_map/ppermute | solution.py:450

commit v4 on v3

--- a/solution.py
+++ b/solution.py
@@ -133,12 +133,12 @@
 
 
 def join_halos(z_halo, y_halo):
-    return [*z_halo[1:], *y_halo, z_halo[0]]
+    return [*z_halo[1:], z_halo[0], *y_halo]
 
 
 def split_halos(counts, refs):
     halos = refs[: sum(counts)]
-    return [halos[-1], *halos[: counts[0] - 1]], halos[counts[0] - 1 : -1]
+    return [halos[counts[0] - 1], *halos[: counts[0] - 1]], halos[counts[0] :]
 
 
 def start_kernel(
@@ -164,7 +164,8 @@
 
 
 def x_bands_kernel(
-    heat_ref, conduct_ref, left_ref, right_ref, low_ref, high_ref, inverse_ref, ends_ref, local_ref
+    heat_ref, conduct_ref, left_ref, right_ref, low_ref, high_ref, inverse_ref, ends_ref, local_ref,
+    low_block_ref, high_block_ref
 ):
     nz, ny, nx = conduct_ref.shape
     conduct = conduct_ref[...]
@@ -176,17 +177,21 @@
     row = lax.broadcasted_iota(jnp.int32, conduct.shape, 1)
     across = 2.0 * link_of(FLAT_SCALE, conduct, roll(conduct, 1, 1)) * (heat - roll(heat, 1, 1))
     across = jnp.where(row > 0, across, 0.0)
-    local_ref[...] = local - across + roll(across, -1, 1)
+    local = local - across + roll(across, -1, 1)
+    local_ref[...] = local
     lines = conduct.reshape(nz * ny, nx).T
     row = lax.broadcasted_iota(jnp.int32, lines.shape, 0)
     link = jnp.where(row > 0, link_of(FLAT_SCALE, lines, roll(lines, 1, 0)), 0.0)
     low, high, inverse, own = reduce_interior(link, 0, left_ref, right_ref)
     low_ref[...], high_ref[...], inverse_ref[...] = low, high, inverse
+    low_block_ref[...] = low.T.reshape(nz, ny, nx)
+    high_block_ref[...] = high.T.reshape(nz, ny, nx)
+    local = local.reshape(nz * ny, nx).T
     first, last = link[1:2], link[nx - 1 :]
     ends_ref[...] = jnp.concatenate(
         [
-            first,
-            last,
+            jnp.sum(low * local, 0, keepdims=True),
+            jnp.sum(high * local, 0, keepdims=True),
             1.0 + first * own[1:2],
             1.0 + last * own[nx - 2 : nx - 1],
             first * high[1:2],
@@ -198,38 +203,54 @@
     )
 
 
-def x_source_kernel(
-    halo_counts, heat_ref, conduct_ref, edge_ref, local_ref, left_ref, right_ref, inverse_ref,
-    ends_ref, *refs
+def x_message_kernel(
+    halo_counts, heat_ref, conduct_ref, edge_ref, low_ref, high_ref, ends_ref, *refs
 ):
     z_halo, y_halo = split_halos(halo_counts, refs)
-    part_ref, message_ref, source_ref = refs[sum(halo_counts) :]
+    message_ref, z_flow_ref, y_flow_ref = refs[sum(halo_counts) :]
     nz, ny, nx = conduct_ref.shape
+    lanes = nz * ny
     index_z, index_y = lax.axis_index("gz"), lax.axis_index("gy")
     below, above = pick_halo("gz", z_halo, index_z % 2 == 1)
-    source_ref[...] = local_ref[...]
-    ground = UPWARD_SCALE * conduct_ref[0] * edge_ref[...]
-    ground = jnp.where(index_z == 0, ground, 0.0)
+    ground = jnp.where(index_z == 0, UPWARD_SCALE * conduct_ref[0] * edge_ref[...], 0.0)
     flow = link_of(UPWARD_SCALE, conduct_ref[0], below[1]) * (below[0] - heat_ref[0])
-    source_ref[0] += 2.0 * (flow - ground * heat_ref[0])
+    z_flow_ref[0] = 2.0 * (flow - ground * heat_ref[0])
     flow = link_of(UPWARD_SCALE, conduct_ref[nz - 1], above[1]) * (above[0] - heat_ref[nz - 1])
-    source_ref[nz - 1] += 2.0 * flow
+    z_flow_ref[1] = 2.0 * flow
     below, above = pick_halo("gy", y_halo, index_y % 2 == 1)
     flow = link_of(FLAT_SCALE, conduct_ref[:, 0, :], below[1]) * (below[0] - heat_ref[:, 0, :])
-    source_ref[:, 0, :] += 2.0 * flow
+    y_flow_ref[0] = 2.0 * flow
     flow = link_of(FLAT_SCALE, conduct_ref[:, ny - 1, :], above[1])
-    source_ref[:, ny - 1, :] += 2.0 * flow * (above[0] - heat_ref[:, ny - 1, :])
+    y_flow_ref[1] = 2.0 * flow * (above[0] - heat_ref[:, ny - 1, :])
+
+    def spread(values, first, step):
+        shape = (values.shape[0], lanes)
+        row = lax.broadcasted_iota(jnp.int32, shape, 0)
+        lane = lax.broadcasted_iota(jnp.int32, shape, 1)
+        return jnp.where(lane == first + step * row, jnp.sum(values, 1, keepdims=True), 0.0)
+
+    sums = []
+    for share in (low_ref, high_ref):
+        layers = spread(share[0] * z_flow_ref[0], 0, 1)
+        layers = layers + spread(share[nz - 1] * z_flow_ref[1], lanes - ny, 1)
+        rows = spread(share[:, 0, :] * y_flow_ref[0], 0, ny)
+        rows = rows + spread(share[:, ny - 1, :] * y_flow_ref[1], ny - 1, ny)
+        sums.append(jnp.sum(layers, 0, keepdims=True) + jnp.sum(rows, 0, keepdims=True))
+    ends = ends_ref[...]
+    message_ref[...] = jnp.concatenate([ends[0:1] + sums[0], ends[1:2] + sums[1], ends[2:8]], 0)
+
+
+def x_source_kernel(
+    local_ref, z_flow_ref, y_flow_ref, left_ref, right_ref, inverse_ref, part_ref, source_ref
+):
+    nz, ny, nx = local_ref.shape
+    source_ref[...] = local_ref[...]
+    source_ref[0] += z_flow_ref[0]
+    source_ref[nz - 1] += z_flow_ref[1]
+    source_ref[:, 0, :] += y_flow_ref[0]
+    source_ref[:, ny - 1, :] += y_flow_ref[1]
     source = source_ref[...].reshape(nz * ny, nx).T
-    part = reduce_source(source, 0, left_ref, right_ref, inverse_ref[...])
-    part_ref[...] = part
-    message_ref[...] = jnp.concatenate(
-        [
-            source[:1] + ends_ref[0:1] * part[1:2],
-            source[nx - 1 :] + ends_ref[1:2] * part[nx - 2 : nx - 1],
-            ends_ref[2:8],
-        ],
-        0,
-    )
+    part_ref[...] = reduce_source(source, 0, left_ref, right_ref, inverse_ref[...])
 
 
 def end_bands(link, first, last, axis, high, own):
@@ -247,7 +268,7 @@
 ):
     z_halo, y_halo = split_halos(halo_counts, refs)
     (
-        yl_ref, yr_ref, ylow_ref, yhigh_ref, yinv_ref, yends_ref,
+        yl_ref, yr_ref, ylow_ref, yhigh_ref, yinv_ref, yends_ref, *y_two_refs,
         zl_ref, zr_ref, zlow_ref, zhigh_ref, zinv_ref, zends_ref,
     ) = refs[sum(halo_counts) :]
     nz, ny, nx = conduct_ref.shape
@@ -265,6 +286,16 @@
     outer_high = link_of(FLAT_SCALE, conduct_ref[:, ny - 1, :], above[1])
     for i, value in enumerate((first, last, own_first, own_last, between, outer_low, outer_high)):
         yends_ref[i] = value
+    if y_two_refs:
+        ysum_ref, yshare_ref = y_two_refs
+        odd = index_y % 2 == 1
+        near_own, far_own = jnp.where(odd, own_first, own_last), jnp.where(odd, own_last, own_first)
+        share = between / (far_own + between)
+        ysum_ref[0] = near_own + share * far_own
+        ysum_ref[1] = share
+        for k in range(nz):
+            near, far = jnp.where(odd, low[k], high[k]), jnp.where(odd, high[k], low[k])
+            yshare_ref[k] = near + ysum_ref[1, pl.ds(k, 1), :] * far
     link = link_of(UPWARD_SCALE, conduct[1:], conduct[:-1])
     link = jnp.concatenate([jnp.zeros_like(conduct[:1]), link], 0)
     low, high, inverse, own = reduce_interior(link, 0, zl_ref, zr_ref)
@@ -290,8 +321,8 @@
 
 def chain_ends(name, messages, ends_ref, source_first, blocks_ref, state_ref):
     count, index = lax.axis_size(name), lax.axis_index(name)
-    for mask, message in enumerate(messages):
-        blocks_ref[index ^ mask] = message[...]
+    for shift, message in enumerate(messages):
+        blocks_ref[lax.rem(index - shift + count, count)] = message[...]
     blocks = [tuple(blocks_ref[k, i] for i in range(5)) for k in range(count)]
     below, last = chain(blocks, count, index, state_ref)
     own_first, between, outer = ends_ref[2], ends_ref[4], ends_ref[5]
@@ -299,17 +330,17 @@
     return first, last
 
 
-def y_source_kernel(
-    count_x, count_y, heat_ref, part_ref, low_ref, high_ref, yl_ref, yr_ref, yinv_ref, yends_ref,
-    *refs
-):
-    messages, (ypart_ref, ysource_ref, message_ref, blocks_ref, rows_ref, state_ref, d_ref) = (
-        refs[:count_x], refs[count_x:]
-    )
+def y_message_kernel(
+    count_x, count_y, heat_ref, part_ref, low_ref, high_ref, yends_ref, *refs
+):
+    messages, refs = refs[:count_x], refs[count_x:]
+    shares, refs = (refs[:2], refs[2:]) if count_y > 2 else (refs[:1], refs[1:])
+    sums_ref, refs = (None, refs) if count_y > 2 else (refs[0], refs[1:])
+    source_ref, message_ref, blocks_ref, rows_ref, state_ref = refs
     nz, ny, nx = heat_ref.shape
     index = lax.axis_index("gx") // 2
-    for mask, message in enumerate(messages):
-        blocks_ref[index ^ mask] = message[...]
+    for shift, message in enumerate(messages):
+        blocks_ref[lax.rem(index - shift + count_x, count_x)] = message[...]
     first, last, own_first, own_last, between, c_first, c_last = (
         blocks_ref[:, i, :] for i in range(7)
     )
@@ -334,35 +365,33 @@
     first = whole(5, index) + whole(6, index) * below + whole(7, index) * last
     lines = part_ref[...] + low_ref[...] * first[:1] + high_ref[...] * last[:1]
     source = lines.T.reshape(nz, ny, nx) - 2.0 * heat_ref[...]
-    d_ref[...] = source
-    part = reduce_source(source, 1, yl_ref, yr_ref, yinv_ref[...])
+    source_ref[...] = source
+    sums = [jnp.sum(share[...] * source, 1) for share in shares]
+    if count_y > 2:
+        chain_message(yends_ref, *sums, message_ref)
+    else:
+        message_ref[0], message_ref[1] = sums_ref[0], sums[0]
+
+
+def y_source_kernel(
+    source_ref, yl_ref, yr_ref, yinv_ref, yends_ref, ypart_ref, ysource_ref
+):
+    ny = source_ref.shape[1]
+    part = reduce_source(source_ref[...], 1, yl_ref, yr_ref, yinv_ref[...])
     ypart_ref[...] = part
-    source_first = d_ref[:, 0, :] + yends_ref[0] * ypart_ref[:, 1, :]
-    source_last = d_ref[:, ny - 1, :] + yends_ref[1] * ypart_ref[:, ny - 2, :]
-    ysource_ref[0], ysource_ref[1] = source_first, source_last
-    if count_y > 2:
-        chain_message(yends_ref, source_first, source_last, message_ref)
-        return
-    odd = lax.axis_index("gy") % 2 == 1
-    near_own = jnp.where(odd, yends_ref[2], yends_ref[3])
-    far_own = jnp.where(odd, yends_ref[3], yends_ref[2])
-    share = yends_ref[4] / (far_own + yends_ref[4])
-    message_ref[0] = near_own + share * far_own
-    message_ref[1] = jnp.where(odd, source_first, source_last) + share * jnp.where(
-        odd, source_last, source_first
-    )
-
-
-def z_source_kernel(
-    count_y, ypart_ref, ylow_ref, yhigh_ref, yends_ref, ysource_ref, zl_ref, zr_ref, zinv_ref,
+    ysource_ref[0] = source_ref[:, 0, :] + yends_ref[0] * ypart_ref[:, 1, :]
+    ysource_ref[1] = source_ref[:, ny - 1, :] + yends_ref[1] * ypart_ref[:, ny - 2, :]
+
+
+def z_message_kernel(
+    count_y, ypart_ref, ylow_ref, yhigh_ref, yends_ref, ysource_ref, zlow_ref, zhigh_ref,
     zends_ref, *refs
 ):
-    messages, (zpart_ref, zsource_ref, message_ref, ends_ref, blocks_ref, state_ref) = (
-        refs[:count_y], refs[count_y:]
-    )
+    messages, refs = refs[:count_y], refs[count_y:]
+    source_ref, zsource_ref, message_ref, ends_ref, *state = refs
     nz, ny, nx = ypart_ref.shape
     if count_y > 2:
-        first, last = chain_ends("gy", messages, yends_ref, ysource_ref[0], blocks_ref, state_ref)
+        first, last = chain_ends("gy", messages, yends_ref, ysource_ref[0], *state)
     else:
         odd = lax.axis_index("gy") % 2 == 1
         mine, other = messages
@@ -375,28 +404,28 @@
         far = (far_source + between * near) / (far_own + between)
         first, last = jnp.where(odd, near, far), jnp.where(odd, far, near)
     ends_ref[0], ends_ref[1] = first, last
-    source = jnp.stack(
-        [
+    source_first, source_last = jnp.zeros((ny, nx), F32), jnp.zeros((ny, nx), F32)
+    for k in range(nz):
+        source = (
             ypart_ref[k]
             + ylow_ref[k] * ends_ref[0, pl.ds(k, 1), :]
             + yhigh_ref[k] * ends_ref[1, pl.ds(k, 1), :]
-            for k in range(nz)
-        ],
-        0,
-    )
-    part = reduce_source(source, 0, zl_ref, zr_ref, zinv_ref[...])
-    zpart_ref[...] = part
-    source_first = source[0] + zends_ref[0] * part[1]
-    source_last = source[nz - 1] + zends_ref[1] * part[nz - 2]
+        )
+        source_ref[k] = source
+        source_first = source_first + zlow_ref[k] * source
+        source_last = source_last + zhigh_ref[k] * source
     zsource_ref[...] = source_first
     chain_message(zends_ref, source_first, source_last, message_ref)
 
 
+def z_source_kernel(source_ref, zl_ref, zr_ref, zinv_ref, zpart_ref):
+    zpart_ref[...] = reduce_source(source_ref[...], 0, zl_ref, zr_ref, zinv_ref[...])
+
+
 def finish_kernel(
     count_z, heat_ref, zpart_ref, zlow_ref, zhigh_ref, zends_ref, zsource_ref, *refs
 ):
-    messages = refs[:count_z][::-1]
-    theirs_ref, mine_ref, blocks_ref, state_ref = refs[count_z:]
+    messages, (theirs_ref, mine_ref, blocks_ref, state_ref) = refs[:count_z], refs[count_z:]
     first, last = chain_ends("gz", messages, zends_ref, zsource_ref[...], blocks_ref, state_ref)
     nx = theirs_ref.shape[-1]
     heated = heat_ref[...] + zpart_ref[...] + zlow_ref[...] * first + zhigh_ref[...] * last
@@ -440,8 +469,8 @@
 def swap_all(name, message, stride=1):
     count = lax.axis_size(name)
     return [message] + [
-        lax.ppermute(message, name, [(i, i ^ mask) for i in range(count)])
-        for mask in range(stride, count, stride)
+        lax.ppermute(message, name, [(i, (i + shift) % count) for i in range(count)])
+        for shift in range(stride, count, stride)
     ]
 
 
@@ -467,52 +496,65 @@
     z_halo = neighbour_swaps("gz", "gy", faces[: halo_counts[0]])
     y_halo = neighbour_swaps("gy", "gz", faces[halo_counts[0] :])
 
-    x_left, x_right, x_low, x_high, x_inverse, x_ends, source = call(
+    x_left, x_right, x_low, x_high, x_inverse, x_ends, x_local, x_low_block, x_high_block = call(
         x_bands_kernel,
-        [(x_steps, *lines)] * 2 + [lines] * 3 + [(8, lines[1]), block],
+        [(x_steps, *lines)] * 2 + [lines] * 3 + [(8, lines[1])] + [block] * 3,
         [heat, conduct],
     )
-    x_part, x_message = call(
-        functools.partial(x_source_kernel, halo_counts),
-        [lines, (8, lines[1])],
-        [heat, conduct, edge, source, x_left, x_right, x_inverse, x_ends, *join_halos(z_halo, y_halo)],
-        [block],
+    x_message, z_flow, y_flow = call(
+        functools.partial(x_message_kernel, halo_counts),
+        [(8, lines[1]), (2, *layer), (2, *rows)],
+        [heat, conduct, edge, x_low_block, x_high_block, x_ends, *join_halos(z_halo, y_halo)],
     )
     x_messages = swap_all("gx", x_message, 2)
+    two = count_y == 2
     (
-        y_left, y_right, y_low, y_high, y_inverse, y_ends,
+        y_left, y_right, y_low, y_high, y_inverse, y_ends, *y_two,
         z_left, z_right, z_low, z_high, z_inverse, z_ends,
     ) = call(
         functools.partial(yz_bands_kernel, halo_counts),
-        [(y_steps, *block)] * 2 + [block] * 3 + [(7, *rows)]
+        [(y_steps, *block)] * 2 + [block] * 3 + [(7, *rows)] + [(2, *rows), block] * two
         + [(z_steps, *block)] * 2 + [block] * 3 + [(6, *layer)],
         [conduct, edge, *join_halos(z_halo, y_halo)],
     )
-    y_rows = 5 if count_y > 2 else 2
-    y_part, y_source, y_message = call(
-        functools.partial(y_source_kernel, count_x, count_y),
-        [block, (2, *rows), (y_rows, *rows)],
-        [heat, x_part, x_low, x_high, y_left, y_right, y_inverse, y_ends, *x_messages],
-        [(count_x, 8, lines[1]), (8, count_x, lines[1]), (5, count_x, 8, lines[1]), block],
+    y_sum, y_share = y_two[:1], y_two[1:]
+    (x_part,) = call(
+        x_source_kernel,
+        [lines],
+        [x_local, z_flow, y_flow, x_left, x_right, x_inverse],
+        [block],
+    )
+    y_rows = 2 if two else 5
+    y_source, y_message = call(
+        functools.partial(y_message_kernel, count_x, count_y),
+        [block, (y_rows, *rows)],
+        [heat, x_part, x_low, x_high, y_ends, *x_messages, *(y_share or (y_low, y_high)), *y_sum],
+        [(count_x, 8, lines[1]), (8, count_x, lines[1]), (5, count_x, 8, lines[1])],
     )
     y_messages = swap_all("gy", y_message)
-    z_part, z_source, z_message = call(
-        functools.partial(z_source_kernel, count_y),
+    y_part, y_end_sources = call(
+        y_source_kernel,
+        [block, (2, *rows)],
+        [y_source, y_left, y_right, y_inverse, y_ends],
+    )
+    z_source, z_first, z_message = call(
+        functools.partial(z_message_kernel, count_y),
         [block, layer, (5, *layer)],
-        [y_part, y_low, y_high, y_ends, y_source, z_left, z_right, z_inverse, z_ends, *y_messages],
-        [(2, *rows), (count_y, y_rows, *rows), (5, count_y, *rows)],
+        [y_part, y_low, y_high, y_ends, y_end_sources, z_low, z_high, z_ends, *y_messages],
+        [(2, *rows)] + ([] if two else [(count_y, y_rows, *rows), (5, count_y, *rows)]),
     )
     z_messages = swap_all("gz", z_message)
+    (z_part,) = call(z_source_kernel, [block], [z_source, z_left, z_right, z_inverse])
     return call(
         functools.partial(finish_kernel, count_z),
         [heat_a.shape] * 2,
-        [heat, z_part, z_low, z_high, z_ends, z_source, *z_messages[::-1]],
+        [heat, z_part, z_low, z_high, z_ends, z_first, *z_messages],
         [(count_z, 5, *layer), (5, count_z, *layer)],
     )
 
 
 def local(heat, label, table, edge):
-    others = [other_core(values) for values in (label, heat, edge)]
+    label_a, heat_a, edge_a = (other_core(values) for values in (label, heat, edge))
     entries = table.shape[0]
     own_heat, own_conduct, rows, own_edge = call(
         stage_kernel,
@@ -524,7 +566,6 @@
         [HBM] * 4,
         vmem=60,
     )
-    label_a, heat_a, edge_a = others
     second = lax.axis_index("gx") % 2 == 1
     theirs, mine = lax.cond(
         second,

time: 22.9 us -> 22.4 us (0.978)
  starting transfers between devices: 20.2 us -> 19.7 us
    ppermute x4, starting transfers between devices: 20.2 us -> 19.7 us  [other_core(): return lax.ppermute(values, 'gx', [(i, i ^ 1) for i in range(count)])]
where the time goes in v4:
time: 22.4 us; the launch traced here: 22.3 us
  starting transfers between devices  19.7 us (88%)
  waiting for transfers between devices  0.98 us (4%)
  Pallas kernels  0.93 us (4%)
  other arithmetic  0.64 us (3%)
    ppermute x4, starting transfers between devices, other_core(): return lax.ppermute(values, 'gx', [(i, i ^ 1) for i in range(count)])  19.7 us
    ppermute x4, waiting for transfers between devices, other_core(): return lax.ppermute(values, 'gx', [(i, i ^ 1) for i in range(count)])  0.98 us
    pallas_call x1, Pallas kernels, call(): pl.pallas_call(kernel, out_shape=[jax.ShapeDtypeStruct(out, F32) if isins...  0.93 us
    select_n x1, other arithmetic, local(): return jnp.where(second, mine, other_core(theirs))  0.64 us
  transfers between devices with their start and end apart: 4, of which 2 were waited for; matrix products, arithmetic and copies ran while one was open for 0% of the time, Pallas kernels for 4%

profile of v4, /device:TPU:0, one launch (start us, length us, event | category | flops | bytes accessed | tf_op | source)
XLA Modules:
  0.0 22.3 jit_solution(11096909884942247420)
XLA Ops:
  0.0 0.5 %collective-permute-start.8 = (f32[16,8,128]{2,1,0:T(8,128)}, f32[16,8,128]{2,1,0:T(8,128)S(1)}, u32[]{:S(2)}, u32[]{:S(2)}) collective-permute-start(f32[16,8,128]{2,1,0:T(8,128)} %heat_in.1), channel_id=1, source_target_pairs={{0,8},{8,0},{16,24},{24,16},{1,9},{9,1},{17,25},{25,17},{2,10},{10... | collective-permute-start | bytes 196616 | tf_op jit(solution)/shard_map/ppermute | solution.py:479
  0.5 0.1 collective-permute-start.9
  0.5 0.5 %collective-permute-start.10 = (s32[8,128]{1,0:T(8,128)}, s32[8,128]{1,0:T(8,128)S(1)}, u32[]{:S(2)}, u32[]{:S(2)}) collective-permute-start(s32[8,128]{1,0:T(8,128)} %edge_in.1), channel_id=1, source_target_pairs={{0,8},{8,0},{16,24},{24,16},{1,9},{9,1},{17,25},{25,17},{2,10},{10... | collective-permute-start | bytes 12296 | tf_op jit(solution)/shard_map/ppermute | solution.py:479
  1.0 0.9 %shard_map.46 = (f32[16,8,128]{2,1,0:T(8,128)S(1)}, f32[16,8,128]{2,1,0:T(8,128)S(1)}, f32[13,8,128]{2,1,0:T(8,128)S(1)}, s32[8,128]{1,0:T(8,128)S(1)}) custom-call(f32[16,8,128]{2,1,0:T(8,128)} %heat_in.1, s32[16,8,128]{2,1,0:T(8,128)} %label_in.1, f32[13]{0:T(128)} %table_in.1, s32[8,128]{1,0:T(8,128)} %edge_in.1), custom_call_target="tpu_custom_call" | custom-call | flops 200000 | bytes 200000 | tf_op jit(solution)/shard_map/pallas_call | solution.py:440
  1.9 0.0 collective-permute-done.8
  1.9 0.1 collective-permute-done.10
  2.0 0.0 collective-permute-done.9
  2.0 18.7 %collective-permute-start.11 = (f32[16,8,128]{2,1,0:T(8,128)S(1)}, f32[16,8,128]{2,1,0:T(8,128)S(1)}, u32[]{:S(2)}, u32[]{:S(2)}) collective-permute-start(f32[16,8,128]{2,1,0:T(8,128)S(1)} %get-tuple-element.80), channel_id=1, source_target_pairs={{0,8},{8,0},{16,24},{24,16},{1,9},{9,1},{17,25},{25,17},{2,10},{10... | collective-permute-start | bytes 196616 | tf_op jit(solution)/shard_map/ppermute | solution.py:479
  20.7 0.9 %collective-permute-done.11 = f32[16,8,128]{2,1,0:T(8,128)S(1)} collective-permute-done((f32[16,8,128]{2,1,0:T(8,128)S(1)}, f32[16,8,128]{2,1,0:T(8,128)S(1)}, u32[]{:S(2)}, u32[]{:S(2)}) %collective-permute-start.11) | collective-permute-done | bytes 65568 | tf_op jit(solution)/shard_map/ppermute | solution.py:479
  21.6 0.6 %broadcast_select_fusion = f32[16,8,128]{2,1,0:T(8,128)} fusion(f32[16,8,128]{2,1,0:T(8,128)S(1)} %get-tuple-element.79, f32[16,8,128]{2,1,0:T(8,128)S(1)} %collective-permute-done.11, pred[]{:T(512)S(6)} %eq.5), kind=kLoop, calls=%fused_computation | loop fusion | flops 16384 | bytes 196609 | tf_op jit(solution)/shard_map/jit(_where)/select_n | solution.py:576
  (1 shorter events, 0.0 us)
Async XLA Ops:
  0.0 1.9 %collective-permute-start.8 = (f32[16,8,128]{2,1,0:T(8,128)}, f32[16,8,128]{2,1,0:T(8,128)S(1)}, u32[]{:S(2)}, u32[]{:S(2)}) collective-permute-start(f32[16,8,128]{2,1,0:T(8,128)} %heat_in.1), channel_id=1, source_target_pairs={{0,8},{8,0},{16,24},{24,16},{1,9},{9,1},{17,25},{25,17},{2,10},{10... | collective-permute-start | bytes 196616 | tf_op jit(solution)/shard_map/ppermute | solution.py:479
  0.5 1.5 %collective-permute-start.9 = (s32[16,8,128]{2,1,0:T(8,128)}, s32[16,8,128]{2,1,0:T(8,128)S(1)}, u32[]{:S(2)}, u32[]{:S(2)}) collective-permute-start(s32[16,8,128]{2,1,0:T(8,128)} %label_in.1), channel_id=1, source_target_pairs={{0,8},{8,0},{16,24},{24,16},{1,9},{9,1},{17,25},{25,17},{2,10},{10... | collective-permute-start | bytes 196616 | tf_op jit(solution)/shard_map/ppermute | solution.py:479
  0.5 1.5 %collective-permute-start.10 = (s32[8,128]{1,0:T(8,128)}, s32[8,128]{1,0:T(8,128)S(1)}, u32[]{:S(2)}, u32[]{:S(2)}) collective-permute-start(s32[8,128]{1,0:T(8,128)} %edge_in.1), channel_id=1, source_target_pairs={{0,8},{8,0},{16,24},{24,16},{1,9},{9,1},{17,25},{25,17},{2,10},{10... | collective-permute-start | bytes 12296 | tf_op jit(solution)/shard_map/ppermute | solution.py:479
  2.0 19.6 %collective-permute-start.11 = (f32[16,8,128]{2,1,0:T(8,128)S(1)}, f32[16,8,128]{2,1,0:T(8,128)S(1)}, u32[]{:S(2)}, u32[]{:S(2)}) collective-permute-start(f32[16,8,128]{2,1,0:T(8,128)S(1)} %get-tuple-element.80), channel_id=1, source_target_pairs={{0,8},{8,0},{16,24},{24,16},{1,9},{9,1},{17,25},{25,17},{2,10},{10... | collective-permute-start | bytes 196616 | tf_op jit(solution)/shard_map/ppermute | solution.py:479

commit v5 on v4

--- a/solution.py
+++ b/solution.py
@@ -163,12 +163,28 @@
             face_ref[i] = jnp.where(pick, low, high)
 
 
+def end_bands(link, first, last, axis, high, own):
+    length = high.shape[axis]
+    at = lambda values, i: lax.index_in_dim(values, i, axis, keepdims=False)
+    return (
+        1.0 + first * at(own, 1),
+        1.0 + last * at(own, length - 2),
+        first * at(high, 1),
+    )
+
+
 def x_bands_kernel(
     heat_ref, conduct_ref, left_ref, right_ref, low_ref, high_ref, inverse_ref, ends_ref, local_ref,
-    low_block_ref, high_block_ref
+    low_block_ref, high_block_ref, zl_ref, zr_ref, zlow_ref, zhigh_ref, zinv_ref, zinner_ref
 ):
     nz, ny, nx = conduct_ref.shape
     conduct = conduct_ref[...]
+    link = link_of(UPWARD_SCALE, conduct[1:], conduct[:-1])
+    link = jnp.concatenate([jnp.zeros_like(conduct[:1]), link], 0)
+    low, high, inverse, own = reduce_interior(link, 0, zl_ref, zr_ref)
+    zlow_ref[...], zhigh_ref[...], zinv_ref[...] = low, high, inverse
+    for i, value in enumerate(end_bands(link, link[1], link[nz - 1], 0, high, own)):
+        zinner_ref[i] = value
     heat = heat_ref[...]
     local = 2.0 * heat
     across = 2.0 * link_of(UPWARD_SCALE, conduct[1:], conduct[:-1]) * (heat[1:] - heat[:-1])
@@ -204,17 +220,24 @@
 
 
 def x_message_kernel(
-    halo_counts, heat_ref, conduct_ref, edge_ref, low_ref, high_ref, ends_ref, *refs
+    halo_counts, heat_ref, conduct_ref, edge_ref, low_ref, high_ref, ends_ref, zinner_ref, *refs
 ):
     z_halo, y_halo = split_halos(halo_counts, refs)
-    message_ref, z_flow_ref, y_flow_ref = refs[sum(halo_counts) :]
+    message_ref, z_flow_ref, y_flow_ref, zends_ref = refs[sum(halo_counts) :]
     nz, ny, nx = conduct_ref.shape
     lanes = nz * ny
     index_z, index_y = lax.axis_index("gz"), lax.axis_index("gy")
     below, above = pick_halo("gz", z_halo, index_z % 2 == 1)
     ground = jnp.where(index_z == 0, UPWARD_SCALE * conduct_ref[0] * edge_ref[...], 0.0)
-    flow = link_of(UPWARD_SCALE, conduct_ref[0], below[1]) * (below[0] - heat_ref[0])
-    z_flow_ref[0] = 2.0 * (flow - ground * heat_ref[0])
+    outer = link_of(UPWARD_SCALE, conduct_ref[0], below[1])
+    z_flow_ref[0] = 2.0 * (outer * (below[0] - heat_ref[0]) - ground * heat_ref[0])
+    own_first, own_last, between = zinner_ref[0] + ground, zinner_ref[1], zinner_ref[2]
+    inverse = 1.0 / (own_first + between + outer)
+    for i, value in enumerate((outer, between, inverse)):
+        zends_ref[i] = value
+    zends_ref[3] = outer * between * inverse
+    zends_ref[4] = outer * own_first * inverse
+    zends_ref[5] = own_last + between * own_first * inverse
     flow = link_of(UPWARD_SCALE, conduct_ref[nz - 1], above[1]) * (above[0] - heat_ref[nz - 1])
     z_flow_ref[1] = 2.0 * flow
     below, above = pick_halo("gy", y_halo, index_y % 2 == 1)
@@ -253,26 +276,11 @@
     part_ref[...] = reduce_source(source, 0, left_ref, right_ref, inverse_ref[...])
 
 
-def end_bands(link, first, last, axis, high, own):
-    length = high.shape[axis]
-    at = lambda values, i: lax.index_in_dim(values, i, axis, keepdims=False)
-    return (
-        1.0 + first * at(own, 1),
-        1.0 + last * at(own, length - 2),
-        first * at(high, 1),
-    )
-
-
-def yz_bands_kernel(
-    halo_counts, conduct_ref, edge_ref, *refs
-):
-    z_halo, y_halo = split_halos(halo_counts, refs)
-    (
-        yl_ref, yr_ref, ylow_ref, yhigh_ref, yinv_ref, yends_ref, *y_two_refs,
-        zl_ref, zr_ref, zlow_ref, zhigh_ref, zinv_ref, zends_ref,
-    ) = refs[sum(halo_counts) :]
+def y_bands_kernel(halo_count, conduct_ref, *refs):
+    y_halo = refs[:halo_count]
+    yl_ref, yr_ref, ylow_ref, yhigh_ref, yinv_ref, yends_ref, *y_two_refs = refs[halo_count:]
     nz, ny, nx = conduct_ref.shape
-    index_z, index_y = lax.axis_index("gz"), lax.axis_index("gy")
+    index_y = lax.axis_index("gy")
     conduct = conduct_ref[...]
     row = lax.broadcasted_iota(jnp.int32, conduct.shape, 1)
     link = jnp.where(row > 0, link_of(FLAT_SCALE, conduct, roll(conduct, 1, 1)), 0.0)
@@ -296,17 +304,6 @@
         for k in range(nz):
             near, far = jnp.where(odd, low[k], high[k]), jnp.where(odd, high[k], low[k])
             yshare_ref[k] = near + ysum_ref[1, pl.ds(k, 1), :] * far
-    link = link_of(UPWARD_SCALE, conduct[1:], conduct[:-1])
-    link = jnp.concatenate([jnp.zeros_like(conduct[:1]), link], 0)
-    low, high, inverse, own = reduce_interior(link, 0, zl_ref, zr_ref)
-    zlow_ref[...], zhigh_ref[...], zinv_ref[...] = low, high, inverse
-    below, above = pick_halo("gz", z_halo, index_z % 2 == 1)
-    own_first, own_last, between = end_bands(link, link[1], link[nz - 1], 0, high, own)
-    ground = UPWARD_SCALE * conduct[0] * edge_ref[...]
-    own_first = own_first + jnp.where(index_z == 0, ground, 0.0)
-    outer = link_of(UPWARD_SCALE, conduct[0], below[1])
-    for i, value in enumerate((link[1], link[nz - 1], own_first, own_last, between, outer)):
-        zends_ref[i] = value
 
 
 def chain_message(ends_ref, source_first, source_last, message_ref):
@@ -344,7 +341,9 @@
     first, last, own_first, own_last, between, c_first, c_last = (
         blocks_ref[:, i, :] for i in range(7)
     )
-    before = jnp.concatenate([jnp.zeros_like(c_last[:1]), c_last[:-1]], 0)
+    before = jnp.zeros_like(c_last[:1])
+    if count_x > 1:
+        before = jnp.concatenate([before, c_last[:-1]], 0)
     outer = link_of(FLAT_SCALE, c_first, before)
     inverse = 1.0 / (own_first + between + outer)
     rows = (
@@ -415,7 +414,10 @@
         source_first = source_first + zlow_ref[k] * source
         source_last = source_last + zhigh_ref[k] * source
     zsource_ref[...] = source_first
-    chain_message(zends_ref, source_first, source_last, message_ref)
+    outer, between, inverse = (zends_ref[i] for i in range(3))
+    message_ref[0], message_ref[1], message_ref[3] = (zends_ref[i] for i in range(3, 6))
+    message_ref[2] = outer * inverse * source_first
+    message_ref[4] = source_last + between * inverse * source_first
 
 
 def z_source_kernel(source_ref, zl_ref, zr_ref, zinv_ref, zpart_ref):
@@ -426,7 +428,13 @@
     count_z, heat_ref, zpart_ref, zlow_ref, zhigh_ref, zends_ref, zsource_ref, *refs
 ):
     messages, (theirs_ref, mine_ref, blocks_ref, state_ref) = refs[:count_z], refs[count_z:]
-    first, last = chain_ends("gz", messages, zends_ref, zsource_ref[...], blocks_ref, state_ref)
+    index = lax.axis_index("gz")
+    for shift, message in enumerate(messages):
+        blocks_ref[lax.rem(index - shift + count_z, count_z)] = message[...]
+    blocks = [tuple(blocks_ref[k, i] for i in range(5)) for k in range(count_z)]
+    below, last = chain(blocks, count_z, index, state_ref)
+    outer, between, inverse = (zends_ref[i] for i in range(3))
+    first = (zsource_ref[...] + outer * below + between * last) * inverse
     nx = theirs_ref.shape[-1]
     heated = heat_ref[...] + zpart_ref[...] + zlow_ref[...] * first + zhigh_ref[...] * last
     theirs_ref[...], mine_ref[...] = heated[:, :, :nx], heated[:, :, nx:]
@@ -496,26 +504,27 @@
     z_halo = neighbour_swaps("gz", "gy", faces[: halo_counts[0]])
     y_halo = neighbour_swaps("gy", "gz", faces[halo_counts[0] :])
 
-    x_left, x_right, x_low, x_high, x_inverse, x_ends, x_local, x_low_block, x_high_block = call(
+    (
+        x_left, x_right, x_low, x_high, x_inverse, x_ends, x_local, x_low_block, x_high_block,
+        z_left, z_right, z_low, z_high, z_inverse, z_inner,
+    ) = call(
         x_bands_kernel,
-        [(x_steps, *lines)] * 2 + [lines] * 3 + [(8, lines[1])] + [block] * 3,
+        [(x_steps, *lines)] * 2 + [lines] * 3 + [(8, lines[1])] + [block] * 3
+        + [(z_steps, *block)] * 2 + [block] * 3 + [(3, *layer)],
         [heat, conduct],
     )
-    x_message, z_flow, y_flow = call(
+    x_message, z_flow, y_flow, z_ends = call(
         functools.partial(x_message_kernel, halo_counts),
-        [(8, lines[1]), (2, *layer), (2, *rows)],
-        [heat, conduct, edge, x_low_block, x_high_block, x_ends, *join_halos(z_halo, y_halo)],
+        [(8, lines[1]), (2, *layer), (2, *rows), (6, *layer)],
+        [heat, conduct, edge, x_low_block, x_high_block, x_ends, z_inner,
+         *join_halos(z_halo, y_halo)],
     )
     x_messages = swap_all("gx", x_message, 2)
     two = count_y == 2
-    (
-        y_left, y_right, y_low, y_high, y_inverse, y_ends, *y_two,
-        z_left, z_right, z_low, z_high, z_inverse, z_ends,
-    ) = call(
-        functools.partial(yz_bands_kernel, halo_counts),
-        [(y_steps, *block)] * 2 + [block] * 3 + [(7, *rows)] + [(2, *rows), block] * two
-        + [(z_steps, *block)] * 2 + [block] * 3 + [(6, *layer)],
-        [conduct, edge, *join_halos(z_halo, y_halo)],
+    y_left, y_right, y_low, y_high, y_inverse, y_ends, *y_two = call(
+        functools.partial(y_bands_kernel, len(y_halo)),
+        [(y_steps, *block)] * 2 + [block] * 3 + [(7, *rows)] + [(2, *rows), block] * two,
+        [conduct, *y_halo],
     )
     y_sum, y_share = y_two[:1], y_two[1:]
     (x_part,) = call(

time: 22.4 us -> 22.3 us (level)
  no operation moved by 1% of the time
where the time goes in v5:
time: 22.3 us; the launch traced here: 22.2 us
  starting transfers between devices  19.6 us (88%)
  waiting for transfers between devices  0.98 us (4%)
  Pallas kernels  0.93 us (4%)
  other arithmetic  0.64 us (3%)
    ppermute x4, starting transfers between devices, other_core(): return lax.ppermute(values, 'gx', [(i, i ^ 1) for i in range(count)])  19.6 us
    ppermute x4, waiting for transfers between devices, other_core(): return lax.ppermute(values, 'gx', [(i, i ^ 1) for i in range(count)])  0.98 us
    pallas_call x1, Pallas kernels, call(): pl.pallas_call(kernel, out_shape=[jax.ShapeDtypeStruct(out, F32) if isins...  0.93 us
    select_n x1, other arithmetic, local(): return jnp.where(second, mine, other_core(theirs))  0.64 us
  transfers between devices with their start and end apart: 4, of which 2 were waited for; matrix products, arithmetic and copies ran while one was open for 0% of the time, Pallas kernels for 4%

profile of v5, /device:TPU:0, one launch (start us, length us, event | category | flops | bytes accessed | tf_op | source)
XLA Modules:
  0.0 22.2 jit_solution(7173580959735089901)
XLA Ops:
  0.0 0.5 %collective-permute-start.8 = (f32[16,8,128]{2,1,0:T(8,128)}, f32[16,8,128]{2,1,0:T(8,128)S(1)}, u32[]{:S(2)}, u32[]{:S(2)}) collective-permute-start(f32[16,8,128]{2,1,0:T(8,128)} %heat_in.1), channel_id=1, source_target_pairs={{0,8},{8,0},{16,24},{24,16},{1,9},{9,1},{17,25},{25,17},{2,10},{10... | collective-permute-start | bytes 196616 | tf_op jit(solution)/shard_map/ppermute | solution.py:487
  0.5 0.1 collective-permute-start.9
  0.5 0.5 %collective-permute-start.10 = (s32[8,128]{1,0:T(8,128)}, s32[8,128]{1,0:T(8,128)S(1)}, u32[]{:S(2)}, u32[]{:S(2)}) collective-permute-start(s32[8,128]{1,0:T(8,128)} %edge_in.1), channel_id=1, source_target_pairs={{0,8},{8,0},{16,24},{24,16},{1,9},{9,1},{17,25},{25,17},{2,10},{10... | collective-permute-start | bytes 12296 | tf_op jit(solution)/shard_map/ppermute | solution.py:487
  1.0 0.9 %shard_map.46 = (f32[16,8,128]{2,1,0:T(8,128)S(1)}, f32[16,8,128]{2,1,0:T(8,128)S(1)}, f32[13,8,128]{2,1,0:T(8,128)S(1)}, s32[8,128]{1,0:T(8,128)S(1)}) custom-call(f32[16,8,128]{2,1,0:T(8,128)} %heat_in.1, s32[16,8,128]{2,1,0:T(8,128)} %label_in.1, f32[13]{0:T(128)} %table_in.1, s32[8,128]{1,0:T(8,128)} %edge_in.1), custom_call_target="tpu_custom_call" | custom-call | flops 200000 | bytes 200000 | tf_op jit(solution)/shard_map/pallas_call | solution.py:448
  1.9 0.0 collective-permute-done.8
  1.9 0.1 collective-permute-done.10
  2.0 0.0 collective-permute-done.9
  2.0 18.6 %collective-permute-start.11 = (f32[16,8,128]{2,1,0:T(8,128)S(1)}, f32[16,8,128]{2,1,0:T(8,128)S(1)}, u32[]{:S(2)}, u32[]{:S(2)}) collective-permute-start(f32[16,8,128]{2,1,0:T(8,128)S(1)} %get-tuple-element.81), channel_id=1, source_target_pairs={{0,8},{8,0},{16,24},{24,16},{1,9},{9,1},{17,25},{25,17},{2,10},{10... | collective-permute-start | bytes 196616 | tf_op jit(solution)/shard_map/ppermute | solution.py:487
  20.6 0.9 %collective-permute-done.11 = f32[16,8,128]{2,1,0:T(8,128)S(1)} collective-permute-done((f32[16,8,128]{2,1,0:T(8,128)S(1)}, f32[16,8,128]{2,1,0:T(8,128)S(1)}, u32[]{:S(2)}, u32[]{:S(2)}) %collective-permute-start.11) | collective-permute-done | bytes 65568 | tf_op jit(solution)/shard_map/ppermute | solution.py:487
  21.5 0.6 %broadcast_select_fusion = f32[16,8,128]{2,1,0:T(8,128)} fusion(f32[16,8,128]{2,1,0:T(8,128)S(1)} %get-tuple-element.80, f32[16,8,128]{2,1,0:T(8,128)S(1)} %collective-permute-done.11, pred[]{:T(512)S(6)} %eq.5), kind=kLoop, calls=%fused_computation | loop fusion | flops 16384 | bytes 196609 | tf_op jit(solution)/shard_map/jit(_where)/select_n | solution.py:585
  (1 shorter events, 0.0 us)
Async XLA Ops:
  0.0 1.9 %collective-permute-start.8 = (f32[16,8,128]{2,1,0:T(8,128)}, f32[16,8,128]{2,1,0:T(8,128)S(1)}, u32[]{:S(2)}, u32[]{:S(2)}) collective-permute-start(f32[16,8,128]{2,1,0:T(8,128)} %heat_in.1), channel_id=1, source_target_pairs={{0,8},{8,0},{16,24},{24,16},{1,9},{9,1},{17,25},{25,17},{2,10},{10... | collective-permute-start | bytes 196616 | tf_op jit(solution)/shard_map/ppermute | solution.py:487
  0.5 1.5 %collective-permute-start.9 = (s32[16,8,128]{2,1,0:T(8,128)}, s32[16,8,128]{2,1,0:T(8,128)S(1)}, u32[]{:S(2)}, u32[]{:S(2)}) collective-permute-start(s32[16,8,128]{2,1,0:T(8,128)} %label_in.1), channel_id=1, source_target_pairs={{0,8},{8,0},{16,24},{24,16},{1,9},{9,1},{17,25},{25,17},{2,10},{10... | collective-permute-start | bytes 196616 | tf_op jit(solution)/shard_map/ppermute | solution.py:487
  0.5 1.5 %collective-permute-start.10 = (s32[8,128]{1,0:T(8,128)}, s32[8,128]{1,0:T(8,128)S(1)}, u32[]{:S(2)}, u32[]{:S(2)}) collective-permute-start(s32[8,128]{1,0:T(8,128)} %edge_in.1), channel_id=1, source_target_pairs={{0,8},{8,0},{16,24},{24,16},{1,9},{9,1},{17,25},{25,17},{2,10},{10... | collective-permute-start | bytes 12296 | tf_op jit(solution)/shard_map/ppermute | solution.py:487
  2.0 19.5 %collective-permute-start.11 = (f32[16,8,128]{2,1,0:T(8,128)S(1)}, f32[16,8,128]{2,1,0:T(8,128)S(1)}, u32[]{:S(2)}, u32[]{:S(2)}) collective-permute-start(f32[16,8,128]{2,1,0:T(8,128)S(1)} %get-tuple-element.81), channel_id=1, source_target_pairs={{0,8},{8,0},{16,24},{24,16},{1,9},{9,1},{17,25},{25,17},{2,10},{10... | collective-permute-start | bytes 196616 | tf_op jit(solution)/shard_map/ppermute | solution.py:487

commit v6 on v5

--- a/solution.py
+++ b/solution.py
@@ -175,7 +175,8 @@
 
 def x_bands_kernel(
     heat_ref, conduct_ref, left_ref, right_ref, low_ref, high_ref, inverse_ref, ends_ref, local_ref,
-    low_block_ref, high_block_ref, zl_ref, zr_ref, zlow_ref, zhigh_ref, zinv_ref, zinner_ref
+    low_block_ref, high_block_ref, zl_ref, zr_ref, zlow_ref, zhigh_ref, zinv_ref, zinner_ref,
+    yl_ref, yr_ref, ylow_ref, yhigh_ref, yinv_ref, yends_ref, *y_two_refs
 ):
     nz, ny, nx = conduct_ref.shape
     conduct = conduct_ref[...]
@@ -185,14 +186,32 @@
     zlow_ref[...], zhigh_ref[...], zinv_ref[...] = low, high, inverse
     for i, value in enumerate(end_bands(link, link[1], link[nz - 1], 0, high, own)):
         zinner_ref[i] = value
+    row = lax.broadcasted_iota(jnp.int32, conduct.shape, 1)
+    link = jnp.where(row > 0, link_of(FLAT_SCALE, conduct, roll(conduct, 1, 1)), 0.0)
+    link_y = link
+    low, high, inverse, own = reduce_interior(link, 1, yl_ref, yr_ref)
+    ylow_ref[...], yhigh_ref[...], yinv_ref[...] = low, high, inverse
+    first = link_of(FLAT_SCALE, conduct_ref[:, 0, :], conduct_ref[:, 1, :])
+    last = link_of(FLAT_SCALE, conduct_ref[:, ny - 1, :], conduct_ref[:, ny - 2, :])
+    own_first, own_last, between = end_bands(link, first, last, 1, high, own)
+    for i, value in enumerate((first, last, own_first, own_last, between)):
+        yends_ref[i] = value
+    if y_two_refs:
+        ysum_ref, yshare_ref, factor_ref = y_two_refs
+        odd = lax.axis_index("gy") % 2 == 1
+        near_own, far_own = jnp.where(odd, own_first, own_last), jnp.where(odd, own_last, own_first)
+        share = between / (far_own + between)
+        ysum_ref[...] = near_own + share * far_own
+        factor_ref[...] = share
+        for k in range(nz):
+            near, far = jnp.where(odd, low[k], high[k]), jnp.where(odd, high[k], low[k])
+            yshare_ref[k] = near + factor_ref[pl.ds(k, 1), :] * far
     heat = heat_ref[...]
     local = 2.0 * heat
     across = 2.0 * link_of(UPWARD_SCALE, conduct[1:], conduct[:-1]) * (heat[1:] - heat[:-1])
     nothing = jnp.zeros_like(heat[:1])
     local = local + jnp.concatenate([across, nothing], 0) - jnp.concatenate([nothing, across], 0)
-    row = lax.broadcasted_iota(jnp.int32, conduct.shape, 1)
-    across = 2.0 * link_of(FLAT_SCALE, conduct, roll(conduct, 1, 1)) * (heat - roll(heat, 1, 1))
-    across = jnp.where(row > 0, across, 0.0)
+    across = 2.0 * link_y * (heat - roll(heat, 1, 1))
     local = local - across + roll(across, -1, 1)
     local_ref[...] = local
     lines = conduct.reshape(nz * ny, nx).T
@@ -223,7 +242,7 @@
     halo_counts, heat_ref, conduct_ref, edge_ref, low_ref, high_ref, ends_ref, zinner_ref, *refs
 ):
     z_halo, y_halo = split_halos(halo_counts, refs)
-    message_ref, z_flow_ref, y_flow_ref, zends_ref = refs[sum(halo_counts) :]
+    message_ref, z_flow_ref, y_flow_ref, zends_ref, youter_ref = refs[sum(halo_counts) :]
     nz, ny, nx = conduct_ref.shape
     lanes = nz * ny
     index_z, index_y = lax.axis_index("gz"), lax.axis_index("gy")
@@ -241,10 +260,10 @@
     flow = link_of(UPWARD_SCALE, conduct_ref[nz - 1], above[1]) * (above[0] - heat_ref[nz - 1])
     z_flow_ref[1] = 2.0 * flow
     below, above = pick_halo("gy", y_halo, index_y % 2 == 1)
-    flow = link_of(FLAT_SCALE, conduct_ref[:, 0, :], below[1]) * (below[0] - heat_ref[:, 0, :])
-    y_flow_ref[0] = 2.0 * flow
-    flow = link_of(FLAT_SCALE, conduct_ref[:, ny - 1, :], above[1])
-    y_flow_ref[1] = 2.0 * flow * (above[0] - heat_ref[:, ny - 1, :])
+    youter_ref[0] = link_of(FLAT_SCALE, conduct_ref[:, 0, :], below[1])
+    youter_ref[1] = link_of(FLAT_SCALE, conduct_ref[:, ny - 1, :], above[1])
+    y_flow_ref[0] = 2.0 * youter_ref[0] * (below[0] - heat_ref[:, 0, :])
+    y_flow_ref[1] = 2.0 * youter_ref[1] * (above[0] - heat_ref[:, ny - 1, :])
 
     def spread(values, first, step):
         shape = (values.shape[0], lanes)
@@ -276,38 +295,9 @@
     part_ref[...] = reduce_source(source, 0, left_ref, right_ref, inverse_ref[...])
 
 
-def y_bands_kernel(halo_count, conduct_ref, *refs):
-    y_halo = refs[:halo_count]
-    yl_ref, yr_ref, ylow_ref, yhigh_ref, yinv_ref, yends_ref, *y_two_refs = refs[halo_count:]
-    nz, ny, nx = conduct_ref.shape
-    index_y = lax.axis_index("gy")
-    conduct = conduct_ref[...]
-    row = lax.broadcasted_iota(jnp.int32, conduct.shape, 1)
-    link = jnp.where(row > 0, link_of(FLAT_SCALE, conduct, roll(conduct, 1, 1)), 0.0)
-    low, high, inverse, own = reduce_interior(link, 1, yl_ref, yr_ref)
-    ylow_ref[...], yhigh_ref[...], yinv_ref[...] = low, high, inverse
-    below, above = pick_halo("gy", y_halo, index_y % 2 == 1)
-    first = link_of(FLAT_SCALE, conduct_ref[:, 0, :], conduct_ref[:, 1, :])
-    last = link_of(FLAT_SCALE, conduct_ref[:, ny - 1, :], conduct_ref[:, ny - 2, :])
-    own_first, own_last, between = end_bands(link, first, last, 1, high, own)
-    outer_low = link_of(FLAT_SCALE, conduct_ref[:, 0, :], below[1])
-    outer_high = link_of(FLAT_SCALE, conduct_ref[:, ny - 1, :], above[1])
-    for i, value in enumerate((first, last, own_first, own_last, between, outer_low, outer_high)):
-        yends_ref[i] = value
-    if y_two_refs:
-        ysum_ref, yshare_ref = y_two_refs
-        odd = index_y % 2 == 1
-        near_own, far_own = jnp.where(odd, own_first, own_last), jnp.where(odd, own_last, own_first)
-        share = between / (far_own + between)
-        ysum_ref[0] = near_own + share * far_own
-        ysum_ref[1] = share
-        for k in range(nz):
-            near, far = jnp.where(odd, low[k], high[k]), jnp.where(odd, high[k], low[k])
-            yshare_ref[k] = near + ysum_ref[1, pl.ds(k, 1), :] * far
-
-
-def chain_message(ends_ref, source_first, source_last, message_ref):
-    own_first, own_last, between, outer = (ends_ref[i] for i in range(2, 6))
+def chain_message(ends_ref, outer_ref, source_first, source_last, message_ref):
+    own_first, own_last, between = (ends_ref[i] for i in range(2, 5))
+    outer = outer_ref[0]
     inverse = 1.0 / (own_first + between + outer)
     message_ref[0] = outer * between * inverse
     message_ref[1] = outer * own_first * inverse
@@ -316,23 +306,22 @@
     message_ref[4] = source_last + between * inverse * source_first
 
 
-def chain_ends(name, messages, ends_ref, source_first, blocks_ref, state_ref):
+def chain_ends(name, messages, ends_ref, outer_ref, source_first, blocks_ref, state_ref):
     count, index = lax.axis_size(name), lax.axis_index(name)
     for shift, message in enumerate(messages):
         blocks_ref[lax.rem(index - shift + count, count)] = message[...]
     blocks = [tuple(blocks_ref[k, i] for i in range(5)) for k in range(count)]
     below, last = chain(blocks, count, index, state_ref)
-    own_first, between, outer = ends_ref[2], ends_ref[4], ends_ref[5]
+    own_first, between, outer = ends_ref[2], ends_ref[4], outer_ref[0]
     first = (source_first + outer * below + between * last) / (own_first + between + outer)
     return first, last
 
 
 def y_message_kernel(
-    count_x, count_y, heat_ref, part_ref, low_ref, high_ref, yends_ref, *refs
+    count_x, count_y, heat_ref, part_ref, low_ref, high_ref, yends_ref, youter_ref, *refs
 ):
     messages, refs = refs[:count_x], refs[count_x:]
     shares, refs = (refs[:2], refs[2:]) if count_y > 2 else (refs[:1], refs[1:])
-    sums_ref, refs = (None, refs) if count_y > 2 else (refs[0], refs[1:])
     source_ref, message_ref, blocks_ref, rows_ref, state_ref = refs
     nz, ny, nx = heat_ref.shape
     index = lax.axis_index("gx") // 2
@@ -367,9 +356,9 @@
     source_ref[...] = source
     sums = [jnp.sum(share[...] * source, 1) for share in shares]
     if count_y > 2:
-        chain_message(yends_ref, *sums, message_ref)
+        chain_message(yends_ref, youter_ref, *sums, message_ref)
     else:
-        message_ref[0], message_ref[1] = sums_ref[0], sums[0]
+        message_ref[0] = sums[0]
 
 
 def y_source_kernel(
@@ -383,21 +372,25 @@
 
 
 def z_message_kernel(
-    count_y, ypart_ref, ylow_ref, yhigh_ref, yends_ref, ysource_ref, zlow_ref, zhigh_ref,
-    zends_ref, *refs
+    count_y, ypart_ref, ylow_ref, yhigh_ref, yends_ref, youter_ref, ysource_ref, zlow_ref,
+    zhigh_ref, zends_ref, *refs
 ):
     messages, refs = refs[:count_y], refs[count_y:]
+    owns, refs = ((), refs) if count_y > 2 else (refs[:2], refs[2:])
     source_ref, zsource_ref, message_ref, ends_ref, *state = refs
     nz, ny, nx = ypart_ref.shape
     if count_y > 2:
-        first, last = chain_ends("gy", messages, yends_ref, ysource_ref[0], *state)
+        first, last = chain_ends(
+            "gy", messages, yends_ref, youter_ref, ysource_ref[0], *state
+        )
     else:
         odd = lax.axis_index("gy") % 2 == 1
         mine, other = messages
-        outer = jnp.where(odd, yends_ref[5], yends_ref[6])
+        outer = jnp.where(odd, youter_ref[0], youter_ref[1])
         between = yends_ref[4]
-        factor = outer / (other[0] + outer)
-        near = (mine[1] + factor * other[1]) / (mine[0] + factor * other[0])
+        mine_own, other_own = (own[...] for own in owns)
+        factor = outer / (other_own + outer)
+        near = (mine[0] + factor * other[0]) / (mine_own + factor * other_own)
         far_own = jnp.where(odd, yends_ref[3], yends_ref[2])
         far_source = jnp.where(odd, ysource_ref[1], ysource_ref[0])
         far = (far_source + between * near) / (far_own + between)
@@ -427,7 +420,7 @@
 def finish_kernel(
     count_z, heat_ref, zpart_ref, zlow_ref, zhigh_ref, zends_ref, zsource_ref, *refs
 ):
-    messages, (theirs_ref, mine_ref, blocks_ref, state_ref) = refs[:count_z], refs[count_z:]
+    messages, (theirs_ref, mine_ref, blocks_ref, state_ref) = refs[:count_z][::-1], refs[count_z:]
     index = lax.axis_index("gz")
     for shift, message in enumerate(messages):
         blocks_ref[lax.rem(index - shift + count_z, count_z)] = message[...]
@@ -496,6 +489,7 @@
     x_steps, y_steps, z_steps = (len(steps_of(length)) for length in (nx, ny, nz))
 
     halo_counts = swaps_along("gz"), swaps_along("gy")
+    two = count_y == 2
     heat, conduct, edge, *faces = call(
         start_kernel,
         [block, block, layer] + [(2, *layer)] * halo_counts[0] + [(2, *rows)] * halo_counts[1],
@@ -507,37 +501,35 @@
     (
         x_left, x_right, x_low, x_high, x_inverse, x_ends, x_local, x_low_block, x_high_block,
         z_left, z_right, z_low, z_high, z_inverse, z_inner,
+        y_left, y_right, y_low, y_high, y_inverse, y_ends, *y_two,
     ) = call(
         x_bands_kernel,
         [(x_steps, *lines)] * 2 + [lines] * 3 + [(8, lines[1])] + [block] * 3
-        + [(z_steps, *block)] * 2 + [block] * 3 + [(3, *layer)],
+        + [(z_steps, *block)] * 2 + [block] * 3 + [(3, *layer)]
+        + [(y_steps, *block)] * 2 + [block] * 3 + [(5, *rows)] + [rows, block] * two,
         [heat, conduct],
-    )
-    x_message, z_flow, y_flow, z_ends = call(
+        [rows] * two,
+    )
+    y_sum, y_share = y_two[:1], y_two[1:]
+    y_sums = swap_all("gy", y_sum[0]) if two else []
+    x_message, z_flow, y_flow, z_ends, y_outer = call(
         functools.partial(x_message_kernel, halo_counts),
-        [(8, lines[1]), (2, *layer), (2, *rows), (6, *layer)],
+        [(8, lines[1]), (2, *layer), (2, *rows), (6, *layer), (2, *rows)],
         [heat, conduct, edge, x_low_block, x_high_block, x_ends, z_inner,
          *join_halos(z_halo, y_halo)],
     )
     x_messages = swap_all("gx", x_message, 2)
-    two = count_y == 2
-    y_left, y_right, y_low, y_high, y_inverse, y_ends, *y_two = call(
-        functools.partial(y_bands_kernel, len(y_halo)),
-        [(y_steps, *block)] * 2 + [block] * 3 + [(7, *rows)] + [(2, *rows), block] * two,
-        [conduct, *y_halo],
-    )
-    y_sum, y_share = y_two[:1], y_two[1:]
     (x_part,) = call(
         x_source_kernel,
         [lines],
         [x_local, z_flow, y_flow, x_left, x_right, x_inverse],
         [block],
     )
-    y_rows = 2 if two else 5
+    y_rows = 1 if two else 5
     y_source, y_message = call(
         functools.partial(y_message_kernel, count_x, count_y),
         [block, (y_rows, *rows)],
-        [heat, x_part, x_low, x_high, y_ends, *x_messages, *(y_share or (y_low, y_high)), *y_sum],
+        [heat, x_part, x_low, x_high, y_ends, y_outer, *x_messages, *(y_share or (y_low, y_high))],
         [(count_x, 8, lines[1]), (8, count_x, lines[1]), (5, count_x, 8, lines[1])],
     )
     y_messages = swap_all("gy", y_message)
@@ -549,7 +541,8 @@
     z_source, z_first, z_message = call(
         functools.partial(z_message_kernel, count_y),
         [block, layer, (5, *layer)],
-        [y_part, y_low, y_high, y_ends, y_end_sources, z_low, z_high, z_ends, *y_messages],
+        [y_part, y_low, y_high, y_ends, y_outer, y_end_sources, z_low, z_high, z_ends, *y_messages,
+         *y_sums],
         [(2, *rows)] + ([] if two else [(count_y, y_rows, *rows), (5, count_y, *rows)]),
     )
     z_messages = swap_all("gz", z_message)
@@ -557,7 +550,7 @@
     return call(
         functools.partial(finish_kernel, count_z),
         [heat_a.shape] * 2,
-        [heat, z_part, z_low, z_high, z_ends, z_first, *z_messages],
+        [heat, z_part, z_low, z_high, z_ends, z_first, *z_messages[::-1]],
         [(count_z, 5, *layer), (5, count_z, *layer)],
     )
 

time: 22.3 us -> 22.3 us (level)
  no operation moved by 1% of the time
where the time goes in v6:
time: 22.3 us; the launch traced here: 22.1 us
  starting transfers between devices  19.5 us (87%)
  waiting for transfers between devices  0.98 us (4%)
  Pallas kernels  0.93 us (4%)
  other arithmetic  0.64 us (3%)
    ppermute x4, starting transfers between devices, other_core(): return lax.ppermute(values, 'gx', [(i, i ^ 1) for i in range(count)])  19.5 us
    ppermute x4, waiting for transfers between devices, other_core(): return lax.ppermute(values, 'gx', [(i, i ^ 1) for i in range(count)])  0.98 us
    pallas_call x1, Pallas kernels, call(): pl.pallas_call(kernel, out_shape=[jax.ShapeDtypeStruct(out, F32) if isins...  0.93 us
    select_n x1, other arithmetic, local(): return jnp.where(second, mine, other_core(theirs))  0.64 us
  transfers between devices with their start and end apart: 4, of which 2 were waited for; matrix products, arithmetic and copies ran while one was open for 0% of the time, Pallas kernels for 4%

profile of v6, /device:TPU:0, one launch (start us, length us, event | category | flops | bytes accessed | tf_op | source)
XLA Modules:
  0.0 22.1 jit_solution(8675560675508942768)
XLA Ops:
  0.0 0.5 %collective-permute-start.9 = (f32[16,8,128]{2,1,0:T(8,128)}, f32[16,8,128]{2,1,0:T(8,128)S(1)}, u32[]{:S(2)}, u32[]{:S(2)}) collective-permute-start(f32[16,8,128]{2,1,0:T(8,128)} %heat_in.1), channel_id=1, source_target_pairs={{0,8},{8,0},{16,24},{24,16},{1,9},{9,1},{17,25},{25,17},{2,10},{10... | collective-permute-start | bytes 196616 | tf_op jit(solution)/shard_map/ppermute | solution.py:480
  0.5 0.1 collective-permute-start.10
  0.5 0.5 %collective-permute-start.11 = (s32[8,128]{1,0:T(8,128)}, s32[8,128]{1,0:T(8,128)S(1)}, u32[]{:S(2)}, u32[]{:S(2)}) collective-permute-start(s32[8,128]{1,0:T(8,128)} %edge_in.1), channel_id=1, source_target_pairs={{0,8},{8,0},{16,24},{24,16},{1,9},{9,1},{17,25},{25,17},{2,10},{10... | collective-permute-start | bytes 12296 | tf_op jit(solution)/shard_map/ppermute | solution.py:480
  1.0 0.9 %shard_map.46 = (f32[16,8,128]{2,1,0:T(8,128)S(1)}, f32[16,8,128]{2,1,0:T(8,128)S(1)}, f32[13,8,128]{2,1,0:T(8,128)S(1)}, s32[8,128]{1,0:T(8,128)S(1)}) custom-call(f32[16,8,128]{2,1,0:T(8,128)} %heat_in.1, s32[16,8,128]{2,1,0:T(8,128)} %label_in.1, f32[13]{0:T(128)} %table_in.1, s32[8,128]{1,0:T(8,128)} %edge_in.1), custom_call_target="tpu_custom_call" | custom-call | flops 200000 | bytes 200000 | tf_op jit(solution)/shard_map/pallas_call | solution.py:441
  1.9 0.0 collective-permute-done.9
  1.9 0.1 collective-permute-done.11
  2.0 0.0 collective-permute-done.10
  2.0 18.6 %collective-permute-start.12 = (f32[16,8,128]{2,1,0:T(8,128)S(1)}, f32[16,8,128]{2,1,0:T(8,128)S(1)}, u32[]{:S(2)}, u32[]{:S(2)}) collective-permute-start(f32[16,8,128]{2,1,0:T(8,128)S(1)} %get-tuple-element.82), channel_id=1, source_target_pairs={{0,8},{8,0},{16,24},{24,16},{1,9},{9,1},{17,25},{25,17},{2,10},{10... | collective-permute-start | bytes 196616 | tf_op jit(solution)/shard_map/ppermute | solution.py:480
  20.6 0.9 %collective-permute-done.12 = f32[16,8,128]{2,1,0:T(8,128)S(1)} collective-permute-done((f32[16,8,128]{2,1,0:T(8,128)S(1)}, f32[16,8,128]{2,1,0:T(8,128)S(1)}, u32[]{:S(2)}, u32[]{:S(2)}) %collective-permute-start.12) | collective-permute-done | bytes 65568 | tf_op jit(solution)/shard_map/ppermute | solution.py:480
  21.5 0.6 %broadcast_select_fusion = f32[16,8,128]{2,1,0:T(8,128)} fusion(f32[16,8,128]{2,1,0:T(8,128)S(1)} %get-tuple-element.81, f32[16,8,128]{2,1,0:T(8,128)S(1)} %collective-permute-done.12, pred[]{:T(512)S(6)} %eq.5), kind=kLoop, calls=%fused_computation | loop fusion | flops 16384 | bytes 196609 | tf_op jit(solution)/shard_map/jit(_where)/select_n | solution.py:578
  (1 shorter events, 0.0 us)
Async XLA Ops:
  0.0 1.9 %collective-permute-start.9 = (f32[16,8,128]{2,1,0:T(8,128)}, f32[16,8,128]{2,1,0:T(8,128)S(1)}, u32[]{:S(2)}, u32[]{:S(2)}) collective-permute-start(f32[16,8,128]{2,1,0:T(8,128)} %heat_in.1), channel_id=1, source_target_pairs={{0,8},{8,0},{16,24},{24,16},{1,9},{9,1},{17,25},{25,17},{2,10},{10... | collective-permute-start | bytes 196616 | tf_op jit(solution)/shard_map/ppermute | solution.py:480
  0.5 1.5 %collective-permute-start.10 = (s32[16,8,128]{2,1,0:T(8,128)}, s32[16,8,128]{2,1,0:T(8,128)S(1)}, u32[]{:S(2)}, u32[]{:S(2)}) collective-permute-start(s32[16,8,128]{2,1,0:T(8,128)} %label_in.1), channel_id=1, source_target_pairs={{0,8},{8,0},{16,24},{24,16},{1,9},{9,1},{17,25},{25,17},{2,10},{10... | collective-permute-start | bytes 196616 | tf_op jit(solution)/shard_map/ppermute | solution.py:480
  0.5 1.5 %collective-permute-start.11 = (s32[8,128]{1,0:T(8,128)}, s32[8,128]{1,0:T(8,128)S(1)}, u32[]{:S(2)}, u32[]{:S(2)}) collective-permute-start(s32[8,128]{1,0:T(8,128)} %edge_in.1), channel_id=1, source_target_pairs={{0,8},{8,0},{16,24},{24,16},{1,9},{9,1},{17,25},{25,17},{2,10},{10... | collective-permute-start | bytes 12296 | tf_op jit(solution)/shard_map/ppermute | solution.py:480
  2.0 19.5 %collective-permute-start.12 = (f32[16,8,128]{2,1,0:T(8,128)S(1)}, f32[16,8,128]{2,1,0:T(8,128)S(1)}, u32[]{:S(2)}, u32[]{:S(2)}) collective-permute-start(f32[16,8,128]{2,1,0:T(8,128)S(1)} %get-tuple-element.82), channel_id=1, source_target_pairs={{0,8},{8,0},{16,24},{24,16},{1,9},{9,1},{17,25},{25,17},{2,10},{10... | collective-permute-start | bytes 196616 | tf_op jit(solution)/shard_map/ppermute | solution.py:480

commit v7 on v5

--- a/solution.py
+++ b/solution.py
@@ -61,6 +61,110 @@
             + right_ref[step] * roll(source, -distance, axis)
         )
     return source * inverse
+
+
+def halvings(count):
+    rows, stages = list(range(count)), []
+    while len(rows) > 1:
+        near = [
+            (row, rows[i - 1] if i else None, rows[i + 1] if i + 1 < len(rows) else None)
+            for i, row in enumerate(rows)
+        ]
+        stages.append((near[0::2], near[1::2]))
+        rows = rows[0::2]
+    return stages
+
+
+def reduce_lines(link, left_ref, right_ref, kept_ref, gone_ref):
+    length = link.shape[0]
+    count = length // 8
+    row = lax.broadcasted_iota(jnp.int32, link.shape, 0)
+    low, high, own = link, roll(link, -1, 0), jnp.ones_like(link)
+    for step, distance in enumerate((1, 2, 4)):
+        inverse = 1.0 / (own + low + high)
+        open_low, open_high = row > distance, row < length - 1 - distance
+        left = jnp.where(open_low, low * roll(inverse, distance, 0), 0.0)
+        right = jnp.where(open_high, high * roll(inverse, -distance, 0), 0.0)
+        left_ref[step], right_ref[step] = left, right
+        own = own + left * roll(own, distance, 0) + right * roll(own, -distance, 0)
+        low = jnp.where(open_low, left * roll(low, distance, 0), low)
+        high = jnp.where(open_high, right * roll(high, -distance, 0), high)
+    first, last = row == 0, row == length - 1
+    own = jnp.where(first | last, 0.0, own)
+    low = jnp.where(first, 1.0, jnp.where(last, 0.0, low))
+    high = jnp.where(last, 1.0, jnp.where(first, 0.0, high))
+    tiles = lambda values: [values[8 * k : 8 * k + 8] for k in range(count)]
+    own, low, high = tiles(own), tiles(low), tiles(high)
+    inverse, share_low, share_high, share_own = {}, {}, {}, {}
+
+    def finish(k):
+        inverse[k] = 1.0 / (own[k] + low[k] + high[k])
+        gone_ref[0, k], gone_ref[1, k] = low[k] * inverse[k], high[k] * inverse[k]
+        gone_ref[2, k] = inverse[k]
+
+    slot = 0
+    for kept, gone in halvings(count):
+        for k, _, _ in gone:
+            finish(k)
+        for k, below, above in kept:
+            new_low, new_high = low[k], high[k]
+            if below is not None:
+                factor = low[k] * inverse[below]
+                kept_ref[0, slot] = factor
+                own[k] = own[k] + factor * own[below]
+                new_low = factor * low[below]
+            if above is not None:
+                factor = high[k] * inverse[above]
+                kept_ref[1, slot] = factor
+                own[k] = own[k] + factor * own[above]
+                new_high = factor * high[above]
+            low[k], high[k] = new_low, new_high
+            slot += 1
+    finish(0)
+    share_low[0], share_high[0] = low[0] * inverse[0], high[0] * inverse[0]
+    share_own[0] = own[0] * inverse[0]
+    for _, gone in halvings(count)[::-1]:
+        for k, below, above in gone:
+            to_low, to_high = low[k] * inverse[k], high[k] * inverse[k]
+            share_low[k] = to_low * share_low[below]
+            share_high[k] = to_low * share_high[below]
+            if above is None:
+                share_high[k] = share_high[k] + to_high
+                share_own[k] = own[k] * inverse[k] + to_low * share_own[below]
+            else:
+                share_low[k] = share_low[k] + to_high * share_low[above]
+                share_high[k] = share_high[k] + to_high * share_high[above]
+    whole = lambda shares: jnp.concatenate([shares[k] for k in range(count)], 0)
+    return whole(share_low), whole(share_high), share_own[0][1:2], share_own[count - 1][6:7]
+
+
+def solve_lines(source, left_ref, right_ref, kept_ref, gone_ref):
+    length = source.shape[0]
+    count = length // 8
+    for step, distance in enumerate((1, 2, 4)):
+        source = (
+            source
+            + left_ref[step] * roll(source, distance, 0)
+            + right_ref[step] * roll(source, -distance, 0)
+        )
+    row = lax.broadcasted_iota(jnp.int32, source.shape, 0)
+    source = jnp.where((row == 0) | (row == length - 1), 0.0, source)
+    source = [source[8 * k : 8 * k + 8] for k in range(count)]
+    slot, stages = 0, halvings(count)
+    for kept, _ in stages:
+        for k, below, above in kept:
+            if below is not None:
+                source[k] = source[k] + kept_ref[0, slot] * source[below]
+            if above is not None:
+                source[k] = source[k] + kept_ref[1, slot] * source[above]
+            slot += 1
+    solved = {0: source[0] * gone_ref[2, 0]}
+    for _, gone in stages[::-1]:
+        for k, below, above in gone:
+            solved[k] = source[k] * gone_ref[2, k] + gone_ref[0, k] * solved[below]
+            if above is not None:
+                solved[k] = solved[k] + gone_ref[1, k] * solved[above]
+    return jnp.concatenate([solved[k] for k in range(count)], 0)
 
 
 def chain(blocks, count, index, state):
@@ -174,8 +278,8 @@
 
 
 def x_bands_kernel(
-    heat_ref, conduct_ref, left_ref, right_ref, low_ref, high_ref, inverse_ref, ends_ref, local_ref,
-    low_block_ref, high_block_ref, zl_ref, zr_ref, zlow_ref, zhigh_ref, zinv_ref, zinner_ref
+    heat_ref, conduct_ref, left_ref, right_ref, low_ref, high_ref, kept_ref, gone_ref, ends_ref,
+    local_ref, low_block_ref, high_block_ref, zl_ref, zr_ref, zlow_ref, zhigh_ref, zinv_ref, zinner_ref
 ):
     nz, ny, nx = conduct_ref.shape
     conduct = conduct_ref[...]
@@ -198,8 +302,8 @@
     lines = conduct.reshape(nz * ny, nx).T
     row = lax.broadcasted_iota(jnp.int32, lines.shape, 0)
     link = jnp.where(row > 0, link_of(FLAT_SCALE, lines, roll(lines, 1, 0)), 0.0)
-    low, high, inverse, own = reduce_interior(link, 0, left_ref, right_ref)
-    low_ref[...], high_ref[...], inverse_ref[...] = low, high, inverse
+    low, high, own_low, own_high = reduce_lines(link, left_ref, right_ref, kept_ref, gone_ref)
+    low_ref[...], high_ref[...] = low, high
     low_block_ref[...] = low.T.reshape(nz, ny, nx)
     high_block_ref[...] = high.T.reshape(nz, ny, nx)
     local = local.reshape(nz * ny, nx).T
@@ -208,8 +312,8 @@
         [
             jnp.sum(low * local, 0, keepdims=True),
             jnp.sum(high * local, 0, keepdims=True),
-            1.0 + first * own[1:2],
-            1.0 + last * own[nx - 2 : nx - 1],
+            1.0 + first * own_low,
+            1.0 + last * own_high,
             first * high[1:2],
             lines[:1],
             lines[nx - 1 :],
@@ -264,7 +368,7 @@
 
 
 def x_source_kernel(
-    local_ref, z_flow_ref, y_flow_ref, left_ref, right_ref, inverse_ref, part_ref, source_ref
+    local_ref, z_flow_ref, y_flow_ref, left_ref, right_ref, kept_ref, gone_ref, part_ref, source_ref
 ):
     nz, ny, nx = local_ref.shape
     source_ref[...] = local_ref[...]
@@ -273,7 +377,7 @@
     source_ref[:, 0, :] += y_flow_ref[0]
     source_ref[:, ny - 1, :] += y_flow_ref[1]
     source = source_ref[...].reshape(nz * ny, nx).T
-    part_ref[...] = reduce_source(source, 0, left_ref, right_ref, inverse_ref[...])
+    part_ref[...] = solve_lines(source, left_ref, right_ref, kept_ref, gone_ref)
 
 
 def y_bands_kernel(halo_count, conduct_ref, *refs):
@@ -493,7 +597,8 @@
     block, lines, layer, rows = (nz, ny, nx), (nx, nz * ny), (ny, nx), (nz, nx)
     count_x, count_y, count_z = (lax.axis_size(name) for name in ("gx", "gy", "gz"))
     count_x = count_x // 2
-    x_steps, y_steps, z_steps = (len(steps_of(length)) for length in (nx, ny, nz))
+    tiles = (nx // 8, 8, lines[1])
+    y_steps, z_steps = (len(steps_of(length)) for length in (ny, nz))
 
     halo_counts = swaps_along("gz"), swaps_along("gy")
     heat, conduct, edge, *faces = call(
@@ -505,11 +610,11 @@
     y_halo = neighbour_swaps("gy", "gz", faces[halo_counts[0] :])
 
     (
-        x_left, x_right, x_low, x_high, x_inverse, x_ends, x_local, x_low_block, x_high_block,
+        x_left, x_right, x_low, x_high, x_kept, x_gone, x_ends, x_local, x_low_block, x_high_block,
         z_left, z_right, z_low, z_high, z_inverse, z_inner,
     ) = call(
         x_bands_kernel,
-        [(x_steps, *lines)] * 2 + [lines] * 3 + [(8, lines[1])] + [block] * 3
+        [(3, *lines)] * 2 + [lines] * 2 + [(2, *tiles), (3, *tiles), (8, lines[1])] + [block] * 3
         + [(z_steps, *block)] * 2 + [block] * 3 + [(3, *layer)],
         [heat, conduct],
     )
@@ -530,7 +635,7 @@
     (x_part,) = call(
         x_source_kernel,
         [lines],
-        [x_local, z_flow, y_flow, x_left, x_right, x_inverse],
+        [x_local, z_flow, y_flow, x_left, x_right, x_kept, x_gone],
         [block],
     )
     y_rows = 2 if two else 5

time: 22.3 us -> 22.3 us (level)
  no operation moved by 1% of the time
where the time goes in v7:
time: 22.3 us; the launch traced here: 22.2 us
  starting transfers between devices  19.6 us (88%)
  waiting for transfers between devices  0.98 us (4%)
  Pallas kernels  0.93 us (4%)
  other arithmetic  0.64 us (3%)
    ppermute x4, starting transfers between devices, other_core(): return lax.ppermute(values, 'gx', [(i, i ^ 1) for i in range(count)])  19.6 us
    ppermute x4, waiting for transfers between devices, other_core(): return lax.ppermute(values, 'gx', [(i, i ^ 1) for i in range(count)])  0.98 us
    pallas_call x1, Pallas kernels, call(): pl.pallas_call(kernel, out_shape=[jax.ShapeDtypeStruct(out, F32) if isins...  0.93 us
    select_n x1, other arithmetic, local(): return jnp.where(second, mine, other_core(theirs))  0.64 us
  transfers between devices with their start and end apart: 4, of which 2 were waited for; matrix products, arithmetic and copies ran while one was open for 0% of the time, Pallas kernels for 4%

profile of v7, /device:TPU:0, one launch (start us, length us, event | category | flops | bytes accessed | tf_op | source)
XLA Modules:
  0.0 22.2 jit_solution(14879280995943355583)
XLA Ops:
  0.0 0.5 %collective-permute-start.8 = (f32[16,8,128]{2,1,0:T(8,128)}, f32[16,8,128]{2,1,0:T(8,128)S(1)}, u32[]{:S(2)}, u32[]{:S(2)}) collective-permute-start(f32[16,8,128]{2,1,0:T(8,128)} %heat_in.1), channel_id=1, source_target_pairs={{0,8},{8,0},{16,24},{24,16},{1,9},{9,1},{17,25},{25,17},{2,10},{10... | collective-permute-start | bytes 196616 | tf_op jit(solution)/shard_map/ppermute | solution.py:591
  0.5 0.1 collective-permute-start.9
  0.5 0.5 %collective-permute-start.10 = (s32[8,128]{1,0:T(8,128)}, s32[8,128]{1,0:T(8,128)S(1)}, u32[]{:S(2)}, u32[]{:S(2)}) collective-permute-start(s32[8,128]{1,0:T(8,128)} %edge_in.1), channel_id=1, source_target_pairs={{0,8},{8,0},{16,24},{24,16},{1,9},{9,1},{17,25},{25,17},{2,10},{10... | collective-permute-start | bytes 12296 | tf_op jit(solution)/shard_map/ppermute | solution.py:591
  1.0 0.9 %shard_map.46 = (f32[16,8,128]{2,1,0:T(8,128)S(1)}, f32[16,8,128]{2,1,0:T(8,128)S(1)}, f32[13,8,128]{2,1,0:T(8,128)S(1)}, s32[8,128]{1,0:T(8,128)S(1)}) custom-call(f32[16,8,128]{2,1,0:T(8,128)} %heat_in.1, s32[16,8,128]{2,1,0:T(8,128)} %label_in.1, f32[13]{0:T(128)} %table_in.1, s32[8,128]{1,0:T(8,128)} %edge_in.1), custom_call_target="tpu_custom_call" | custom-call | flops 200000 | bytes 200000 | tf_op jit(solution)/shard_map/pallas_call | solution.py:552
  1.9 0.0 collective-permute-done.8
  1.9 0.1 collective-permute-done.10
  2.0 0.0 collective-permute-done.9
  2.0 18.6 %collective-permute-start.11 = (f32[16,8,128]{2,1,0:T(8,128)S(1)}, f32[16,8,128]{2,1,0:T(8,128)S(1)}, u32[]{:S(2)}, u32[]{:S(2)}) collective-permute-start(f32[16,8,128]{2,1,0:T(8,128)S(1)} %get-tuple-element.82), channel_id=1, source_target_pairs={{0,8},{8,0},{16,24},{24,16},{1,9},{9,1},{17,25},{25,17},{2,10},{10... | collective-permute-start | bytes 196616 | tf_op jit(solution)/shard_map/ppermute | solution.py:591
  20.6 0.9 %collective-permute-done.11 = f32[16,8,128]{2,1,0:T(8,128)S(1)} collective-permute-done((f32[16,8,128]{2,1,0:T(8,128)S(1)}, f32[16,8,128]{2,1,0:T(8,128)S(1)}, u32[]{:S(2)}, u32[]{:S(2)}) %collective-permute-start.11) | collective-permute-done | bytes 65568 | tf_op jit(solution)/shard_map/ppermute | solution.py:591
  21.5 0.6 %broadcast_select_fusion = f32[16,8,128]{2,1,0:T(8,128)} fusion(f32[16,8,128]{2,1,0:T(8,128)S(1)} %get-tuple-element.81, f32[16,8,128]{2,1,0:T(8,128)S(1)} %collective-permute-done.11, pred[]{:T(512)S(6)} %eq.5), kind=kLoop, calls=%fused_computation | loop fusion | flops 16384 | bytes 196609 | tf_op jit(solution)/shard_map/jit(_where)/select_n | solution.py:690
  (1 shorter events, 0.0 us)
Async XLA Ops:
  0.0 1.9 %collective-permute-start.8 = (f32[16,8,128]{2,1,0:T(8,128)}, f32[16,8,128]{2,1,0:T(8,128)S(1)}, u32[]{:S(2)}, u32[]{:S(2)}) collective-permute-start(f32[16,8,128]{2,1,0:T(8,128)} %heat_in.1), channel_id=1, source_target_pairs={{0,8},{8,0},{16,24},{24,16},{1,9},{9,1},{17,25},{25,17},{2,10},{10... | collective-permute-start | bytes 196616 | tf_op jit(solution)/shard_map/ppermute | solution.py:591
  0.5 1.5 %collective-permute-start.9 = (s32[16,8,128]{2,1,0:T(8,128)}, s32[16,8,128]{2,1,0:T(8,128)S(1)}, u32[]{:S(2)}, u32[]{:S(2)}) collective-permute-start(s32[16,8,128]{2,1,0:T(8,128)} %label_in.1), channel_id=1, source_target_pairs={{0,8},{8,0},{16,24},{24,16},{1,9},{9,1},{17,25},{25,17},{2,10},{10... | collective-permute-start | bytes 196616 | tf_op jit(solution)/shard_map/ppermute | solution.py:591
  0.5 1.5 %collective-permute-start.10 = (s32[8,128]{1,0:T(8,128)}, s32[8,128]{1,0:T(8,128)S(1)}, u32[]{:S(2)}, u32[]{:S(2)}) collective-permute-start(s32[8,128]{1,0:T(8,128)} %edge_in.1), channel_id=1, source_target_pairs={{0,8},{8,0},{16,24},{24,16},{1,9},{9,1},{17,25},{25,17},{2,10},{10... | collective-permute-start | bytes 12296 | tf_op jit(solution)/shard_map/ppermute | solution.py:591
  2.0 19.5 %collective-permute-start.11 = (f32[16,8,128]{2,1,0:T(8,128)S(1)}, f32[16,8,128]{2,1,0:T(8,128)S(1)}, u32[]{:S(2)}, u32[]{:S(2)}) collective-permute-start(f32[16,8,128]{2,1,0:T(8,128)S(1)} %get-tuple-element.82), channel_id=1, source_target_pairs={{0,8},{8,0},{16,24},{24,16},{1,9},{9,1},{17,25},{25,17},{2,10},{10... | collective-permute-start | bytes 196616 | tf_op jit(solution)/shard_map/ppermute | solution.py:591

commit v8 on v7

--- a/solution.py
+++ b/solution.py
@@ -287,7 +287,8 @@
     link = jnp.concatenate([jnp.zeros_like(conduct[:1]), link], 0)
     low, high, inverse, own = reduce_interior(link, 0, zl_ref, zr_ref)
     zlow_ref[...], zhigh_ref[...], zinv_ref[...] = low, high, inverse
-    for i, value in enumerate(end_bands(link, link[1], link[nz - 1], 0, high, own)):
+    inner = end_bands(link, link[1], link[nz - 1], 0, high, own)
+    for i, value in enumerate((*inner, link[1], link[nz - 1])):
         zinner_ref[i] = value
     heat = heat_ref[...]
     local = 2.0 * heat
@@ -337,11 +338,8 @@
     z_flow_ref[0] = 2.0 * (outer * (below[0] - heat_ref[0]) - ground * heat_ref[0])
     own_first, own_last, between = zinner_ref[0] + ground, zinner_ref[1], zinner_ref[2]
     inverse = 1.0 / (own_first + between + outer)
-    for i, value in enumerate((outer, between, inverse)):
+    for i, value in enumerate((outer, between, inverse, zinner_ref[3], zinner_ref[4])):
         zends_ref[i] = value
-    zends_ref[3] = outer * between * inverse
-    zends_ref[4] = outer * own_first * inverse
-    zends_ref[5] = own_last + between * own_first * inverse
     flow = link_of(UPWARD_SCALE, conduct_ref[nz - 1], above[1]) * (above[0] - heat_ref[nz - 1])
     z_flow_ref[1] = 2.0 * flow
     below, above = pick_halo("gy", y_halo, index_y % 2 == 1)
@@ -477,8 +475,11 @@
 
 
 def y_source_kernel(
-    source_ref, yl_ref, yr_ref, yinv_ref, yends_ref, ypart_ref, ysource_ref
+    heat_ref, source_ref, yl_ref, yr_ref, yinv_ref, yends_ref, ypart_ref, ysource_ref, spare_ref,
+    heat_out_ref
 ):
+    spare_ref[...] = jnp.zeros_like(spare_ref)
+    heat_out_ref[...] = heat_ref[...]
     ny = source_ref.shape[1]
     part = reduce_source(source_ref[...], 1, yl_ref, yr_ref, yinv_ref[...])
     ypart_ref[...] = part
@@ -491,7 +492,7 @@
     zends_ref, *refs
 ):
     messages, refs = refs[:count_y], refs[count_y:]
-    source_ref, zsource_ref, message_ref, ends_ref, *state = refs
+    source_ref, small_ref, message_ref, ends_ref, *state = refs
     nz, ny, nx = ypart_ref.shape
     if count_y > 2:
         first, last = chain_ends("gy", messages, yends_ref, ysource_ref[0], *state)
@@ -517,31 +518,94 @@
         source_ref[k] = source
         source_first = source_first + zlow_ref[k] * source
         source_last = source_last + zhigh_ref[k] * source
-    zsource_ref[...] = source_first
     outer, between, inverse = (zends_ref[i] for i in range(3))
-    message_ref[0], message_ref[1], message_ref[3] = (zends_ref[i] for i in range(3, 6))
-    message_ref[2] = outer * inverse * source_first
-    message_ref[4] = source_last + between * inverse * source_first
-
-
-def z_source_kernel(source_ref, zl_ref, zr_ref, zinv_ref, zpart_ref):
-    zpart_ref[...] = reduce_source(source_ref[...], 0, zl_ref, zr_ref, zinv_ref[...])
-
-
-def finish_kernel(
-    count_z, heat_ref, zpart_ref, zlow_ref, zhigh_ref, zends_ref, zsource_ref, *refs
+    for i, value in enumerate(
+        (outer, between, inverse, source_first, zends_ref[3], zends_ref[4])
+    ):
+        small_ref[i] = value
+    message_ref[0] = outer * inverse * source_first
+    message_ref[1] = source_last + between * inverse * source_first
+
+
+def z_source_kernel(heat_ref, source_ref, zl_ref, zr_ref, zinv_ref, small_ref, ready_ref):
+    nz = source_ref.shape[0]
+    inverse = zinv_ref[...]
+    ready_ref[0] = heat_ref[...] + reduce_source(source_ref[...], 0, zl_ref, zr_ref, inverse)
+    nothing = jnp.zeros_like(small_ref[0])
+    low = jnp.stack([nothing, small_ref[4]] + [nothing] * (nz - 2), 0)
+    ready_ref[1] = reduce_source(low, 0, zl_ref, zr_ref, inverse)
+    ready_ref[1, 0] = jnp.ones_like(nothing)
+    high = jnp.stack([nothing] * (nz - 2) + [small_ref[5], nothing], 0)
+    ready_ref[2] = reduce_source(high, 0, zl_ref, zr_ref, inverse)
+    ready_ref[2, nz - 1] = jnp.ones_like(nothing)
+
+
+def starting_order(messages, back=False):
+    if back:
+        return [messages[0], messages[-1], *messages[1:-1]]
+    return [messages[0], *messages[2:], messages[1]]
+
+
+def join_kernel(small_ref, *refs):
+    tail_ref, count, index = refs[-1], len(refs) - 1, lax.axis_index("gz")
+    messages = [refs[k] for k in starting_order(list(range(count)), True)]
+    tail_ref[:4] = small_ref[:4]
+    for shift, message in enumerate(messages):
+        place = 4 + 2 * lax.rem(index - shift + count, count)
+        tail_ref[pl.ds(place, 2)] = message[...]
+
+
+def finish_kernel(ready_ref, tail_ref, bands_ref, theirs_ref, mine_ref, state_ref):
+    count, index = (tail_ref.shape[0] - 4) // 2, lax.axis_index("gz")
+    blocks = [
+        (bands_ref[3 * k], bands_ref[3 * k + 1], tail_ref[4 + 2 * k], bands_ref[3 * k + 2],
+         tail_ref[5 + 2 * k])
+        for k in range(count)
+    ]
+    below, last = chain(blocks, count, index, state_ref)
+    outer, between, inverse, source_first = (tail_ref[i] for i in range(4))
+    first = (source_first + outer * below + between * last) * inverse
+    nx = theirs_ref.shape[-1]
+    heated = ready_ref[0] + ready_ref[1] * first + ready_ref[2] * last
+    theirs_ref[...], mine_ref[...] = heated[:, :, :nx], heated[:, :, nx:]
+
+
+def ends_kernel(
+    conduct_a_ref, edge_a_ref, label_b_ref, edge_b_ref, table_ref, zl_ref, zr_ref, zinv_ref,
+    message_ref, conduct_ref, edge_ref
 ):
-    messages, (theirs_ref, mine_ref, blocks_ref, state_ref) = refs[:count_z], refs[count_z:]
-    index = lax.axis_index("gz")
+    half = conduct_a_ref.shape[-1]
+    conduct_ref[:, :, :half] = conduct_a_ref[...]
+    conduct_ref[:, :, half:] = look_up(label_b_ref[...], table_ref)
+    edge_ref[:, :half] = edge_a_ref[...].astype(F32)
+    edge_ref[:, half:] = edge_b_ref[...].astype(F32)
+    conduct = conduct_ref[...]
+    nz = conduct.shape[0]
+    link = link_of(UPWARD_SCALE, conduct[1:], conduct[:-1])
+    link = jnp.concatenate([jnp.zeros_like(conduct[:1]), link], 0)
+    _, high, inverse, own = reduce_interior(link, 0, zl_ref, zr_ref)
+    zinv_ref[...] = inverse
+    own_first, own_last, between = end_bands(link, link[1], link[nz - 1], 0, high, own)
+    ground = UPWARD_SCALE * conduct[0] * edge_ref[...]
+    own_first = own_first + jnp.where(lax.axis_index("gz") == 0, ground, 0.0)
+    for i, value in enumerate((own_first, own_last, between, conduct[0], conduct[nz - 1])):
+        message_ref[i] = value
+
+
+def all_bands_kernel(*refs):
+    messages, (bands_ref, blocks_ref) = refs[:-2], refs[-2:]
+    count, index = len(messages), lax.axis_index("gz")
     for shift, message in enumerate(messages):
-        blocks_ref[lax.rem(index - shift + count_z, count_z)] = message[...]
-    blocks = [tuple(blocks_ref[k, i] for i in range(5)) for k in range(count_z)]
-    below, last = chain(blocks, count_z, index, state_ref)
-    outer, between, inverse = (zends_ref[i] for i in range(3))
-    first = (zsource_ref[...] + outer * below + between * last) * inverse
-    nx = theirs_ref.shape[-1]
-    heated = heat_ref[...] + zpart_ref[...] + zlow_ref[...] * first + zhigh_ref[...] * last
-    theirs_ref[...], mine_ref[...] = heated[:, :, :nx], heated[:, :, nx:]
+        blocks_ref[lax.rem(index - shift + count, count)] = message[...]
+    for k in range(count):
+        own_first, own_last, between, first, _ = (blocks_ref[k, i] for i in range(5))
+        outer = jnp.zeros_like(first)
+        if k > 0:
+            outer = link_of(UPWARD_SCALE, first, blocks_ref[k - 1, 4])
+        inverse = 1.0 / (own_first + between + outer)
+        bands_ref[3 * k] = outer * between * inverse
+        bands_ref[3 * k + 1] = outer * own_first * inverse
+        bands_ref[3 * k + 2] = own_last + between * own_first * inverse
 
 
 VMEM = pl.BlockSpec(memory_space=pltpu.VMEM)
@@ -615,12 +679,12 @@
     ) = call(
         x_bands_kernel,
         [(3, *lines)] * 2 + [lines] * 2 + [(2, *tiles), (3, *tiles), (8, lines[1])] + [block] * 3
-        + [(z_steps, *block)] * 2 + [block] * 3 + [(3, *layer)],
+        + [(z_steps, *block)] * 2 + [block] * 3 + [(5, *layer)],
         [heat, conduct],
     )
     x_message, z_flow, y_flow, z_ends = call(
         functools.partial(x_message_kernel, halo_counts),
-        [(8, lines[1]), (2, *layer), (2, *rows), (6, *layer)],
+        [(8, lines[1]), (2, *layer), (2, *rows), (5, *layer)],
         [heat, conduct, edge, x_low_block, x_high_block, x_ends, z_inner,
          *join_halos(z_halo, y_halo)],
     )
@@ -646,25 +710,61 @@
         [(count_x, 8, lines[1]), (8, count_x, lines[1]), (5, count_x, 8, lines[1])],
     )
     y_messages = swap_all("gy", y_message)
-    y_part, y_end_sources = call(
+    y_part, y_end_sources, spare, heat_out = call(
         y_source_kernel,
-        [block, (2, *rows)],
-        [y_source, y_left, y_right, y_inverse, y_ends],
-    )
-    z_source, z_first, z_message = call(
+        [block, (2, *rows), (bands_rows(count_z, nz), *layer), block],
+        [heat, y_source, y_left, y_right, y_inverse, y_ends],
+    )
+    z_source, z_small, z_message = call(
         functools.partial(z_message_kernel, count_y),
-        [block, layer, (5, *layer)],
+        [block, (6, *layer), (2, *layer)],
         [y_part, y_low, y_high, y_ends, y_end_sources, z_low, z_high, z_ends, *y_messages],
         [(2, *rows)] + ([] if two else [(count_y, y_rows, *rows), (5, count_y, *rows)]),
     )
-    z_messages = swap_all("gz", z_message)
-    (z_part,) = call(z_source_kernel, [block], [z_source, z_left, z_right, z_inverse])
-    return call(
-        functools.partial(finish_kernel, count_z),
-        [heat_a.shape] * 2,
-        [heat, z_part, z_low, z_high, z_ends, z_first, *z_messages],
-        [(count_z, 5, *layer), (5, count_z, *layer)],
-    )
+    return heat_out, spare, z_source, z_left, z_right, z_inverse, z_small, z_message
+
+
+def bands_rows(count_z, nz):
+    return -(-3 * count_z // nz) * nz
+
+
+def chip_bands(heat_b, label_b, edge_b, heat_a, conduct_a, edge_a, table):
+    nz, ny, half = conduct_a.shape
+    nx = 2 * half
+    block, layer, count_z = (nz, ny, nx), (ny, nx), lax.axis_size("gz")
+    z_steps = len(steps_of(nz))
+    z_left, z_right, z_inverse, message = call(
+        ends_kernel,
+        [(z_steps, *block)] * 2 + [block] + [(5, *layer)],
+        [conduct_a, edge_a, label_b, edge_b, table],
+        [block, layer],
+    )
+    (bands,) = call(
+        all_bands_kernel,
+        [(bands_rows(count_z, nz), *layer)],
+        swap_all("gz", message),
+        [(count_z, 5, *layer)],
+    )
+    zeros = lambda *shape: jnp.zeros(shape, F32)
+    return (
+        zeros(*block), bands, zeros(*block), z_left, z_right, z_inverse, zeros(6, *layer),
+        zeros(2, *layer),
+    )
+
+
+def z_round(heat, _, z_source, z_left, z_right, z_inverse, z_small, z_message):
+    count_z, block, layer = lax.axis_size("gz"), heat.shape, heat.shape[1:]
+    messages = swap_all("gz", z_message)
+    (ready,) = call(
+        z_source_kernel, [(3, *block)], [heat, z_source, z_left, z_right, z_inverse, z_small]
+    )
+    (tail,) = call(join_kernel, [(4 + 2 * count_z, *layer)], [z_small, *starting_order(messages)])
+    return ready, tail
+
+
+def z_idle(heat, *_):
+    count_z, block, layer = lax.axis_size("gz"), heat.shape, heat.shape[1:]
+    return jnp.zeros((3, *block), F32), jnp.zeros((4 + 2 * count_z, *layer), F32)
 
 
 def local(heat, label, table, edge):
@@ -681,11 +781,17 @@
         vmem=60,
     )
     second = lax.axis_index("gx") % 2 == 1
-    theirs, mine = lax.cond(
-        second,
-        chip_step,
-        lambda heat_a, label_a, edge_a, heat_b, *rest: (heat_a, heat_b),
+    state = lax.cond(
+        second, chip_step, chip_bands,
         heat_a, label_a, edge_a, own_heat, own_conduct, own_edge, rows,
+    )
+    bands = other_core(state[1])
+    ready, tail = lax.cond(second, z_round, z_idle, *state)
+    theirs, mine = call(
+        finish_kernel,
+        [heat_a.shape] * 2,
+        [ready, tail, bands],
+        [(5, lax.axis_size("gz"), *tail.shape[1:])],
     )
     return jnp.where(second, mine, other_core(theirs))
 

time: 22.3 us -> 22.1 us (level)
  starting transfers between devices: 19.6 us -> 15.3 us
  waiting for transfers between devices: 0.98 us -> 4.57 us
  Pallas kernels: 0.93 us -> 1.32 us
    ppermute x4 -> x5, starting transfers between devices: 19.6 us -> 8.38 us  [other_core(): return lax.ppermute(values, 'gx', [(i, i ^ 1) for i in range(count)])]
    ppermute x0 -> x3, starting transfers between devices: none -> 6.9 us  [swap_all(): lax.ppermute(message, name, [(i, (i + shift) % count) for i in range(coun...]
    ppermute x0 -> x3, waiting for transfers between devices: none -> 2.65 us  [swap_all(): lax.ppermute(message, name, [(i, (i + shift) % count) for i in range(coun...]
    ppermute x4 -> x5, waiting for transfers between devices: 0.98 us -> 1.92 us  [other_core(): return lax.ppermute(values, 'gx', [(i, i ^ 1) for i in range(count)])]
    pallas_call x1 -> x4, Pallas kernels: 0.93 us -> 1.32 us  [call(): pl.pallas_call(kernel, out_shape=[jax.ShapeDtypeStruct(out, F32) if isins...]
  transfers between devices with their start and end apart: 4 -> 8, of which waited for: 2 -> 6; matrix products, arithmetic and copies ran while one was open for 0% -> 0% of each run, Pallas kernels for 4% -> 4%
where the time goes in v8:
time: 22.1 us; the launch traced here: 22 us
  starting transfers between devices  15.3 us (69%)
  waiting for transfers between devices  4.57 us (21%)
  Pallas kernels  1.32 us (6%)
  other arithmetic  0.64 us (3%)
    ppermute x5, starting transfers between devices, other_core(): return lax.ppermute(values, 'gx', [(i, i ^ 1) for i in range(count)])  8.38 us
    ppermute x3, starting transfers between devices, swap_all(): lax.ppermute(message, name, [(i, (i + shift) % count) for i in range(coun...  6.9 us
    ppermute x3, waiting for transfers between devices, swap_all(): lax.ppermute(message, name, [(i, (i + shift) % count) for i in range(coun...  2.65 us
    ppermute x5, waiting for transfers between devices, other_core(): return lax.ppermute(values, 'gx', [(i, i ^ 1) for i in range(count)])  1.92 us
    pallas_call x4, Pallas kernels, call(): pl.pallas_call(kernel, out_shape=[jax.ShapeDtypeStruct(out, F32) if isins...  1.32 us
    select_n x1, other arithmetic, local(): return jnp.where(second, mine, other_core(theirs))  0.64 us
  transfers between devices with their start and end apart: 8, of which 6 were waited for; matrix products, arithmetic and copies ran while one was open for 0% of the time, Pallas kernels for 4%

profile of v8, /device:TPU:0, one launch (start us, length us, event | category | flops | bytes accessed | tf_op | source)
XLA Modules:
  0.0 22.0 jit_solution(11114288153661986958)
XLA Ops:
  0.0 0.5 %collective-permute-start.11 = (s32[16,8,128]{2,1,0:T(8,128)}, s32[16,8,128]{2,1,0:T(8,128)S(1)}, u32[]{:S(2)}, u32[]{:S(2)}) collective-permute-start(s32[16,8,128]{2,1,0:T(8,128)} %label_in.1), channel_id=1, source_target_pairs={{0,8},{8,0},{16,24},{24,16},{1,9},{9,1},{17,25},{25,17},{2,10},{10... | collective-permute-start | bytes 196616 | tf_op jit(solution)/shard_map/ppermute | solution.py:655
  0.5 0.1 collective-permute-start.13
  0.5 0.5 %collective-permute-start.12 = (s32[8,128]{1,0:T(8,128)}, s32[8,128]{1,0:T(8,128)S(1)}, u32[]{:S(2)}, u32[]{:S(2)}) collective-permute-start(s32[8,128]{1,0:T(8,128)} %edge_in.1), channel_id=1, source_target_pairs={{0,8},{8,0},{16,24},{24,16},{1,9},{9,1},{17,25},{25,17},{2,10},{10... | collective-permute-start | bytes 12296 | tf_op jit(solution)/shard_map/ppermute | solution.py:655
  1.0 0.9 %shard_map.46 = (f32[16,8,128]{2,1,0:T(8,128)S(1)}, f32[16,8,128]{2,1,0:T(8,128)S(1)}, f32[13,8,128]{2,1,0:T(8,128)S(1)}, s32[8,128]{1,0:T(8,128)S(1)}) custom-call(f32[16,8,128]{2,1,0:T(8,128)} %heat_in.1, s32[16,8,128]{2,1,0:T(8,128)} %label_in.1, f32[13]{0:T(128)} %table_in.1, s32[8,128]{1,0:T(8,128)} %edge_in.1), custom_call_target="tpu_custom_call" | custom-call | flops 200000 | bytes 200000 | tf_op jit(solution)/shard_map/pallas_call | solution.py:616
  1.9 0.1 collective-permute-done.12
  2.0 0.0 collective-permute-done.11
  2.0 0.0 collective-permute-done.13
  2.0 9.9 %conditional.2 = (f32[16,8,256]{2,1,0:T(8,128)S(1)}, f32[16,8,256]{2,1,0:T(8,128)S(1)}, f32[16,8,256]{2,1,0:T(8,128)S(1)}, f32[4,16,8,256]{3,2,1,0:T(8,128)S(1)}...) conditional(s32[]{:T(128)} %convert_element_type.4, ...), branch_computations={%region_0.1_spmd, %region_1.2_spmd} | conditional | flops 1600000 | bytes 2009864 | solution.py:784
  2.0 0.3 %branch_0_fun.2 = (f32[4,16,8,256]{3,2,1,0:T(8,128)S(1)}, f32[4,16,8,256]{3,2,1,0:T(8,128)S(1)}, f32[16,8,256]{2,1,0:T(8,128)S(1)}, f32[5,8,256]{2,1,0:T(8,128)S(1)}) custom-call(f32[16,8,128]{2,1,0:T(8,128)S(1)} %get-tuple-element.43.conduct_a_ref, s32[8,128]{1,0:T(8,128)S(1)} %get-tuple-element.44.edge_a_ref, ...), custom_call_target="tpu_custom_call" | custom-call | flops 200000 | bytes 200000 | tf_op jit(solution)/shard_map/cond/branch_0_fun/pallas_call | solution.py:616
  2.3 3.0 %collective-permute-start = (f32[5,8,256]{2,1,0:T(8,128)S(1)}, f32[5,8,256]{2,1,0:T(8,128)S(1)}, u32[]{:S(2)}, u32[]{:S(2)}) collective-permute-start(f32[5,8,256]{2,1,0:T(8,128)S(1)} %get-tuple-element.48.refs_0_), channel_id=1, source_target_pairs={{0,1},{1,2},{2,3},{3,0},{4,5},{5,6},{6,7},{7,4},{8,9},{9,10},{10,1... | collective-permute-start | bytes 122888 | tf_op jit(solution)/shard_map/cond/branch_0_fun/ppermute | solution.py:648
  5.2 2.6 %collective-permute-start.1 = (f32[5,8,256]{2,1,0:T(8,128)S(1)}, f32[5,8,256]{2,1,0:T(8,128)S(1)}, u32[]{:S(2)}, u32[]{:S(2)}) collective-permute-start(f32[5,8,256]{2,1,0:T(8,128)S(1)} %get-tuple-element.48.refs_0_), channel_id=1, source_target_pairs={{0,2},{1,3},{2,0},{3,1},{4,6},{5,7},{6,4},{7,5},{8,10},{9,11},{10,... | collective-permute-start | bytes 122888 | tf_op jit(solution)/shard_map/cond/branch_0_fun/ppermute | solution.py:648
  7.8 1.3 %collective-permute-start.2 = (f32[5,8,256]{2,1,0:T(8,128)S(1)}, f32[5,8,256]{2,1,0:T(8,128)S(1)}, u32[]{:S(2)}, u32[]{:S(2)}) collective-permute-start(f32[5,8,256]{2,1,0:T(8,128)S(1)} %get-tuple-element.48.refs_0_), channel_id=1, source_target_pairs={{0,3},{1,0},{2,1},{3,2},{4,7},{5,4},{6,5},{7,6},{8,11},{9,8},{10,9... | collective-permute-start | bytes 122888 | tf_op jit(solution)/shard_map/cond/branch_0_fun/ppermute | solution.py:648
  9.2 0.1 collective-permute-done.refs_1_
  9.3 0.9 %collective-permute-done.1.refs_2_ = f32[5,8,256]{2,1,0:T(8,128)S(1)} collective-permute-done((f32[5,8,256]{2,1,0:T(8,128)S(1)}, f32[5,8,256]{2,1,0:T(8,128)S(1)}, u32[]{:S(2)}, u32[]{:S(2)}) %collective-permute-start.1) | collective-permute-done | bytes 40992 | tf_op jit(solution)/shard_map/cond/branch_0_fun/ppermute | solution.py:648
  10.1 1.7 %collective-permute-done.2.refs_3_ = f32[5,8,256]{2,1,0:T(8,128)S(1)} collective-permute-done((f32[5,8,256]{2,1,0:T(8,128)S(1)}, f32[5,8,256]{2,1,0:T(8,128)S(1)}, u32[]{:S(2)}, u32[]{:S(2)}) %collective-permute-start.2) | collective-permute-done | bytes 40992 | tf_op jit(solution)/shard_map/cond/branch_0_fun/ppermute | solution.py:648
  12.0 3.1 %collective-permute-start.14 = (f32[16,8,256]{2,1,0:T(8,128)S(1)}, f32[16,8,256]{2,1,0:T(8,128)S(1)}, u32[]{:S(2)}, u32[]{:S(2)}) collective-permute-start(f32[16,8,256]{2,1,0:T(8,128)S(1)} %get-tuple-element.138), channel_id=1, source_target_pairs={{0,8},{8,0},{16,24},{24,16},{1,9},{9,1},{17,25},{25,17},{2,10},{10... | collective-permute-start | bytes 393224 | tf_op jit(solution)/shard_map/ppermute | solution.py:655
  15.2 0.9 %collective-permute-done.14.bands_ref = f32[16,8,256]{2,1,0:T(8,128)S(1)} collective-permute-done((f32[16,8,256]{2,1,0:T(8,128)S(1)}, f32[16,8,256]{2,1,0:T(8,128)S(1)}, u32[]{:S(2)}, u32[]{:S(2)}) %collective-permute-start.14) | collective-permute-done | bytes 131104 | tf_op jit(solution)/shard_map/ppermute | solution.py:655
  16.1 0.1 shard_map.47
  16.2 4.3 %collective-permute-start.15 = (f32[16,8,128]{2,1,0:T(8,128)S(1)}, f32[16,8,128]{2,1,0:T(8,128)S(1)}, u32[]{:S(2)}, u32[]{:S(2)}) collective-permute-start(f32[16,8,128]{2,1,0:T(8,128)S(1)} %get-tuple-element.140), channel_id=1, source_target_pairs={{0,8},{8,0},{16,24},{24,16},{1,9},{9,1},{17,25},{25,17},{2,10},{10... | collective-permute-start | bytes 196616 | tf_op jit(solution)/shard_map/ppermute | solution.py:655
  20.4 0.9 %collective-permute-done.15 = f32[16,8,128]{2,1,0:T(8,128)S(1)} collective-permute-done((f32[16,8,128]{2,1,0:T(8,128)S(1)}, f32[16,8,128]{2,1,0:T(8,128)S(1)}, u32[]{:S(2)}, u32[]{:S(2)}) %collective-permute-start.15) | collective-permute-done | bytes 65568 | tf_op jit(solution)/shard_map/ppermute | solution.py:655
  21.3 0.6 %broadcast_select_fusion = f32[16,8,128]{2,1,0:T(8,128)} fusion(f32[16,8,128]{2,1,0:T(8,128)S(1)} %get-tuple-element.139, f32[16,8,128]{2,1,0:T(8,128)S(1)} %collective-permute-done.15, pred[]{:T(512)S(6)} %eq.5), kind=kLoop, calls=%fused_computation | loop fusion | flops 16384 | bytes 196609 | tf_op jit(solution)/shard_map/jit(_where)/select_n | solution.py:796
  (8 shorter events, 0.2 us)
Async XLA Ops:
  0.0 2.0 %collective-permute-start.11 = (s32[16,8,128]{2,1,0:T(8,128)}, s32[16,8,128]{2,1,0:T(8,128)S(1)}, u32[]{:S(2)}, u32[]{:S(2)}) collective-permute-start(s32[16,8,128]{2,1,0:T(8,128)} %label_in.1), channel_id=1, source_target_pairs={{0,8},{8,0},{16,24},{24,16},{1,9},{9,1},{17,25},{25,17},{2,10},{10... | collective-permute-start | bytes 196616 | tf_op jit(solution)/shard_map/ppermute | solution.py:655
  0.5 1.6 %collective-permute-start.13 = (f32[16,8,128]{2,1,0:T(8,128)}, f32[16,8,128]{2,1,0:T(8,128)S(1)}, u32[]{:S(2)}, u32[]{:S(2)}) collective-permute-start(f32[16,8,128]{2,1,0:T(8,128)} %heat_in.1), channel_id=1, source_target_pairs={{0,8},{8,0},{16,24},{24,16},{1,9},{9,1},{17,25},{25,17},{2,10},{10... | collective-permute-start | bytes 196616 | tf_op jit(solution)/shard_map/ppermute | solution.py:655
  0.5 1.5 %collective-permute-start.12 = (s32[8,128]{1,0:T(8,128)}, s32[8,128]{1,0:T(8,128)S(1)}, u32[]{:S(2)}, u32[]{:S(2)}) collective-permute-start(s32[8,128]{1,0:T(8,128)} %edge_in.1), channel_id=1, source_target_pairs={{0,8},{8,0},{16,24},{24,16},{1,9},{9,1},{17,25},{25,17},{2,10},{10... | collective-permute-start | bytes 12296 | tf_op jit(solution)/shard_map/ppermute | solution.py:655
  2.3 7.0 %collective-permute-start = (f32[5,8,256]{2,1,0:T(8,128)S(1)}, f32[5,8,256]{2,1,0:T(8,128)S(1)}, u32[]{:S(2)}, u32[]{:S(2)}) collective-permute-start(f32[5,8,256]{2,1,0:T(8,128)S(1)} %get-tuple-element.48.refs_0_), channel_id=1, source_target_pairs={{0,1},{1,2},{2,3},{3,0},{4,5},{5,6},{6,7},{7,4},{8,9},{9,10},{10,1... | collective-permute-start | bytes 122888 | tf_op jit(solution)/shard_map/cond/branch_0_fun/ppermute | solution.py:648
  5.2 4.9 %collective-permute-start.1 = (f32[5,8,256]{2,1,0:T(8,128)S(1)}, f32[5,8,256]{2,1,0:T(8,128)S(1)}, u32[]{:S(2)}, u32[]{:S(2)}) collective-permute-start(f32[5,8,256]{2,1,0:T(8,128)S(1)} %get-tuple-element.48.refs_0_), channel_id=1, source_target_pairs={{0,2},{1,3},{2,0},{3,1},{4,6},{5,7},{6,4},{7,5},{8,10},{9,11},{10,... | collective-permute-start | bytes 122888 | tf_op jit(solution)/shard_map/cond/branch_0_fun/ppermute | solution.py:648
  7.8 4.0 %collective-permute-start.2 = (f32[5,8,256]{2,1,0:T(8,128)S(1)}, f32[5,8,256]{2,1,0:T(8,128)S(1)}, u32[]{:S(2)}, u32[]{:S(2)}) collective-permute-start(f32[5,8,256]{2,1,0:T(8,128)S(1)} %get-tuple-element.48.refs_0_), channel_id=1, source_target_pairs={{0,3},{1,0},{2,1},{3,2},{4,7},{5,4},{6,5},{7,6},{8,11},{9,8},{10,9... | collective-permute-start | bytes 122888 | tf_op jit(solution)/shard_map/cond/branch_0_fun/ppermute | solution.py:648
  12.0 4.1 %collective-permute-start.14 = (f32[16,8,256]{2,1,0:T(8,128)S(1)}, f32[16,8,256]{2,1,0:T(8,128)S(1)}, u32[]{:S(2)}, u32[]{:S(2)}) collective-permute-start(f32[16,8,256]{2,1,0:T(8,128)S(1)} %get-tuple-element.138), channel_id=1, source_target_pairs={{0,8},{8,0},{16,24},{24,16},{1,9},{9,1},{17,25},{25,17},{2,10},{10... | collective-permute-start | bytes 393224 | tf_op jit(solution)/shard_map/ppermute | solution.py:655
  16.2 5.2 %collective-permute-start.15 = (f32[16,8,128]{2,1,0:T(8,128)S(1)}, f32[16,8,128]{2,1,0:T(8,128)S(1)}, u32[]{:S(2)}, u32[]{:S(2)}) collective-permute-start(f32[16,8,128]{2,1,0:T(8,128)S(1)} %get-tuple-element.140), channel_id=1, source_target_pairs={{0,8},{8,0},{16,24},{24,16},{1,9},{9,1},{17,25},{25,17},{2,10},{10... | collective-permute-start | bytes 196616 | tf_op jit(solution)/shard_map/ppermute | solution.py:655

commit v9 on v8

--- a/solution.py
+++ b/solution.py
@@ -593,7 +593,7 @@
 
 
 def all_bands_kernel(*refs):
-    messages, (bands_ref, blocks_ref) = refs[:-2], refs[-2:]
+    messages, (bands_ref, blocks_ref) = refs[:-2][::-1], refs[-2:]
     count, index = len(messages), lax.axis_index("gz")
     for shift, message in enumerate(messages):
         blocks_ref[lax.rem(index - shift + count, count)] = message[...]
@@ -742,7 +742,7 @@
     (bands,) = call(
         all_bands_kernel,
         [(bands_rows(count_z, nz), *layer)],
-        swap_all("gz", message),
+        swap_all("gz", message)[::-1],
         [(count_z, 5, *layer)],
     )
     zeros = lambda *shape: jnp.zeros(shape, F32)

time: 22.1 us -> 21.9 us (level)
  starting transfers between devices: 15.3 us -> 12.9 us
  waiting for transfers between devices: 4.57 us -> 6.71 us
    ppermute x3, waiting for transfers between devices: 2.65 us -> 4.79 us  [swap_all(): lax.ppermute(message, name, [(i, (i + shift) % count) for i in range(coun...]
    ppermute x5, starting transfers between devices: 8.38 us -> 6.9 us  [other_core(): return lax.ppermute(values, 'gx', [(i, i ^ 1) for i in range(count)])]
    ppermute x3, starting transfers between devices: 6.9 us -> 6.01 us  [swap_all(): lax.ppermute(message, name, [(i, (i + shift) % count) for i in range(coun...]
where the time goes in v9:
time: 21.9 us; the launch traced here: 21.7 us
  starting transfers between devices  12.9 us (59%)
  waiting for transfers between devices  6.71 us (31%)
  Pallas kernels  1.32 us (6%)
  other arithmetic  0.64 us (3%)
    ppermute x5, starting transfers between devices, other_core(): return lax.ppermute(values, 'gx', [(i, i ^ 1) for i in range(count)])  6.9 us
    ppermute x3, starting transfers between devices, swap_all(): lax.ppermute(message, name, [(i, (i + shift) % count) for i in range(coun...  6.01 us
    ppermute x3, waiting for transfers between devices, swap_all(): lax.ppermute(message, name, [(i, (i + shift) % count) for i in range(coun...  4.79 us
    ppermute x5, waiting for transfers between devices, other_core(): return lax.ppermute(values, 'gx', [(i, i ^ 1) for i in range(count)])  1.92 us
    pallas_call x4, Pallas kernels, call(): pl.pallas_call(kernel, out_shape=[jax.ShapeDtypeStruct(out, F32) if isins...  1.32 us
    select_n x1, other arithmetic, local(): return jnp.where(second, mine, other_core(theirs))  0.64 us
  transfers between devices with their start and end apart: 8, of which 6 were waited for; matrix products, arithmetic and copies ran while one was open for 0% of the time, Pallas kernels for 4%

profile of v9, /device:TPU:0, one launch (start us, length us, event | category | flops | bytes accessed | tf_op | source)
XLA Modules:
  0.0 21.7 jit_solution(13717541206804756756)
XLA Ops:
  0.0 0.5 %collective-permute-start.11 = (s32[16,8,128]{2,1,0:T(8,128)}, s32[16,8,128]{2,1,0:T(8,128)S(1)}, u32[]{:S(2)}, u32[]{:S(2)}) collective-permute-start(s32[16,8,128]{2,1,0:T(8,128)} %label_in.1), channel_id=1, source_target_pairs={{0,8},{8,0},{16,24},{24,16},{1,9},{9,1},{17,25},{25,17},{2,10},{10... | collective-permute-start | bytes 196616 | tf_op jit(solution)/shard_map/ppermute | solution.py:655
  0.5 0.1 collective-permute-start.13
  0.5 0.5 %collective-permute-start.12 = (s32[8,128]{1,0:T(8,128)}, s32[8,128]{1,0:T(8,128)S(1)}, u32[]{:S(2)}, u32[]{:S(2)}) collective-permute-start(s32[8,128]{1,0:T(8,128)} %edge_in.1), channel_id=1, source_target_pairs={{0,8},{8,0},{16,24},{24,16},{1,9},{9,1},{17,25},{25,17},{2,10},{10... | collective-permute-start | bytes 12296 | tf_op jit(solution)/shard_map/ppermute | solution.py:655
  1.0 0.9 %shard_map.46 = (f32[16,8,128]{2,1,0:T(8,128)S(1)}, f32[16,8,128]{2,1,0:T(8,128)S(1)}, f32[13,8,128]{2,1,0:T(8,128)S(1)}, s32[8,128]{1,0:T(8,128)S(1)}) custom-call(f32[16,8,128]{2,1,0:T(8,128)} %heat_in.1, s32[16,8,128]{2,1,0:T(8,128)} %label_in.1, f32[13]{0:T(128)} %table_in.1, s32[8,128]{1,0:T(8,128)} %edge_in.1), custom_call_target="tpu_custom_call" | custom-call | flops 200000 | bytes 200000 | tf_op jit(solution)/shard_map/pallas_call | solution.py:616
  1.9 0.1 collective-permute-done.12
  2.0 0.0 collective-permute-done.11
  2.0 0.0 collective-permute-done.13
  2.0 11.2 %conditional.2 = (f32[16,8,256]{2,1,0:T(8,128)S(1)}, f32[16,8,256]{2,1,0:T(8,128)S(1)}, f32[16,8,256]{2,1,0:T(8,128)S(1)}, f32[4,16,8,256]{3,2,1,0:T(8,128)S(1)}...) conditional(s32[]{:T(128)} %convert_element_type.4, ...), branch_computations={%region_0.1_spmd, %region_1.2_spmd} | conditional | flops 1600000 | bytes 2009864 | solution.py:784
  2.0 0.3 %branch_0_fun.2 = (f32[4,16,8,256]{3,2,1,0:T(8,128)S(1)}, f32[4,16,8,256]{3,2,1,0:T(8,128)S(1)}, f32[16,8,256]{2,1,0:T(8,128)S(1)}, f32[5,8,256]{2,1,0:T(8,128)S(1)}) custom-call(f32[16,8,128]{2,1,0:T(8,128)S(1)} %get-tuple-element.43.conduct_a_ref, s32[8,128]{1,0:T(8,128)S(1)} %get-tuple-element.44.edge_a_ref, ...), custom_call_target="tpu_custom_call" | custom-call | flops 200000 | bytes 200000 | tf_op jit(solution)/shard_map/cond/branch_0_fun/pallas_call | solution.py:616
  2.3 5.0 %collective-permute-start = (f32[5,8,256]{2,1,0:T(8,128)S(1)}, f32[5,8,256]{2,1,0:T(8,128)S(1)}, u32[]{:S(2)}, u32[]{:S(2)}) collective-permute-start(f32[5,8,256]{2,1,0:T(8,128)S(1)} %get-tuple-element.48.refs_3_), channel_id=1, source_target_pairs={{0,3},{1,0},{2,1},{3,2},{4,7},{5,4},{6,5},{7,6},{8,11},{9,8},{10,9... | collective-permute-start | bytes 122888 | tf_op jit(solution)/shard_map/cond/branch_0_fun/ppermute | solution.py:648
  7.3 0.0 collective-permute-start.1
  7.3 1.0 %collective-permute-start.2 = (f32[5,8,256]{2,1,0:T(8,128)S(1)}, f32[5,8,256]{2,1,0:T(8,128)S(1)}, u32[]{:S(2)}, u32[]{:S(2)}) collective-permute-start(f32[5,8,256]{2,1,0:T(8,128)S(1)} %get-tuple-element.48.refs_3_), channel_id=1, source_target_pairs={{0,1},{1,2},{2,3},{3,0},{4,5},{5,6},{6,7},{7,4},{8,9},{9,10},{10,1... | collective-permute-start | bytes 122888 | tf_op jit(solution)/shard_map/cond/branch_0_fun/ppermute | solution.py:648
  8.3 0.7 %collective-permute-done.refs_0_ = f32[5,8,256]{2,1,0:T(8,128)S(1)} collective-permute-done((f32[5,8,256]{2,1,0:T(8,128)S(1)}, f32[5,8,256]{2,1,0:T(8,128)S(1)}, u32[]{:S(2)}, u32[]{:S(2)}) %collective-permute-start) | collective-permute-done | bytes 40992 | tf_op jit(solution)/shard_map/cond/branch_0_fun/ppermute | solution.py:648
  8.9 3.2 %collective-permute-done.1.refs_1_ = f32[5,8,256]{2,1,0:T(8,128)S(1)} collective-permute-done((f32[5,8,256]{2,1,0:T(8,128)S(1)}, f32[5,8,256]{2,1,0:T(8,128)S(1)}, u32[]{:S(2)}, u32[]{:S(2)}) %collective-permute-start.1) | collective-permute-done | bytes 40992 | tf_op jit(solution)/shard_map/cond/branch_0_fun/ppermute | solution.py:648
  12.2 0.9 %collective-permute-done.2.refs_2_ = f32[5,8,256]{2,1,0:T(8,128)S(1)} collective-permute-done((f32[5,8,256]{2,1,0:T(8,128)S(1)}, f32[5,8,256]{2,1,0:T(8,128)S(1)}, u32[]{:S(2)}, u32[]{:S(2)}) %collective-permute-start.2) | collective-permute-done | bytes 40992 | tf_op jit(solution)/shard_map/cond/branch_0_fun/ppermute | solution.py:648
  13.2 1.3 %collective-permute-start.14 = (f32[16,8,256]{2,1,0:T(8,128)S(1)}, f32[16,8,256]{2,1,0:T(8,128)S(1)}, u32[]{:S(2)}, u32[]{:S(2)}) collective-permute-start(f32[16,8,256]{2,1,0:T(8,128)S(1)} %get-tuple-element.138), channel_id=1, source_target_pairs={{0,8},{8,0},{16,24},{24,16},{1,9},{9,1},{17,25},{25,17},{2,10},{10... | collective-permute-start | bytes 393224 | tf_op jit(solution)/shard_map/ppermute | solution.py:655
  14.6 0.9 %collective-permute-done.14.bands_ref = f32[16,8,256]{2,1,0:T(8,128)S(1)} collective-permute-done((f32[16,8,256]{2,1,0:T(8,128)S(1)}, f32[16,8,256]{2,1,0:T(8,128)S(1)}, u32[]{:S(2)}, u32[]{:S(2)}) %collective-permute-start.14) | collective-permute-done | bytes 131104 | tf_op jit(solution)/shard_map/ppermute | solution.py:655
  15.5 0.1 shard_map.47
  15.6 4.6 %collective-permute-start.15 = (f32[16,8,128]{2,1,0:T(8,128)S(1)}, f32[16,8,128]{2,1,0:T(8,128)S(1)}, u32[]{:S(2)}, u32[]{:S(2)}) collective-permute-start(f32[16,8,128]{2,1,0:T(8,128)S(1)} %get-tuple-element.140), channel_id=1, source_target_pairs={{0,8},{8,0},{16,24},{24,16},{1,9},{9,1},{17,25},{25,17},{2,10},{10... | collective-permute-start | bytes 196616 | tf_op jit(solution)/shard_map/ppermute | solution.py:655
  20.2 0.9 %collective-permute-done.15 = f32[16,8,128]{2,1,0:T(8,128)S(1)} collective-permute-done((f32[16,8,128]{2,1,0:T(8,128)S(1)}, f32[16,8,128]{2,1,0:T(8,128)S(1)}, u32[]{:S(2)}, u32[]{:S(2)}) %collective-permute-start.15) | collective-permute-done | bytes 65568 | tf_op jit(solution)/shard_map/ppermute | solution.py:655
  21.1 0.6 %broadcast_select_fusion = f32[16,8,128]{2,1,0:T(8,128)} fusion(f32[16,8,128]{2,1,0:T(8,128)S(1)} %get-tuple-element.139, f32[16,8,128]{2,1,0:T(8,128)S(1)} %collective-permute-done.15, pred[]{:T(512)S(6)} %eq.5), kind=kLoop, calls=%fused_computation | loop fusion | flops 16384 | bytes 196609 | tf_op jit(solution)/shard_map/jit(_where)/select_n | solution.py:796
  (8 shorter events, 0.2 us)
Async XLA Ops:
  0.0 2.0 %collective-permute-start.11 = (s32[16,8,128]{2,1,0:T(8,128)}, s32[16,8,128]{2,1,0:T(8,128)S(1)}, u32[]{:S(2)}, u32[]{:S(2)}) collective-permute-start(s32[16,8,128]{2,1,0:T(8,128)} %label_in.1), channel_id=1, source_target_pairs={{0,8},{8,0},{16,24},{24,16},{1,9},{9,1},{17,25},{25,17},{2,10},{10... | collective-permute-start | bytes 196616 | tf_op jit(solution)/shard_map/ppermute | solution.py:655
  0.5 1.6 %collective-permute-start.13 = (f32[16,8,128]{2,1,0:T(8,128)}, f32[16,8,128]{2,1,0:T(8,128)S(1)}, u32[]{:S(2)}, u32[]{:S(2)}) collective-permute-start(f32[16,8,128]{2,1,0:T(8,128)} %heat_in.1), channel_id=1, source_target_pairs={{0,8},{8,0},{16,24},{24,16},{1,9},{9,1},{17,25},{25,17},{2,10},{10... | collective-permute-start | bytes 196616 | tf_op jit(solution)/shard_map/ppermute | solution.py:655
  0.5 1.5 %collective-permute-start.12 = (s32[8,128]{1,0:T(8,128)}, s32[8,128]{1,0:T(8,128)S(1)}, u32[]{:S(2)}, u32[]{:S(2)}) collective-permute-start(s32[8,128]{1,0:T(8,128)} %edge_in.1), channel_id=1, source_target_pairs={{0,8},{8,0},{16,24},{24,16},{1,9},{9,1},{17,25},{25,17},{2,10},{10... | collective-permute-start | bytes 12296 | tf_op jit(solution)/shard_map/ppermute | solution.py:655
  2.3 6.7 %collective-permute-start = (f32[5,8,256]{2,1,0:T(8,128)S(1)}, f32[5,8,256]{2,1,0:T(8,128)S(1)}, u32[]{:S(2)}, u32[]{:S(2)}) collective-permute-start(f32[5,8,256]{2,1,0:T(8,128)S(1)} %get-tuple-element.48.refs_3_), channel_id=1, source_target_pairs={{0,3},{1,0},{2,1},{3,2},{4,7},{5,4},{6,5},{7,6},{8,11},{9,8},{10,9... | collective-permute-start | bytes 122888 | tf_op jit(solution)/shard_map/cond/branch_0_fun/ppermute | solution.py:648
  7.3 4.9 %collective-permute-start.1 = (f32[5,8,256]{2,1,0:T(8,128)S(1)}, f32[5,8,256]{2,1,0:T(8,128)S(1)}, u32[]{:S(2)}, u32[]{:S(2)}) collective-permute-start(f32[5,8,256]{2,1,0:T(8,128)S(1)} %get-tuple-element.48.refs_3_), channel_id=1, source_target_pairs={{0,2},{1,3},{2,0},{3,1},{4,6},{5,7},{6,4},{7,5},{8,10},{9,11},{10,... | collective-permute-start | bytes 122888 | tf_op jit(solution)/shard_map/cond/branch_0_fun/ppermute | solution.py:648
  7.3 5.8 %collective-permute-start.2 = (f32[5,8,256]{2,1,0:T(8,128)S(1)}, f32[5,8,256]{2,1,0:T(8,128)S(1)}, u32[]{:S(2)}, u32[]{:S(2)}) collective-permute-start(f32[5,8,256]{2,1,0:T(8,128)S(1)} %get-tuple-element.48.refs_3_), channel_id=1, source_target_pairs={{0,1},{1,2},{2,3},{3,0},{4,5},{5,6},{6,7},{7,4},{8,9},{9,10},{10,1... | collective-permute-start | bytes 122888 | tf_op jit(solution)/shard_map/cond/branch_0_fun/ppermute | solution.py:648
  13.2 2.3 %collective-permute-start.14 = (f32[16,8,256]{2,1,0:T(8,128)S(1)}, f32[16,8,256]{2,1,0:T(8,128)S(1)}, u32[]{:S(2)}, u32[]{:S(2)}) collective-permute-start(f32[16,8,256]{2,1,0:T(8,128)S(1)} %get-tuple-element.138), channel_id=1, source_target_pairs={{0,8},{8,0},{16,24},{24,16},{1,9},{9,1},{17,25},{25,17},{2,10},{10... | collective-permute-start | bytes 393224 | tf_op jit(solution)/shard_map/ppermute | solution.py:655
  15.6 5.5 %collective-permute-start.15 = (f32[16,8,128]{2,1,0:T(8,128)S(1)}, f32[16,8,128]{2,1,0:T(8,128)S(1)}, u32[]{:S(2)}, u32[]{:S(2)}) collective-permute-start(f32[16,8,128]{2,1,0:T(8,128)S(1)} %get-tuple-element.140), channel_id=1, source_target_pairs={{0,8},{8,0},{16,24},{24,16},{1,9},{9,1},{17,25},{25,17},{2,10},{10... | collective-permute-start | bytes 196616 | tf_op jit(solution)/shard_map/ppermute | solution.py:655

commit v10 on v9

--- a/solution.py
+++ b/solution.py
@@ -342,11 +342,19 @@
         zends_ref[i] = value
     flow = link_of(UPWARD_SCALE, conduct_ref[nz - 1], above[1]) * (above[0] - heat_ref[nz - 1])
     z_flow_ref[1] = 2.0 * flow
-    below, above = pick_halo("gy", y_halo, index_y % 2 == 1)
-    flow = link_of(FLAT_SCALE, conduct_ref[:, 0, :], below[1]) * (below[0] - heat_ref[:, 0, :])
-    y_flow_ref[0] = 2.0 * flow
-    flow = link_of(FLAT_SCALE, conduct_ref[:, ny - 1, :], above[1])
-    y_flow_ref[1] = 2.0 * flow * (above[0] - heat_ref[:, ny - 1, :])
+    odd = index_y % 2 == 1
+    near = lambda ref: jnp.where(odd, ref[:, 0, :], ref[:, ny - 1, :])
+    if len(y_halo) == 1:
+        flow = link_of(FLAT_SCALE, near(conduct_ref), y_halo[0][1])
+        flow = 2.0 * flow * (y_halo[0][0] - near(heat_ref))
+        y_flow_ref[0] = jnp.where(odd, flow, 0.0)
+        y_flow_ref[1] = jnp.where(odd, 0.0, flow)
+    else:
+        below, above = pick_halo("gy", y_halo, index_y % 2 == 1)
+        flow = link_of(FLAT_SCALE, conduct_ref[:, 0, :], below[1]) * (below[0] - heat_ref[:, 0, :])
+        y_flow_ref[0] = 2.0 * flow
+        flow = link_of(FLAT_SCALE, conduct_ref[:, ny - 1, :], above[1])
+        y_flow_ref[1] = 2.0 * flow * (above[0] - heat_ref[:, ny - 1, :])
 
     def spread(values, first, step):
         shape = (values.shape[0], lanes)
@@ -358,8 +366,11 @@
     for share in (low_ref, high_ref):
         layers = spread(share[0] * z_flow_ref[0], 0, 1)
         layers = layers + spread(share[nz - 1] * z_flow_ref[1], lanes - ny, 1)
-        rows = spread(share[:, 0, :] * y_flow_ref[0], 0, ny)
-        rows = rows + spread(share[:, ny - 1, :] * y_flow_ref[1], ny - 1, ny)
+        if len(y_halo) == 1:
+            rows = spread(near(share) * flow, jnp.where(odd, 0, ny - 1), ny)
+        else:
+            rows = spread(share[:, 0, :] * y_flow_ref[0], 0, ny)
+            rows = rows + spread(share[:, ny - 1, :] * y_flow_ref[1], ny - 1, ny)
         sums.append(jnp.sum(layers, 0, keepdims=True) + jnp.sum(rows, 0, keepdims=True))
     ends = ends_ref[...]
     message_ref[...] = jnp.concatenate([ends[0:1] + sums[0], ends[1:2] + sums[1], ends[2:8]], 0)

time: 21.9 us -> 21.9 us (level)
  no operation moved by 1% of the time
where the time goes in v10:
time: 21.9 us; the launch traced here: 21.7 us
  starting transfers between devices  12.9 us (59%)
  waiting for transfers between devices  6.71 us (31%)
  Pallas kernels  1.32 us (6%)
  other arithmetic  0.64 us (3%)
    ppermute x5, starting transfers between devices, other_core(): return lax.ppermute(values, 'gx', [(i, i ^ 1) for i in range(count)])  6.88 us
    ppermute x3, starting transfers between devices, swap_all(): lax.ppermute(message, name, [(i, (i + shift) % count) for i in range(coun...  6.01 us
    ppermute x3, waiting for transfers between devices, swap_all(): lax.ppermute(message, name, [(i, (i + shift) % count) for i in range(coun...  4.79 us
    ppermute x5, waiting for transfers between devices, other_core(): return lax.ppermute(values, 'gx', [(i, i ^ 1) for i in range(count)])  1.92 us
    pallas_call x4, Pallas kernels, call(): pl.pallas_call(kernel, out_shape=[jax.ShapeDtypeStruct(out, F32) if isins...  1.32 us
    select_n x1, other arithmetic, local(): return jnp.where(second, mine, other_core(theirs))  0.64 us
  transfers between devices with their start and end apart: 8, of which 6 were waited for; matrix products, arithmetic and copies ran while one was open for 0% of the time, Pallas kernels for 4%

profile of v10, /device:TPU:0, one launch (start us, length us, event | category | flops | bytes accessed | tf_op | source)
XLA Modules:
  0.0 21.7 jit_solution(12930861091342537679)
XLA Ops:
  0.0 0.5 %collective-permute-start.11 = (s32[16,8,128]{2,1,0:T(8,128)}, s32[16,8,128]{2,1,0:T(8,128)S(1)}, u32[]{:S(2)}, u32[]{:S(2)}) collective-permute-start(s32[16,8,128]{2,1,0:T(8,128)} %label_in.1), channel_id=1, source_target_pairs={{0,8},{8,0},{16,24},{24,16},{1,9},{9,1},{17,25},{25,17},{2,10},{10... | collective-permute-start | bytes 196616 | tf_op jit(solution)/shard_map/ppermute | solution.py:666
  0.5 0.1 collective-permute-start.13
  0.5 0.5 %collective-permute-start.12 = (s32[8,128]{1,0:T(8,128)}, s32[8,128]{1,0:T(8,128)S(1)}, u32[]{:S(2)}, u32[]{:S(2)}) collective-permute-start(s32[8,128]{1,0:T(8,128)} %edge_in.1), channel_id=1, source_target_pairs={{0,8},{8,0},{16,24},{24,16},{1,9},{9,1},{17,25},{25,17},{2,10},{10... | collective-permute-start | bytes 12296 | tf_op jit(solution)/shard_map/ppermute | solution.py:666
  1.0 0.9 %shard_map.46 = (f32[16,8,128]{2,1,0:T(8,128)S(1)}, f32[16,8,128]{2,1,0:T(8,128)S(1)}, f32[13,8,128]{2,1,0:T(8,128)S(1)}, s32[8,128]{1,0:T(8,128)S(1)}) custom-call(f32[16,8,128]{2,1,0:T(8,128)} %heat_in.1, s32[16,8,128]{2,1,0:T(8,128)} %label_in.1, f32[13]{0:T(128)} %table_in.1, s32[8,128]{1,0:T(8,128)} %edge_in.1), custom_call_target="tpu_custom_call" | custom-call | flops 200000 | bytes 200000 | tf_op jit(solution)/shard_map/pallas_call | solution.py:627
  1.9 0.1 collective-permute-done.12
  2.0 0.0 collective-permute-done.11
  2.0 0.0 collective-permute-done.13
  2.0 11.2 %conditional.2 = (f32[16,8,256]{2,1,0:T(8,128)S(1)}, f32[16,8,256]{2,1,0:T(8,128)S(1)}, f32[16,8,256]{2,1,0:T(8,128)S(1)}, f32[4,16,8,256]{3,2,1,0:T(8,128)S(1)}...) conditional(s32[]{:T(128)} %convert_element_type.4, ...), branch_computations={%region_0.1_spmd, %region_1.2_spmd} | conditional | flops 1600000 | bytes 2009864 | solution.py:795
  2.0 0.3 %branch_0_fun.2 = (f32[4,16,8,256]{3,2,1,0:T(8,128)S(1)}, f32[4,16,8,256]{3,2,1,0:T(8,128)S(1)}, f32[16,8,256]{2,1,0:T(8,128)S(1)}, f32[5,8,256]{2,1,0:T(8,128)S(1)}) custom-call(f32[16,8,128]{2,1,0:T(8,128)S(1)} %get-tuple-element.43.conduct_a_ref, s32[8,128]{1,0:T(8,128)S(1)} %get-tuple-element.44.edge_a_ref, ...), custom_call_target="tpu_custom_call" | custom-call | flops 200000 | bytes 200000 | tf_op jit(solution)/shard_map/cond/branch_0_fun/pallas_call | solution.py:627
  2.3 5.0 %collective-permute-start = (f32[5,8,256]{2,1,0:T(8,128)S(1)}, f32[5,8,256]{2,1,0:T(8,128)S(1)}, u32[]{:S(2)}, u32[]{:S(2)}) collective-permute-start(f32[5,8,256]{2,1,0:T(8,128)S(1)} %get-tuple-element.48.refs_3_), channel_id=1, source_target_pairs={{0,3},{1,0},{2,1},{3,2},{4,7},{5,4},{6,5},{7,6},{8,11},{9,8},{10,9... | collective-permute-start | bytes 122888 | tf_op jit(solution)/shard_map/cond/branch_0_fun/ppermute | solution.py:659
  7.3 0.0 collective-permute-start.1
  7.3 1.0 %collective-permute-start.2 = (f32[5,8,256]{2,1,0:T(8,128)S(1)}, f32[5,8,256]{2,1,0:T(8,128)S(1)}, u32[]{:S(2)}, u32[]{:S(2)}) collective-permute-start(f32[5,8,256]{2,1,0:T(8,128)S(1)} %get-tuple-element.48.refs_3_), channel_id=1, source_target_pairs={{0,1},{1,2},{2,3},{3,0},{4,5},{5,6},{6,7},{7,4},{8,9},{9,10},{10,1... | collective-permute-start | bytes 122888 | tf_op jit(solution)/shard_map/cond/branch_0_fun/ppermute | solution.py:659
  8.3 0.7 %collective-permute-done.refs_0_ = f32[5,8,256]{2,1,0:T(8,128)S(1)} collective-permute-done((f32[5,8,256]{2,1,0:T(8,128)S(1)}, f32[5,8,256]{2,1,0:T(8,128)S(1)}, u32[]{:S(2)}, u32[]{:S(2)}) %collective-permute-start) | collective-permute-done | bytes 40992 | tf_op jit(solution)/shard_map/cond/branch_0_fun/ppermute | solution.py:659
  8.9 3.2 %collective-permute-done.1.refs_1_ = f32[5,8,256]{2,1,0:T(8,128)S(1)} collective-permute-done((f32[5,8,256]{2,1,0:T(8,128)S(1)}, f32[5,8,256]{2,1,0:T(8,128)S(1)}, u32[]{:S(2)}, u32[]{:S(2)}) %collective-permute-start.1) | collective-permute-done | bytes 40992 | tf_op jit(solution)/shard_map/cond/branch_0_fun/ppermute | solution.py:659
  12.2 0.9 %collective-permute-done.2.refs_2_ = f32[5,8,256]{2,1,0:T(8,128)S(1)} collective-permute-done((f32[5,8,256]{2,1,0:T(8,128)S(1)}, f32[5,8,256]{2,1,0:T(8,128)S(1)}, u32[]{:S(2)}, u32[]{:S(2)}) %collective-permute-start.2) | collective-permute-done | bytes 40992 | tf_op jit(solution)/shard_map/cond/branch_0_fun/ppermute | solution.py:659
  13.2 1.3 %collective-permute-start.14 = (f32[16,8,256]{2,1,0:T(8,128)S(1)}, f32[16,8,256]{2,1,0:T(8,128)S(1)}, u32[]{:S(2)}, u32[]{:S(2)}) collective-permute-start(f32[16,8,256]{2,1,0:T(8,128)S(1)} %get-tuple-element.138), channel_id=1, source_target_pairs={{0,8},{8,0},{16,24},{24,16},{1,9},{9,1},{17,25},{25,17},{2,10},{10... | collective-permute-start | bytes 393224 | tf_op jit(solution)/shard_map/ppermute | solution.py:666
  14.6 0.9 %collective-permute-done.14.bands_ref = f32[16,8,256]{2,1,0:T(8,128)S(1)} collective-permute-done((f32[16,8,256]{2,1,0:T(8,128)S(1)}, f32[16,8,256]{2,1,0:T(8,128)S(1)}, u32[]{:S(2)}, u32[]{:S(2)}) %collective-permute-start.14) | collective-permute-done | bytes 131104 | tf_op jit(solution)/shard_map/ppermute | solution.py:666
  15.5 0.1 shard_map.47
  15.6 4.6 %collective-permute-start.15 = (f32[16,8,128]{2,1,0:T(8,128)S(1)}, f32[16,8,128]{2,1,0:T(8,128)S(1)}, u32[]{:S(2)}, u32[]{:S(2)}) collective-permute-start(f32[16,8,128]{2,1,0:T(8,128)S(1)} %get-tuple-element.140), channel_id=1, source_target_pairs={{0,8},{8,0},{16,24},{24,16},{1,9},{9,1},{17,25},{25,17},{2,10},{10... | collective-permute-start | bytes 196616 | tf_op jit(solution)/shard_map/ppermute | solution.py:666
  20.2 0.9 %collective-permute-done.15 = f32[16,8,128]{2,1,0:T(8,128)S(1)} collective-permute-done((f32[16,8,128]{2,1,0:T(8,128)S(1)}, f32[16,8,128]{2,1,0:T(8,128)S(1)}, u32[]{:S(2)}, u32[]{:S(2)}) %collective-permute-start.15) | collective-permute-done | bytes 65568 | tf_op jit(solution)/shard_map/ppermute | solution.py:666
  21.1 0.6 %broadcast_select_fusion = f32[16,8,128]{2,1,0:T(8,128)} fusion(f32[16,8,128]{2,1,0:T(8,128)S(1)} %get-tuple-element.139, f32[16,8,128]{2,1,0:T(8,128)S(1)} %collective-permute-done.15, pred[]{:T(512)S(6)} %eq.5), kind=kLoop, calls=%fused_computation | loop fusion | flops 16384 | bytes 196609 | tf_op jit(solution)/shard_map/jit(_where)/select_n | solution.py:807
  (8 shorter events, 0.2 us)
Async XLA Ops:
  0.0 2.0 %collective-permute-start.11 = (s32[16,8,128]{2,1,0:T(8,128)}, s32[16,8,128]{2,1,0:T(8,128)S(1)}, u32[]{:S(2)}, u32[]{:S(2)}) collective-permute-start(s32[16,8,128]{2,1,0:T(8,128)} %label_in.1), channel_id=1, source_target_pairs={{0,8},{8,0},{16,24},{24,16},{1,9},{9,1},{17,25},{25,17},{2,10},{10... | collective-permute-start | bytes 196616 | tf_op jit(solution)/shard_map/ppermute | solution.py:666
  0.5 1.6 %collective-permute-start.13 = (f32[16,8,128]{2,1,0:T(8,128)}, f32[16,8,128]{2,1,0:T(8,128)S(1)}, u32[]{:S(2)}, u32[]{:S(2)}) collective-permute-start(f32[16,8,128]{2,1,0:T(8,128)} %heat_in.1), channel_id=1, source_target_pairs={{0,8},{8,0},{16,24},{24,16},{1,9},{9,1},{17,25},{25,17},{2,10},{10... | collective-permute-start | bytes 196616 | tf_op jit(solution)/shard_map/ppermute | solution.py:666
  0.5 1.5 %collective-permute-start.12 = (s32[8,128]{1,0:T(8,128)}, s32[8,128]{1,0:T(8,128)S(1)}, u32[]{:S(2)}, u32[]{:S(2)}) collective-permute-start(s32[8,128]{1,0:T(8,128)} %edge_in.1), channel_id=1, source_target_pairs={{0,8},{8,0},{16,24},{24,16},{1,9},{9,1},{17,25},{25,17},{2,10},{10... | collective-permute-start | bytes 12296 | tf_op jit(solution)/shard_map/ppermute | solution.py:666
  2.3 6.7 %collective-permute-start = (f32[5,8,256]{2,1,0:T(8,128)S(1)}, f32[5,8,256]{2,1,0:T(8,128)S(1)}, u32[]{:S(2)}, u32[]{:S(2)}) collective-permute-start(f32[5,8,256]{2,1,0:T(8,128)S(1)} %get-tuple-element.48.refs_3_), channel_id=1, source_target_pairs={{0,3},{1,0},{2,1},{3,2},{4,7},{5,4},{6,5},{7,6},{8,11},{9,8},{10,9... | collective-permute-start | bytes 122888 | tf_op jit(solution)/shard_map/cond/branch_0_fun/ppermute | solution.py:659
  7.3 4.9 %collective-permute-start.1 = (f32[5,8,256]{2,1,0:T(8,128)S(1)}, f32[5,8,256]{2,1,0:T(8,128)S(1)}, u32[]{:S(2)}, u32[]{:S(2)}) collective-permute-start(f32[5,8,256]{2,1,0:T(8,128)S(1)} %get-tuple-element.48.refs_3_), channel_id=1, source_target_pairs={{0,2},{1,3},{2,0},{3,1},{4,6},{5,7},{6,4},{7,5},{8,10},{9,11},{10,... | collective-permute-start | bytes 122888 | tf_op jit(solution)/shard_map/cond/branch_0_fun/ppermute | solution.py:659
  7.3 5.8 %collective-permute-start.2 = (f32[5,8,256]{2,1,0:T(8,128)S(1)}, f32[5,8,256]{2,1,0:T(8,128)S(1)}, u32[]{:S(2)}, u32[]{:S(2)}) collective-permute-start(f32[5,8,256]{2,1,0:T(8,128)S(1)} %get-tuple-element.48.refs_3_), channel_id=1, source_target_pairs={{0,1},{1,2},{2,3},{3,0},{4,5},{5,6},{6,7},{7,4},{8,9},{9,10},{10,1... | collective-permute-start | bytes 122888 | tf_op jit(solution)/shard_map/cond/branch_0_fun/ppermute | solution.py:659
  13.2 2.3 %collective-permute-start.14 = (f32[16,8,256]{2,1,0:T(8,128)S(1)}, f32[16,8,256]{2,1,0:T(8,128)S(1)}, u32[]{:S(2)}, u32[]{:S(2)}) collective-permute-start(f32[16,8,256]{2,1,0:T(8,128)S(1)} %get-tuple-element.138), channel_id=1, source_target_pairs={{0,8},{8,0},{16,24},{24,16},{1,9},{9,1},{17,25},{25,17},{2,10},{10... | collective-permute-start | bytes 393224 | tf_op jit(solution)/shard_map/ppermute | solution.py:666
  15.6 5.5 %collective-permute-start.15 = (f32[16,8,128]{2,1,0:T(8,128)S(1)}, f32[16,8,128]{2,1,0:T(8,128)S(1)}, u32[]{:S(2)}, u32[]{:S(2)}) collective-permute-start(f32[16,8,128]{2,1,0:T(8,128)S(1)} %get-tuple-element.140), channel_id=1, source_target_pairs={{0,8},{8,0},{16,24},{24,16},{1,9},{9,1},{17,25},{25,17},{2,10},{10... | collective-permute-start | bytes 196616 | tf_op jit(solution)/shard_map/ppermute | solution.py:666

commit v11 on v10

--- a/solution.py
+++ b/solution.py
@@ -604,7 +604,7 @@
 
 
 def all_bands_kernel(*refs):
-    messages, (bands_ref, blocks_ref) = refs[:-2][::-1], refs[-2:]
+    messages, (bands_ref, blocks_ref) = starting_order(refs[:-2], True), refs[-2:]
     count, index = len(messages), lax.axis_index("gz")
     for shift, message in enumerate(messages):
         blocks_ref[lax.rem(index - shift + count, count)] = message[...]
@@ -753,7 +753,7 @@
     (bands,) = call(
         all_bands_kernel,
         [(bands_rows(count_z, nz), *layer)],
-        swap_all("gz", message)[::-1],
+        starting_order(swap_all("gz", message)),
         [(count_z, 5, *layer)],
     )
     zeros = lambda *shape: jnp.zeros(shape, F32)

time: 21.9 us -> 21.7 us (level)
  starting transfers between devices: 12.9 us -> 12.4 us
  waiting for transfers between devices: 6.71 us -> 7.04 us
    ppermute x5, starting transfers between devices: 6.88 us -> 6.41 us  [other_core(): return lax.ppermute(values, 'gx', [(i, i ^ 1) for i in range(count)])]
    ppermute x3, waiting for transfers between devices: 4.79 us -> 5.12 us  [swap_all(): lax.ppermute(message, name, [(i, (i + shift) % count) for i in range(coun...]
  transfers between devices with their start and end apart: 8 -> 8, of which waited for: 6 -> 5; matrix products, arithmetic and copies ran while one was open for 0% -> 0% of each run, Pallas kernels for 4% -> 4%
where the time goes in v11:
time: 21.7 us; the launch traced here: 21.6 us
  starting transfers between devices  12.4 us (57%)
  waiting for transfers between devices  7.04 us (32%)
  Pallas kernels  1.31 us (6%)
  other arithmetic  0.64 us (3%)
    ppermute x5, starting transfers between devices, other_core(): return lax.ppermute(values, 'gx', [(i, i ^ 1) for i in range(count)])  6.41 us
    ppermute x3, starting transfers between devices, swap_all(): lax.ppermute(message, name, [(i, (i + shift) % count) for i in range(coun...  6.02 us
    ppermute x3, waiting for transfers between devices, swap_all(): lax.ppermute(message, name, [(i, (i + shift) % count) for i in range(coun...  5.12 us
    ppermute x5, waiting for transfers between devices, other_core(): return lax.ppermute(values, 'gx', [(i, i ^ 1) for i in range(count)])  1.92 us
    pallas_call x4, Pallas kernels, call(): pl.pallas_call(kernel, out_shape=[jax.ShapeDtypeStruct(out, F32) if isins...  1.31 us
    select_n x1, other arithmetic, local(): return jnp.where(second, mine, other_core(theirs))  0.64 us
  transfers between devices with their start and end apart: 8, of which 5 were waited for; matrix products, arithmetic and copies ran while one was open for 0% of the time, Pallas kernels for 4%

profile of v11, /device:TPU:0, one launch (start us, length us, event | category | flops | bytes accessed | tf_op | source)
XLA Modules:
  0.0 21.6 jit_solution(14231460469722052772)
XLA Ops:
  0.0 0.5 %collective-permute-start.11 = (s32[16,8,128]{2,1,0:T(8,128)}, s32[16,8,128]{2,1,0:T(8,128)S(1)}, u32[]{:S(2)}, u32[]{:S(2)}) collective-permute-start(s32[16,8,128]{2,1,0:T(8,128)} %label_in.1), channel_id=1, source_target_pairs={{0,8},{8,0},{16,24},{24,16},{1,9},{9,1},{17,25},{25,17},{2,10},{10... | collective-permute-start | bytes 196616 | tf_op jit(solution)/shard_map/ppermute | solution.py:666
  0.5 0.1 collective-permute-start.13
  0.5 0.5 %collective-permute-start.12 = (s32[8,128]{1,0:T(8,128)}, s32[8,128]{1,0:T(8,128)S(1)}, u32[]{:S(2)}, u32[]{:S(2)}) collective-permute-start(s32[8,128]{1,0:T(8,128)} %edge_in.1), channel_id=1, source_target_pairs={{0,8},{8,0},{16,24},{24,16},{1,9},{9,1},{17,25},{25,17},{2,10},{10... | collective-permute-start | bytes 12296 | tf_op jit(solution)/shard_map/ppermute | solution.py:666
  1.0 0.9 %shard_map.46 = (f32[16,8,128]{2,1,0:T(8,128)S(1)}, f32[16,8,128]{2,1,0:T(8,128)S(1)}, f32[13,8,128]{2,1,0:T(8,128)S(1)}, s32[8,128]{1,0:T(8,128)S(1)}) custom-call(f32[16,8,128]{2,1,0:T(8,128)} %heat_in.1, s32[16,8,128]{2,1,0:T(8,128)} %label_in.1, f32[13]{0:T(128)} %table_in.1, s32[8,128]{1,0:T(8,128)} %edge_in.1), custom_call_target="tpu_custom_call" | custom-call | flops 200000 | bytes 200000 | tf_op jit(solution)/shard_map/pallas_call | solution.py:627
  1.9 0.1 collective-permute-done.12
  2.0 0.0 collective-permute-done.11
  2.0 0.0 collective-permute-done.13
  2.0 11.5 %conditional.2 = (f32[16,8,256]{2,1,0:T(8,128)S(1)}, f32[16,8,256]{2,1,0:T(8,128)S(1)}, f32[16,8,256]{2,1,0:T(8,128)S(1)}, f32[4,16,8,256]{3,2,1,0:T(8,128)S(1)}...) conditional(s32[]{:T(128)} %convert_element_type.4, ...), branch_computations={%region_0.1_spmd, %region_1.2_spmd} | conditional | flops 1600000 | bytes 2009864 | solution.py:795
  2.0 0.3 %branch_0_fun.2 = (f32[4,16,8,256]{3,2,1,0:T(8,128)S(1)}, f32[4,16,8,256]{3,2,1,0:T(8,128)S(1)}, f32[16,8,256]{2,1,0:T(8,128)S(1)}, f32[5,8,256]{2,1,0:T(8,128)S(1)}) custom-call(f32[16,8,128]{2,1,0:T(8,128)S(1)} %get-tuple-element.43.conduct_a_ref, s32[8,128]{1,0:T(8,128)S(1)} %get-tuple-element.44.edge_a_ref, ...), custom_call_target="tpu_custom_call" | custom-call | flops 200000 | bytes 200000 | tf_op jit(solution)/shard_map/cond/branch_0_fun/pallas_call | solution.py:627
  2.3 4.0 %collective-permute-start = (f32[5,8,256]{2,1,0:T(8,128)S(1)}, f32[5,8,256]{2,1,0:T(8,128)S(1)}, u32[]{:S(2)}, u32[]{:S(2)}) collective-permute-start(f32[5,8,256]{2,1,0:T(8,128)S(1)} %get-tuple-element.48.refs_0_), channel_id=1, source_target_pairs={{0,2},{1,3},{2,0},{3,1},{4,6},{5,7},{6,4},{7,5},{8,10},{9,11},{10,... | collective-permute-start | bytes 122888 | tf_op jit(solution)/shard_map/cond/branch_0_fun/ppermute | solution.py:659
  6.3 1.3 %collective-permute-start.1 = (f32[5,8,256]{2,1,0:T(8,128)S(1)}, f32[5,8,256]{2,1,0:T(8,128)S(1)}, u32[]{:S(2)}, u32[]{:S(2)}) collective-permute-start(f32[5,8,256]{2,1,0:T(8,128)S(1)} %get-tuple-element.48.refs_0_), channel_id=1, source_target_pairs={{0,3},{1,0},{2,1},{3,2},{4,7},{5,4},{6,5},{7,6},{8,11},{9,8},{10,9... | collective-permute-start | bytes 122888 | tf_op jit(solution)/shard_map/cond/branch_0_fun/ppermute | solution.py:659
  7.6 0.7 %collective-permute-start.2 = (f32[5,8,256]{2,1,0:T(8,128)S(1)}, f32[5,8,256]{2,1,0:T(8,128)S(1)}, u32[]{:S(2)}, u32[]{:S(2)}) collective-permute-start(f32[5,8,256]{2,1,0:T(8,128)S(1)} %get-tuple-element.48.refs_0_), channel_id=1, source_target_pairs={{0,1},{1,2},{2,3},{3,0},{4,5},{5,6},{6,7},{7,4},{8,9},{9,10},{10,1... | collective-permute-start | bytes 122888 | tf_op jit(solution)/shard_map/cond/branch_0_fun/ppermute | solution.py:659
  8.3 0.0 collective-permute-done.refs_1_
  8.3 2.0 %collective-permute-done.1.refs_2_ = f32[5,8,256]{2,1,0:T(8,128)S(1)} collective-permute-done((f32[5,8,256]{2,1,0:T(8,128)S(1)}, f32[5,8,256]{2,1,0:T(8,128)S(1)}, u32[]{:S(2)}, u32[]{:S(2)}) %collective-permute-start.1) | collective-permute-done | bytes 40992 | tf_op jit(solution)/shard_map/cond/branch_0_fun/ppermute | solution.py:659
  10.3 3.1 %collective-permute-done.2.refs_3_ = f32[5,8,256]{2,1,0:T(8,128)S(1)} collective-permute-done((f32[5,8,256]{2,1,0:T(8,128)S(1)}, f32[5,8,256]{2,1,0:T(8,128)S(1)}, u32[]{:S(2)}, u32[]{:S(2)}) %collective-permute-start.2) | collective-permute-done | bytes 40992 | tf_op jit(solution)/shard_map/cond/branch_0_fun/ppermute | solution.py:659
  13.5 1.0 %collective-permute-start.14 = (f32[16,8,256]{2,1,0:T(8,128)S(1)}, f32[16,8,256]{2,1,0:T(8,128)S(1)}, u32[]{:S(2)}, u32[]{:S(2)}) collective-permute-start(f32[16,8,256]{2,1,0:T(8,128)S(1)} %get-tuple-element.138), channel_id=1, source_target_pairs={{0,8},{8,0},{16,24},{24,16},{1,9},{9,1},{17,25},{25,17},{2,10},{10... | collective-permute-start | bytes 393224 | tf_op jit(solution)/shard_map/ppermute | solution.py:666
  14.6 0.9 %collective-permute-done.14.bands_ref = f32[16,8,256]{2,1,0:T(8,128)S(1)} collective-permute-done((f32[16,8,256]{2,1,0:T(8,128)S(1)}, f32[16,8,256]{2,1,0:T(8,128)S(1)}, u32[]{:S(2)}, u32[]{:S(2)}) %collective-permute-start.14) | collective-permute-done | bytes 131104 | tf_op jit(solution)/shard_map/ppermute | solution.py:666
  15.5 0.1 shard_map.47
  15.6 4.5 %collective-permute-start.15 = (f32[16,8,128]{2,1,0:T(8,128)S(1)}, f32[16,8,128]{2,1,0:T(8,128)S(1)}, u32[]{:S(2)}, u32[]{:S(2)}) collective-permute-start(f32[16,8,128]{2,1,0:T(8,128)S(1)} %get-tuple-element.140), channel_id=1, source_target_pairs={{0,8},{8,0},{16,24},{24,16},{1,9},{9,1},{17,25},{25,17},{2,10},{10... | collective-permute-start | bytes 196616 | tf_op jit(solution)/shard_map/ppermute | solution.py:666
  20.1 0.9 %collective-permute-done.15 = f32[16,8,128]{2,1,0:T(8,128)S(1)} collective-permute-done((f32[16,8,128]{2,1,0:T(8,128)S(1)}, f32[16,8,128]{2,1,0:T(8,128)S(1)}, u32[]{:S(2)}, u32[]{:S(2)}) %collective-permute-start.15) | collective-permute-done | bytes 65568 | tf_op jit(solution)/shard_map/ppermute | solution.py:666
  21.0 0.6 %broadcast_select_fusion = f32[16,8,128]{2,1,0:T(8,128)} fusion(f32[16,8,128]{2,1,0:T(8,128)S(1)} %get-tuple-element.139, f32[16,8,128]{2,1,0:T(8,128)S(1)} %collective-permute-done.15, pred[]{:T(512)S(6)} %eq.5), kind=kLoop, calls=%fused_computation | loop fusion | flops 16384 | bytes 196609 | tf_op jit(solution)/shard_map/jit(_where)/select_n | solution.py:807
  (8 shorter events, 0.2 us)
Async XLA Ops:
  0.0 2.0 %collective-permute-start.11 = (s32[16,8,128]{2,1,0:T(8,128)}, s32[16,8,128]{2,1,0:T(8,128)S(1)}, u32[]{:S(2)}, u32[]{:S(2)}) collective-permute-start(s32[16,8,128]{2,1,0:T(8,128)} %label_in.1), channel_id=1, source_target_pairs={{0,8},{8,0},{16,24},{24,16},{1,9},{9,1},{17,25},{25,17},{2,10},{10... | collective-permute-start | bytes 196616 | tf_op jit(solution)/shard_map/ppermute | solution.py:666
  0.5 1.6 %collective-permute-start.13 = (f32[16,8,128]{2,1,0:T(8,128)}, f32[16,8,128]{2,1,0:T(8,128)S(1)}, u32[]{:S(2)}, u32[]{:S(2)}) collective-permute-start(f32[16,8,128]{2,1,0:T(8,128)} %heat_in.1), channel_id=1, source_target_pairs={{0,8},{8,0},{16,24},{24,16},{1,9},{9,1},{17,25},{25,17},{2,10},{10... | collective-permute-start | bytes 196616 | tf_op jit(solution)/shard_map/ppermute | solution.py:666
  0.5 1.5 %collective-permute-start.12 = (s32[8,128]{1,0:T(8,128)}, s32[8,128]{1,0:T(8,128)S(1)}, u32[]{:S(2)}, u32[]{:S(2)}) collective-permute-start(s32[8,128]{1,0:T(8,128)} %edge_in.1), channel_id=1, source_target_pairs={{0,8},{8,0},{16,24},{24,16},{1,9},{9,1},{17,25},{25,17},{2,10},{10... | collective-permute-start | bytes 12296 | tf_op jit(solution)/shard_map/ppermute | solution.py:666
  2.3 6.0 %collective-permute-start = (f32[5,8,256]{2,1,0:T(8,128)S(1)}, f32[5,8,256]{2,1,0:T(8,128)S(1)}, u32[]{:S(2)}, u32[]{:S(2)}) collective-permute-start(f32[5,8,256]{2,1,0:T(8,128)S(1)} %get-tuple-element.48.refs_0_), channel_id=1, source_target_pairs={{0,2},{1,3},{2,0},{3,1},{4,6},{5,7},{6,4},{7,5},{8,10},{9,11},{10,... | collective-permute-start | bytes 122888 | tf_op jit(solution)/shard_map/cond/branch_0_fun/ppermute | solution.py:659
  6.3 4.0 %collective-permute-start.1 = (f32[5,8,256]{2,1,0:T(8,128)S(1)}, f32[5,8,256]{2,1,0:T(8,128)S(1)}, u32[]{:S(2)}, u32[]{:S(2)}) collective-permute-start(f32[5,8,256]{2,1,0:T(8,128)S(1)} %get-tuple-element.48.refs_0_), channel_id=1, source_target_pairs={{0,3},{1,0},{2,1},{3,2},{4,7},{5,4},{6,5},{7,6},{8,11},{9,8},{10,9... | collective-permute-start | bytes 122888 | tf_op jit(solution)/shard_map/cond/branch_0_fun/ppermute | solution.py:659
  7.6 5.8 %collective-permute-start.2 = (f32[5,8,256]{2,1,0:T(8,128)S(1)}, f32[5,8,256]{2,1,0:T(8,128)S(1)}, u32[]{:S(2)}, u32[]{:S(2)}) collective-permute-start(f32[5,8,256]{2,1,0:T(8,128)S(1)} %get-tuple-element.48.refs_0_), channel_id=1, source_target_pairs={{0,1},{1,2},{2,3},{3,0},{4,5},{5,6},{6,7},{7,4},{8,9},{9,10},{10,1... | collective-permute-start | bytes 122888 | tf_op jit(solution)/shard_map/cond/branch_0_fun/ppermute | solution.py:659
  13.5 1.9 %collective-permute-start.14 = (f32[16,8,256]{2,1,0:T(8,128)S(1)}, f32[16,8,256]{2,1,0:T(8,128)S(1)}, u32[]{:S(2)}, u32[]{:S(2)}) collective-permute-start(f32[16,8,256]{2,1,0:T(8,128)S(1)} %get-tuple-element.138), channel_id=1, source_target_pairs={{0,8},{8,0},{16,24},{24,16},{1,9},{9,1},{17,25},{25,17},{2,10},{10... | collective-permute-start | bytes 393224 | tf_op jit(solution)/shard_map/ppermute | solution.py:666
  15.6 5.4 %collective-permute-start.15 = (f32[16,8,128]{2,1,0:T(8,128)S(1)}, f32[16,8,128]{2,1,0:T(8,128)S(1)}, u32[]{:S(2)}, u32[]{:S(2)}) collective-permute-start(f32[16,8,128]{2,1,0:T(8,128)S(1)} %get-tuple-element.140), channel_id=1, source_target_pairs={{0,8},{8,0},{16,24},{24,16},{1,9},{9,1},{17,25},{25,17},{2,10},{10... | collective-permute-start | bytes 196616 | tf_op jit(solution)/shard_map/ppermute | solution.py:666

commit v12 on v11

--- a/solution.py
+++ b/solution.py
@@ -566,7 +566,15 @@
         tail_ref[pl.ds(place, 2)] = message[...]
 
 
-def finish_kernel(ready_ref, tail_ref, bands_ref, theirs_ref, mine_ref, state_ref):
+def mine_kernel(ready_ref, ends_ref, mine_ref):
+    nx = mine_ref.shape[-1]
+    first, last = ends_ref[0, :, nx:], ends_ref[1, :, nx:]
+    mine_ref[...] = (
+        ready_ref[0, :, :, nx:] + ready_ref[1, :, :, nx:] * first + ready_ref[2, :, :, nx:] * last
+    )
+
+
+def finish_kernel(ready_ref, tail_ref, bands_ref, theirs_ref, ends_ref, state_ref):
     count, index = (tail_ref.shape[0] - 4) // 2, lax.axis_index("gz")
     blocks = [
         (bands_ref[3 * k], bands_ref[3 * k + 1], tail_ref[4 + 2 * k], bands_ref[3 * k + 2],
@@ -577,8 +585,11 @@
     outer, between, inverse, source_first = (tail_ref[i] for i in range(4))
     first = (source_first + outer * below + between * last) * inverse
     nx = theirs_ref.shape[-1]
-    heated = ready_ref[0] + ready_ref[1] * first + ready_ref[2] * last
-    theirs_ref[...], mine_ref[...] = heated[:, :, :nx], heated[:, :, nx:]
+    ends_ref[0], ends_ref[1] = first, last
+    first, last = first[:, :nx], last[:, :nx]
+    theirs_ref[...] = (
+        ready_ref[0, :, :, :nx] + ready_ref[1, :, :, :nx] * first + ready_ref[2, :, :, :nx] * last
+    )
 
 
 def ends_kernel(
@@ -798,13 +809,15 @@
     )
     bands = other_core(state[1])
     ready, tail = lax.cond(second, z_round, z_idle, *state)
-    theirs, mine = call(
+    theirs, ends = call(
         finish_kernel,
-        [heat_a.shape] * 2,
+        [heat_a.shape, (2, *tail.shape[1:])],
         [ready, tail, bands],
         [(5, lax.axis_size("gz"), *tail.shape[1:])],
     )
-    return jnp.where(second, mine, other_core(theirs))
+    received = other_core(theirs)
+    (mine,) = call(mine_kernel, [heat_a.shape], [ready, ends])
+    return jnp.where(second, mine, received)
 
 
 def solution(mesh):

time: 21.7 us -> 21.7 us (level)
    pallas_call x4 -> x5, Pallas kernels: 1.31 us -> 1.32 us  [call(): pl.pallas_call(kernel, out_shape=[jax.ShapeDtypeStruct(out, F32) if isins...]
where the time goes in v12:
time: 21.7 us; the launch traced here: 21.6 us
  starting transfers between devices  12.4 us (57%)
  waiting for transfers between devices  7.02 us (32%)
  Pallas kernels  1.32 us (6%)
  other arithmetic  0.64 us (3%)
    ppermute x5, starting transfers between devices, other_core(): return lax.ppermute(values, 'gx', [(i, i ^ 1) for i in range(count)])  6.41 us
    ppermute x3, starting transfers between devices, swap_all(): lax.ppermute(message, name, [(i, (i + shift) % count) for i in range(coun...  6.02 us
    ppermute x3, waiting for transfers between devices, swap_all(): lax.ppermute(message, name, [(i, (i + shift) % count) for i in range(coun...  5.12 us
    ppermute x5, waiting for transfers between devices, other_core(): return lax.ppermute(values, 'gx', [(i, i ^ 1) for i in range(count)])  1.9 us
    pallas_call x5, Pallas kernels, call(): pl.pallas_call(kernel, out_shape=[jax.ShapeDtypeStruct(out, F32) if isins...  1.32 us
    select_n x1, other arithmetic, local(): return jnp.where(second, mine, received)  0.64 us
  transfers between devices with their start and end apart: 8, of which 5 were waited for; matrix products, arithmetic and copies ran while one was open for 0% of the time, Pallas kernels for 4%

profile of v12, /device:TPU:0, one launch (start us, length us, event | category | flops | bytes accessed | tf_op | source)
XLA Modules:
  0.0 21.6 jit_solution(6184605753097011435)
XLA Ops:
  0.0 0.5 %collective-permute-start.11 = (s32[16,8,128]{2,1,0:T(8,128)}, s32[16,8,128]{2,1,0:T(8,128)S(1)}, u32[]{:S(2)}, u32[]{:S(2)}) collective-permute-start(s32[16,8,128]{2,1,0:T(8,128)} %label_in.1), channel_id=1, source_target_pairs={{0,8},{8,0},{16,24},{24,16},{1,9},{9,1},{17,25},{25,17},{2,10},{10... | collective-permute-start | bytes 196616 | tf_op jit(solution)/shard_map/ppermute | solution.py:677
  0.5 0.1 collective-permute-start.13
  0.5 0.5 %collective-permute-start.12 = (s32[8,128]{1,0:T(8,128)}, s32[8,128]{1,0:T(8,128)S(1)}, u32[]{:S(2)}, u32[]{:S(2)}) collective-permute-start(s32[8,128]{1,0:T(8,128)} %edge_in.1), channel_id=1, source_target_pairs={{0,8},{8,0},{16,24},{24,16},{1,9},{9,1},{17,25},{25,17},{2,10},{10... | collective-permute-start | bytes 12296 | tf_op jit(solution)/shard_map/ppermute | solution.py:677
  1.0 0.9 %shard_map.46 = (f32[16,8,128]{2,1,0:T(8,128)S(1)}, f32[16,8,128]{2,1,0:T(8,128)S(1)}, f32[13,8,128]{2,1,0:T(8,128)S(1)}, s32[8,128]{1,0:T(8,128)S(1)}) custom-call(f32[16,8,128]{2,1,0:T(8,128)} %heat_in.1, s32[16,8,128]{2,1,0:T(8,128)} %label_in.1, f32[13]{0:T(128)} %table_in.1, s32[8,128]{1,0:T(8,128)} %edge_in.1), custom_call_target="tpu_custom_call" | custom-call | flops 200000 | bytes 200000 | tf_op jit(solution)/shard_map/pallas_call | solution.py:638
  1.9 0.1 collective-permute-done.12
  2.0 0.0 collective-permute-done.11
  2.0 0.0 collective-permute-done.13
  2.0 11.5 %conditional.2 = (f32[16,8,256]{2,1,0:T(8,128)S(1)}, f32[16,8,256]{2,1,0:T(8,128)S(1)}, f32[16,8,256]{2,1,0:T(8,128)S(1)}, f32[4,16,8,256]{3,2,1,0:T(8,128)S(1)}...) conditional(s32[]{:T(128)} %convert_element_type.4, ...), branch_computations={%region_0.1_spmd, %region_1.2_spmd} | conditional | flops 1600000 | bytes 2009864 | solution.py:806
  2.0 0.3 %branch_0_fun.2 = (f32[4,16,8,256]{3,2,1,0:T(8,128)S(1)}, f32[4,16,8,256]{3,2,1,0:T(8,128)S(1)}, f32[16,8,256]{2,1,0:T(8,128)S(1)}, f32[5,8,256]{2,1,0:T(8,128)S(1)}) custom-call(f32[16,8,128]{2,1,0:T(8,128)S(1)} %get-tuple-element.43.conduct_a_ref, s32[8,128]{1,0:T(8,128)S(1)} %get-tuple-element.44.edge_a_ref, ...), custom_call_target="tpu_custom_call" | custom-call | flops 200000 | bytes 200000 | tf_op jit(solution)/shard_map/cond/branch_0_fun/pallas_call | solution.py:638
  2.3 4.0 %collective-permute-start = (f32[5,8,256]{2,1,0:T(8,128)S(1)}, f32[5,8,256]{2,1,0:T(8,128)S(1)}, u32[]{:S(2)}, u32[]{:S(2)}) collective-permute-start(f32[5,8,256]{2,1,0:T(8,128)S(1)} %get-tuple-element.48.refs_0_), channel_id=1, source_target_pairs={{0,2},{1,3},{2,0},{3,1},{4,6},{5,7},{6,4},{7,5},{8,10},{9,11},{10,... | collective-permute-start | bytes 122888 | tf_op jit(solution)/shard_map/cond/branch_0_fun/ppermute | solution.py:670
  6.3 1.3 %collective-permute-start.1 = (f32[5,8,256]{2,1,0:T(8,128)S(1)}, f32[5,8,256]{2,1,0:T(8,128)S(1)}, u32[]{:S(2)}, u32[]{:S(2)}) collective-permute-start(f32[5,8,256]{2,1,0:T(8,128)S(1)} %get-tuple-element.48.refs_0_), channel_id=1, source_target_pairs={{0,3},{1,0},{2,1},{3,2},{4,7},{5,4},{6,5},{7,6},{8,11},{9,8},{10,9... | collective-permute-start | bytes 122888 | tf_op jit(solution)/shard_map/cond/branch_0_fun/ppermute | solution.py:670
  7.6 0.7 %collective-permute-start.2 = (f32[5,8,256]{2,1,0:T(8,128)S(1)}, f32[5,8,256]{2,1,0:T(8,128)S(1)}, u32[]{:S(2)}, u32[]{:S(2)}) collective-permute-start(f32[5,8,256]{2,1,0:T(8,128)S(1)} %get-tuple-element.48.refs_0_), channel_id=1, source_target_pairs={{0,1},{1,2},{2,3},{3,0},{4,5},{5,6},{6,7},{7,4},{8,9},{9,10},{10,1... | collective-permute-start | bytes 122888 | tf_op jit(solution)/shard_map/cond/branch_0_fun/ppermute | solution.py:670
  8.3 0.0 collective-permute-done.refs_1_
  8.3 2.0 %collective-permute-done.1.refs_2_ = f32[5,8,256]{2,1,0:T(8,128)S(1)} collective-permute-done((f32[5,8,256]{2,1,0:T(8,128)S(1)}, f32[5,8,256]{2,1,0:T(8,128)S(1)}, u32[]{:S(2)}, u32[]{:S(2)}) %collective-permute-start.1) | collective-permute-done | bytes 40992 | tf_op jit(solution)/shard_map/cond/branch_0_fun/ppermute | solution.py:670
  10.3 3.1 %collective-permute-done.2.refs_3_ = f32[5,8,256]{2,1,0:T(8,128)S(1)} collective-permute-done((f32[5,8,256]{2,1,0:T(8,128)S(1)}, f32[5,8,256]{2,1,0:T(8,128)S(1)}, u32[]{:S(2)}, u32[]{:S(2)}) %collective-permute-start.2) | collective-permute-done | bytes 40992 | tf_op jit(solution)/shard_map/cond/branch_0_fun/ppermute | solution.py:670
  13.5 1.0 %collective-permute-start.14 = (f32[16,8,256]{2,1,0:T(8,128)S(1)}, f32[16,8,256]{2,1,0:T(8,128)S(1)}, u32[]{:S(2)}, u32[]{:S(2)}) collective-permute-start(f32[16,8,256]{2,1,0:T(8,128)S(1)} %get-tuple-element.138), channel_id=1, source_target_pairs={{0,8},{8,0},{16,24},{24,16},{1,9},{9,1},{17,25},{25,17},{2,10},{10... | collective-permute-start | bytes 393224 | tf_op jit(solution)/shard_map/ppermute | solution.py:677
  14.6 0.9 %collective-permute-done.14.bands_ref = f32[16,8,256]{2,1,0:T(8,128)S(1)} collective-permute-done((f32[16,8,256]{2,1,0:T(8,128)S(1)}, f32[16,8,256]{2,1,0:T(8,128)S(1)}, u32[]{:S(2)}, u32[]{:S(2)}) %collective-permute-start.14) | collective-permute-done | bytes 131104 | tf_op jit(solution)/shard_map/ppermute | solution.py:677
  15.5 0.1 shard_map.47
  15.6 4.5 %collective-permute-start.15 = (f32[16,8,128]{2,1,0:T(8,128)S(1)}, f32[16,8,128]{2,1,0:T(8,128)S(1)}, u32[]{:S(2)}, u32[]{:S(2)}) collective-permute-start(f32[16,8,128]{2,1,0:T(8,128)S(1)} %get-tuple-element.140), channel_id=1, source_target_pairs={{0,8},{8,0},{16,24},{24,16},{1,9},{9,1},{17,25},{25,17},{2,10},{10... | collective-permute-start | bytes 196616 | tf_op jit(solution)/shard_map/ppermute | solution.py:677
  20.1 0.9 %collective-permute-done.15 = f32[16,8,128]{2,1,0:T(8,128)S(1)} collective-permute-done((f32[16,8,128]{2,1,0:T(8,128)S(1)}, f32[16,8,128]{2,1,0:T(8,128)S(1)}, u32[]{:S(2)}, u32[]{:S(2)}) %collective-permute-start.15) | collective-permute-done | bytes 65568 | tf_op jit(solution)/shard_map/ppermute | solution.py:677
  20.9 0.6 %broadcast_select_fusion = f32[16,8,128]{2,1,0:T(8,128)} fusion(f32[16,8,128]{2,1,0:T(8,128)S(1)} %shard_map.48, f32[16,8,128]{2,1,0:T(8,128)S(1)} %collective-permute-done.15, pred[]{:T(512)S(6)} %eq.5), kind=kLoop, calls=%fused_computation | loop fusion | flops 16384 | bytes 196609 | tf_op jit(solution)/shard_map/jit(_where)/select_n | solution.py:820
  (9 shorter events, 0.2 us)
Async XLA Ops:
  0.0 2.0 %collective-permute-start.11 = (s32[16,8,128]{2,1,0:T(8,128)}, s32[16,8,128]{2,1,0:T(8,128)S(1)}, u32[]{:S(2)}, u32[]{:S(2)}) collective-permute-start(s32[16,8,128]{2,1,0:T(8,128)} %label_in.1), channel_id=1, source_target_pairs={{0,8},{8,0},{16,24},{24,16},{1,9},{9,1},{17,25},{25,17},{2,10},{10... | collective-permute-start | bytes 196616 | tf_op jit(solution)/shard_map/ppermute | solution.py:677
  0.5 1.6 %collective-permute-start.13 = (f32[16,8,128]{2,1,0:T(8,128)}, f32[16,8,128]{2,1,0:T(8,128)S(1)}, u32[]{:S(2)}, u32[]{:S(2)}) collective-permute-start(f32[16,8,128]{2,1,0:T(8,128)} %heat_in.1), channel_id=1, source_target_pairs={{0,8},{8,0},{16,24},{24,16},{1,9},{9,1},{17,25},{25,17},{2,10},{10... | collective-permute-start | bytes 196616 | tf_op jit(solution)/shard_map/ppermute | solution.py:677
  0.5 1.5 %collective-permute-start.12 = (s32[8,128]{1,0:T(8,128)}, s32[8,128]{1,0:T(8,128)S(1)}, u32[]{:S(2)}, u32[]{:S(2)}) collective-permute-start(s32[8,128]{1,0:T(8,128)} %edge_in.1), channel_id=1, source_target_pairs={{0,8},{8,0},{16,24},{24,16},{1,9},{9,1},{17,25},{25,17},{2,10},{10... | collective-permute-start | bytes 12296 | tf_op jit(solution)/shard_map/ppermute | solution.py:677
  2.3 6.0 %collective-permute-start = (f32[5,8,256]{2,1,0:T(8,128)S(1)}, f32[5,8,256]{2,1,0:T(8,128)S(1)}, u32[]{:S(2)}, u32[]{:S(2)}) collective-permute-start(f32[5,8,256]{2,1,0:T(8,128)S(1)} %get-tuple-element.48.refs_0_), channel_id=1, source_target_pairs={{0,2},{1,3},{2,0},{3,1},{4,6},{5,7},{6,4},{7,5},{8,10},{9,11},{10,... | collective-permute-start | bytes 122888 | tf_op jit(solution)/shard_map/cond/branch_0_fun/ppermute | solution.py:670
  6.3 4.0 %collective-permute-start.1 = (f32[5,8,256]{2,1,0:T(8,128)S(1)}, f32[5,8,256]{2,1,0:T(8,128)S(1)}, u32[]{:S(2)}, u32[]{:S(2)}) collective-permute-start(f32[5,8,256]{2,1,0:T(8,128)S(1)} %get-tuple-element.48.refs_0_), channel_id=1, source_target_pairs={{0,3},{1,0},{2,1},{3,2},{4,7},{5,4},{6,5},{7,6},{8,11},{9,8},{10,9... | collective-permute-start | bytes 122888 | tf_op jit(solution)/shard_map/cond/branch_0_fun/ppermute | solution.py:670
  7.6 5.8 %collective-permute-start.2 = (f32[5,8,256]{2,1,0:T(8,128)S(1)}, f32[5,8,256]{2,1,0:T(8,128)S(1)}, u32[]{:S(2)}, u32[]{:S(2)}) collective-permute-start(f32[5,8,256]{2,1,0:T(8,128)S(1)} %get-tuple-element.48.refs_0_), channel_id=1, source_target_pairs={{0,1},{1,2},{2,3},{3,0},{4,5},{5,6},{6,7},{7,4},{8,9},{9,10},{10,1... | collective-permute-start | bytes 122888 | tf_op jit(solution)/shard_map/cond/branch_0_fun/ppermute | solution.py:670
  13.5 1.9 %collective-permute-start.14 = (f32[16,8,256]{2,1,0:T(8,128)S(1)}, f32[16,8,256]{2,1,0:T(8,128)S(1)}, u32[]{:S(2)}, u32[]{:S(2)}) collective-permute-start(f32[16,8,256]{2,1,0:T(8,128)S(1)} %get-tuple-element.138), channel_id=1, source_target_pairs={{0,8},{8,0},{16,24},{24,16},{1,9},{9,1},{17,25},{25,17},{2,10},{10... | collective-permute-start | bytes 393224 | tf_op jit(solution)/shard_map/ppermute | solution.py:677
  15.6 5.4 %collective-permute-start.15 = (f32[16,8,128]{2,1,0:T(8,128)S(1)}, f32[16,8,128]{2,1,0:T(8,128)S(1)}, u32[]{:S(2)}, u32[]{:S(2)}) collective-permute-start(f32[16,8,128]{2,1,0:T(8,128)S(1)} %get-tuple-element.140), channel_id=1, source_target_pairs={{0,8},{8,0},{16,24},{24,16},{1,9},{9,1},{17,25},{25,17},{2,10},{10... | collective-permute-start | bytes 196616 | tf_op jit(solution)/shard_map/ppermute | solution.py:677
